TPU v7x, 256 devices: a whole 4x4x8 slice. The times are simulated.
256 devices in a mesh: patch: 32 (over z, y_lo, core), head: 8 (over x, y_hi).
Axes of the slice: x: 4, y: 4 (y_hi: 2, y_lo: 2; y = y_hi * 2 + y_lo), z: 8, core: 2. Of those that a mesh axis runs over, the one named last changes fastest.
Arguments:
- fresh_q: bfloat16 [12288, 3072], P(('patch', 'head')), may hold values from -180 to 180
- fresh_k: bfloat16 [12288, 3072], P(('patch', 'head')), may hold values from -180 to 180
- fresh_v: bfloat16 [12288, 3072], P(('patch', 'head')), may hold values from -6 to 6
- stale_k: bfloat16 [12288, 3072], P('patch', 'head'), may hold values from -20 to 20
- stale_v: bfloat16 [12288, 3072], P('patch', 'head'), may hold values from -6 to 6
- q_gain: float32 [3072], replicated, may hold values from 0.1 to 1.9
- k_gain: float32 [3072], replicated, may hold values from 0.1 to 1.9
Outputs:
- attended: bfloat16 [12288, 3072], P(('patch', 'head'))
- key_cache: bfloat16 [12288, 3072], P('patch', 'head')
All inputs are finite; a program needn't handle non-finite values.
Results may differ from a plain program's by a relative error of at most 0.011.
Values may be sent and summed in bfloat16 or wider, within the bound.
No kernel may reach another device: no remote copies, remote signals or barrier semaphores. Data moves between devices by JAX's collectives and lax.ppermute only.
A program may use at most 192 MiB of HBM per device.

v0:
```python
import jax
import jax.numpy as jnp
from jax import lax
from jax.sharding import PartitionSpec as P

HEADS = 24
HD = 128


EPSILON = 1e-06
LOWEST = -1e30


def scale_rows(source, square_sum, gain, width_all):
    values = source.astype(jnp.float32)
    factor = lax.rsqrt(square_sum[:, None] / width_all + EPSILON)
    return (values * factor * gain[None, :]).astype(jnp.bfloat16)


def heads_view(source, heads_dev):
    return source.reshape(source.shape[0], heads_dev, source.shape[1] // heads_dev)


def scaled_scores(queries, key_rows):
    score_scale = HD ** (-0.5)
    return (
        jnp.einsum("qhe,khe->hqk", queries, key_rows, preferred_element_type=jnp.float32)
        * score_scale
    )


def block_stats(scores, value_rows):
    row_max = jnp.max(scores, axis=2)
    weights = jnp.exp(scores - row_max[:, :, None])
    row_sum = jnp.sum(weights, axis=2)
    weighted = jnp.einsum(
        "hqk,khe->hqe", weights.astype(jnp.bfloat16), value_rows, preferred_element_type=jnp.float32
    )
    return (row_max, row_sum, weighted)


def absorb(carried, scores, value_rows):
    row_max, row_sum, weighted = carried
    new_max = jnp.maximum(row_max, jnp.max(scores, axis=2))
    rescale = jnp.exp(row_max - new_max)
    weights = jnp.exp(scores - new_max[:, :, None])
    row_sum = row_sum * rescale + jnp.sum(weights, axis=2)
    added = jnp.einsum(
        "hqk,khe->hqe", weights.astype(jnp.bfloat16), value_rows, preferred_element_type=jnp.float32
    )
    return (new_max, row_sum, weighted * rescale[:, :, None] + added)


def body(fresh_q, fresh_k, fresh_v, stale_k, stale_v, q_gain, k_gain):
    groups = lax.axis_size("head")
    heads_dev = HEADS // groups
    width_dev = heads_dev * HD
    width_all = q_gain.shape[0]
    local_q, local_k, local_v = (
        lax.all_to_all(fresh_q, "head", split_axis=1, concat_axis=0, tiled=True),
        lax.all_to_all(fresh_k, "head", split_axis=1, concat_axis=0, tiled=True),
        lax.all_to_all(fresh_v, "head", split_axis=1, concat_axis=0, tiled=True),
    )
    first_col = lax.axis_index("head") * width_dev
    gain_q = lax.dynamic_slice_in_dim(q_gain, first_col, width_dev, 0)
    gain_k = lax.dynamic_slice_in_dim(k_gain, first_col, width_dev, 0)
    squares_q = jnp.sum(jnp.square(local_q.astype(jnp.float32)), axis=1)
    squares_k = jnp.sum(jnp.square(local_k.astype(jnp.float32)), axis=1)
    total_q, total_k = lax.psum((squares_q, squares_k), "head")
    normed_q = scale_rows(local_q, total_q, gain_q, width_all)
    key_cache = scale_rows(local_k, total_k, gain_k, width_all)
    patch_rows = normed_q.shape[0]
    my_patch = lax.axis_index("patch")
    query_view = heads_view(normed_q, heads_dev)
    fresh_state = block_stats(
        scaled_scores(query_view, heads_view(key_cache, heads_dev)), heads_view(local_v, heads_dev)
    )
    segment = (
        lax.all_gather(stale_k, "patch", axis=0, tiled=True),
        lax.all_gather(stale_v, "patch", axis=0, tiled=True),
    )
    key_rows = heads_view(segment[0], heads_dev)
    value_rows = heads_view(segment[1], heads_dev)
    scores = scaled_scores(query_view, key_rows)
    owner_patch = jnp.arange(segment[0].shape[0], dtype=jnp.int32) // patch_rows
    scores = jnp.where((owner_patch == my_patch)[None, None, :], 2.0 * LOWEST, scores)
    folded = absorb(fresh_state, scores, value_rows)
    row_max, row_sum, weighted = folded
    result = (weighted / row_sum[:, :, None]).astype(jnp.bfloat16)
    result = jnp.transpose(result, (1, 0, 2)).reshape(patch_rows, width_dev)
    attended = lax.all_to_all(result, "head", split_axis=0, concat_axis=1, tiled=True)
    return (attended, key_cache)


def solution(mesh):
    placed = (
        P(("patch", "head"), None),
        P(("patch", "head"), None),
        P(("patch", "head"), None),
        P("patch", "head"),
        P("patch", "head"),
        P(),
        P(),
    )
    return jax.shard_map(
        body,
        mesh=mesh,
        in_specs=placed,
        out_specs=(P(("patch", "head"), None), P("patch", "head")),
        check_vma=False,
    )
```

profile of v0, /device:TPU:1, one launch (start us, length us, event | category | flops | bytes accessed | tf_op | source)
XLA Modules:
  0.0 217.4 jit_solution(2293015738586347032)
XLA Ops:
  7.2 1.8 copy.45
  9.1 1.8 copy.47
  11.0 1.7 copy.79
  12.7 7.5 %all-to-all-start.1 = ((bf16[48,8,384]{2,0,1:T(8,128)(2,1)}), bf16[48,8,384]{2,0,1:T(8,128)(2,1)S(1)}, u32[]{:S(2)}, u32[]{:S(2)}) async-start(bf16[48,8,384]{2,0,1:T(8,128)(2,1)} %bitcast.59), calls=%async_computation.1 | async-start | bytes 589824 | tf_op jit(solution)/shard_map/all_to_all | solution.py:61
  20.2 0.8 dynamic-slice_bitcast_fusion.1
  21.1 1.7 copy.80
  22.8 1.7 copy.78
  24.5 3.2 %all-to-all-done.1 = bf16[48,8,384]{2,0,1:T(8,128)(2,1)S(1)} async-done(((bf16[48,8,384]{2,0,1:T(8,128)(2,1)}), bf16[48,8,384]{2,0,1:T(8,128)(2,1)S(1)}, u32[]{:S(2)}, u32[]{:S(2)}) %all-to-all-start.1) | async-done | bytes 294944 | tf_op jit(solution)/shard_map/all_to_all | solution.py:61
  27.7 3.9 %all-to-all-start = ((bf16[48,8,384]{2,0,1:T(8,128)(2,1)}), bf16[48,8,384]{2,0,1:T(8,128)(2,1)S(1)}, u32[]{:S(2)}, u32[]{:S(2)}) async-start(bf16[48,8,384]{2,0,1:T(8,128)(2,1)} %bitcast.60), calls=%async_computation | async-start | bytes 589824 | tf_op jit(solution)/shard_map/all_to_all | solution.py:60
  31.7 7.2 %all-to-all-done = bf16[48,8,384]{2,0,1:T(8,128)(2,1)S(1)} async-done(((bf16[48,8,384]{2,0,1:T(8,128)(2,1)}), bf16[48,8,384]{2,0,1:T(8,128)(2,1)S(1)}, u32[]{:S(2)}, u32[]{:S(2)}) %all-to-all-start) | async-done | bytes 294944 | tf_op jit(solution)/shard_map/all_to_all | solution.py:60
  38.9 3.4 %all-to-all-start.2 = ((bf16[48,8,384]{2,0,1:T(8,128)(2,1)}), bf16[48,8,384]{2,0,1:T(8,128)(2,1)S(1)}, u32[]{:S(2)}, u32[]{:S(2)}) async-start(bf16[48,8,384]{2,0,1:T(8,128)(2,1)} %bitcast.58), calls=%async_computation.2 | async-start | bytes 589824 | tf_op jit(solution)/shard_map/all_to_all | solution.py:62
  43.2 6.6 %all-to-all-done.2 = bf16[48,8,384]{2,0,1:T(8,128)(2,1)S(1)} async-done(((bf16[48,8,384]{2,0,1:T(8,128)(2,1)}), bf16[48,8,384]{2,0,1:T(8,128)(2,1)S(1)}, u32[]{:S(2)}, u32[]{:S(2)}) %all-to-all-start.2) | async-done | bytes 294944 | tf_op jit(solution)/shard_map/all_to_all | solution.py:62
  49.8 0.9 reshape.106
  50.6 17.3 %all-reduce = (f32[384]{0:T(512)S(1)}, f32[384]{0:T(512)S(1)}) all-reduce(f32[384]{0:T(512)S(1)} %reduce_sum.50, f32[384]{0:T(512)S(1)} %reduce_sum.53), channel_id=1, replica_groups=mesh['patch'=32,'head'=8] {'head'}, use_global_device_ids=true, to_apply=%region_1.0 | all-reduce | flops 768 | bytes 6144 | tf_op jit(solution)/shard_map/psum | solution.py:69
  69.2 22.4 %all-gather.3.cloned.1.call-done = bf16[12288,384]{0,1:T(8,128)(2,1)} async-done(((bf16[384,384]{0,1:T(8,128)(2,1)}), bf16[12288,384]{0,1:T(8,128)(2,1)}) %all-gather.3.cloned.1.call-update) | async-done | bytes 9437200 | tf_op jit(solution)/shard_map/all_gather | solution.py:79
  91.6 26.1 %fusion = (f32[3,384]{1,0:T(4,128)S(1)}, f32[3,384,12288]{2,1,0:T(8,128)}) fusion(pred[12288]{0:T(1024)(128)(4,1)S(1)} %fusion.26, bf16[12288,3,128]{0,2,1:T(8,128)(2,1)} %bitcast.61, f32[384,3,128]{2,1,0:T(4,128)S(1)} %reshape.109, f32[3,128]{1,0:T(4,128)S(1)} %dynamic-slice_bitcast_fusion, f32[384]{0:T(512)S(1)} %add_rsqrt_fusion.1), kind=kOutput, calls=%fused_computation.2 | convolution fusion | flops 3666787328 | bytes 66670080 | tf_op jit(solution)/shard_map/qhe,khe->hqk/dot_general | solution.py:27
  117.7 19.7 %fusion.1 = f32[3,384]{1,0:T(4,128)S(1)} fusion(f32[3,384,12288]{2,1,0:T(8,128)} %get-tuple-element.9, f32[3,384]{1,0:T(4,128)S(1)} %max.18, pred[12288]{0:T(1024)(128)(4,1)S(1)} %fusion.26), kind=kLoop, calls=%fused_computation.3 | loop fusion | flops 56621952 | bytes 56644608 | tf_op jit(solution)/shard_map/reduce_sum | solution.py:47
  137.4 30.8 %all-gather.5.cloned.1.call-done = bf16[12288,384]{0,1:T(8,128)(2,1)} async-done(((bf16[384,384]{0,1:T(8,128)(2,1)}), bf16[12288,384]{0,1:T(8,128)(2,1)}) %all-gather.5.cloned.1.call-update) | async-done | bytes 9437200 | tf_op jit(solution)/shard_map/all_gather | solution.py:80
  168.2 25.5 %fusion.11 = f32[384,3,128]{2,0,1:T(8,128)S(1)} fusion(bf16[12288,3,128]{0,2,1:T(8,128)(2,1)} %bitcast.70, f32[3,384,12288]{2,1,0:T(8,128)} %get-tuple-element.9, f32[3,384]{1,0:T(4,128)S(1)} %max.18, pred[12288]{0:T(1024)(128)(4,1)S(1)} %fusion.26), kind=kOutput, calls=%fused_computation.15 | convolution fusion | flops 3680501760 | bytes 66667008 | tf_op jit(solution)/shard_map/hqk,khe->hqe/dot_general | solution.py:48
  194.8 1.0 all_to_all.53
  195.7 6.2 %all-to-all-start.3 = ((bf16[8,48,384]{2,1,0:T(8,128)(2,1)}), bf16[8,48,384]{2,1,0:T(8,128)(2,1)S(1)}, u32[]{:S(2)}, u32[]{:S(2)}) async-start(bf16[8,48,384]{2,1,0:T(8,128)(2,1)} %all_to_all.53), calls=%async_computation.3 | async-start | bytes 589824 | tf_op jit(solution)/shard_map/all_to_all | solution.py:91
  201.9 0.8 dynamic_slice.7
  202.7 0.9 fusion.20
  203.5 6.3 %all-to-all-done.3 = bf16[8,48,384]{2,1,0:T(8,128)(2,1)S(1)} async-done(((bf16[8,48,384]{2,1,0:T(8,128)(2,1)}), bf16[8,48,384]{2,1,0:T(8,128)(2,1)S(1)}, u32[]{:S(2)}, u32[]{:S(2)}) %all-to-all-start.3) | async-done | bytes 294944 | tf_op jit(solution)/shard_map/all_to_all | solution.py:91
  (30 shorter events, 4.3 us)
Async XLA Ops:
  7.2 13.8 %copy-start = (f32[3072]{0:T(1024)S(1)}, f32[3072]{0:T(1024)}, u32[]{:S(2)}) copy-start(f32[3072]{0:T(1024)} %param.12) | copy-start | bytes 36868
  7.2 84.5 %all-gather.3.cloned.1.call-start = ((), (), s32[]{:S(2)}) async-start(), calls=%async_computation.4 | async-start | bytes 9732096 | tf_op jit(solution)/shard_map/all_gather | solution.py:79
  9.1 159.1 %all-gather.5.cloned.1.call-start = ((), (), s32[]{:S(2)}) async-start(), calls=%async_computation.5 | async-start | bytes 9732096 | tf_op jit(solution)/shard_map/all_gather | solution.py:80
  12.7 14.9 %all-to-all-start.1 = ((bf16[48,8,384]{2,0,1:T(8,128)(2,1)}), bf16[48,8,384]{2,0,1:T(8,128)(2,1)S(1)}, u32[]{:S(2)}, u32[]{:S(2)}) async-start(bf16[48,8,384]{2,0,1:T(8,128)(2,1)} %bitcast.59), calls=%async_computation.1 | async-start | bytes 589824 | tf_op jit(solution)/shard_map/all_to_all | solution.py:61
  27.7 11.3 %all-to-all-start = ((bf16[48,8,384]{2,0,1:T(8,128)(2,1)}), bf16[48,8,384]{2,0,1:T(8,128)(2,1)S(1)}, u32[]{:S(2)}, u32[]{:S(2)}) async-start(bf16[48,8,384]{2,0,1:T(8,128)(2,1)} %bitcast.60), calls=%async_computation | async-start | bytes 589824 | tf_op jit(solution)/shard_map/all_to_all | solution.py:60
  38.9 10.8 %all-to-all-start.2 = ((bf16[48,8,384]{2,0,1:T(8,128)(2,1)}), bf16[48,8,384]{2,0,1:T(8,128)(2,1)S(1)}, u32[]{:S(2)}, u32[]{:S(2)}) async-start(bf16[48,8,384]{2,0,1:T(8,128)(2,1)} %bitcast.58), calls=%async_computation.2 | async-start | bytes 589824 | tf_op jit(solution)/shard_map/all_to_all | solution.py:62
  168.2 25.6 %copy-start.2 = (bf16[384,3,128]{2,1,0:T(4,128)(2,1)S(1)}, bf16[384,3,128]{2,1,0:T(4,128)(2,1)}, u32[]{:S(2)}) copy-start(bf16[384,3,128]{2,1,0:T(4,128)(2,1)} %reshape.106) | copy-start | bytes 884740
  168.2 42.4 %copy-start.1 = (f32[3072]{0:T(1024)S(1)}, f32[3072]{0:T(1024)}, u32[]{:S(2)}) copy-start(f32[3072]{0:T(1024)} %param.12) | copy-start | bytes 36868
  195.7 14.1 %all-to-all-start.3 = ((bf16[8,48,384]{2,1,0:T(8,128)(2,1)}), bf16[8,48,384]{2,1,0:T(8,128)(2,1)S(1)}, u32[]{:S(2)}, u32[]{:S(2)}) async-start(bf16[8,48,384]{2,1,0:T(8,128)(2,1)} %all_to_all.53), calls=%async_computation.3 | async-start | bytes 589824 | tf_op jit(solution)/shard_map/all_to_all | solution.py:91
Sparse Core Ops, SparseCore 0:
  10.4 81.1 all-gather.2
  94.0 74.1 all-gather.4
where the time goes:
time: 218 us; the launch traced here: 217 us
  waiting for transfers between devices  76.5 us (35%)
  matrix products  52.8 us (24%)
  other arithmetic  21.7 us (10%)
  starting transfers between devices  21 us (10%)
  blocking collectives  17.3 us (8%)
  between operations  14.2 us (7%)
  local copies, waits for them, and re-layouts  13.9 us (6%)
    all_gather x1, waiting for transfers between devices, body(): lax.all_gather(stale_v, 'patch', axis=0, tiled=True)  30.8 us
    dot_general x2, matrix products, scaled_scores(): jnp.einsum('qhe,khe->hqk', queries, key_rows, preferred_element_type=jnp....  26.6 us
    dot_general x1, matrix products, absorb(): jnp.einsum('hqk,khe->hqe', weights.astype(jnp.bfloat16), value_rows, pref...  25.5 us
    all_gather x1, waiting for transfers between devices, body(): lax.all_gather(stale_k, 'patch', axis=0, tiled=True)  22.4 us
    reduce_sum x1, other arithmetic, absorb(): row_sum = row_sum * rescale + jnp.sum(weights, axis=2)  19.7 us
    psum x1, blocking collectives, body(): total_q, total_k = lax.psum((squares_q, squares_k), 'head')  17.3 us
    all_to_all x1, starting transfers between devices, body(): lax.all_to_all(fresh_k, 'head', split_axis=1, concat_axis=0, tiled=True)  7.48 us
    all_to_all x1, waiting for transfers between devices, body(): lax.all_to_all(fresh_q, 'head', split_axis=1, concat_axis=0, tiled=True)  7.24 us
  transfers between devices with their start and end apart: 6, of which 6 were waited for; matrix products, arithmetic and copies ran while one was open for 27% of the time, Pallas kernels for 0%

commit v1 on v0

v1 whole, which is shorter than its diff:
```python
import functools
import jax
import jax.numpy as jnp
from jax import lax
from jax.experimental import pallas as pl
from jax.experimental.pallas import tpu as pltpu
from jax.sharding import Mesh, PartitionSpec as P

HEADS = 24
HD = 128
EPSILON = 1e-06
LOG2E = 1.4426950408889634
SCALE2 = HD**-0.5 * LOG2E
BF = jnp.bfloat16
F32 = jnp.float32
LIMIT = 48 * 2**20
ROWS = 64


def prep_kernel(groups, copies, q_ref, k_ref, v_ref, gq_ref, gk_ref, q_out, kv_out):
    width = q_ref.shape[1]
    per = width // groups

    def norm(src, gain):
        values = src[...].astype(F32)
        mean = jnp.sum(values * values, axis=1, keepdims=True) / width
        return (values * lax.rsqrt(mean + EPSILON) * gain[...]).astype(BF)

    q = norm(q_ref, gq_ref)
    k = norm(k_ref, gk_ref)
    for g in range(groups):
        cols = slice(g * per, (g + 1) * per)
        for c in range(copies):
            q_out[c * groups + g] = q[:, cols]
        kv_out[g, :, :per] = k[:, cols]
        kv_out[g, :, per:] = v_ref[:, cols]


def prep(fresh_q, fresh_k, fresh_v, q_gain, k_gain, groups, copies):
    rows, width = fresh_q.shape
    per = width // groups
    return pl.pallas_call(
        functools.partial(prep_kernel, groups, copies),
        out_shape=(
            jax.ShapeDtypeStruct((copies * groups, rows, per), BF),
            jax.ShapeDtypeStruct((groups, rows, 2 * per), BF),
        ),
        in_specs=[pl.BlockSpec(memory_space=pltpu.VMEM)] * 5,
        out_specs=[pl.BlockSpec(memory_space=pltpu.VMEM)] * 2,
        compiler_params=pltpu.CompilerParams(vmem_limit_bytes=LIMIT),
        name="prep",
    )(fresh_q, fresh_k, fresh_v, q_gain[None, :], k_gain[None, :])


def attn_kernel(nb, fresh, first, last, bq, *refs):
    refs = list(refs)
    own_ref = refs.pop(0) if fresh else None
    q_ref = refs.pop(0)
    k_refs = [refs.pop(0) for _ in range(nb)]
    v_refs = [refs.pop(0) for _ in range(nb)]
    if fresh:
        fk_ref, fv_ref = refs.pop(0), refs.pop(0)
    if not first:
        acc_in, m_in, l_in = refs.pop(0), refs.pop(0), refs.pop(0)
    if last:
        out_ref = refs.pop(0)
    else:
        acc_out, m_out, l_out = refs.pop(0), refs.pop(0), refs.pop(0)
    ks, vs = refs
    head = pl.program_id(0)
    off = 0
    for kr, vr in zip(k_refs, v_refs):
        n = kr.shape[0]
        ks[off : off + n] = kr[...]
        vs[off : off + n, :HD] = vr[...]
        off += n

    @pl.when(head == 0)
    def _():
        vs[:, HD:] = jnp.ones((off, HD), BF)

    nq = q_ref.shape[0]
    tiles = nq // bq

    def scores(t):
        return lax.dot_general(
            q_ref[t * bq : (t + 1) * bq], ks[...], (((1,), (1,)), ((), ())), preferred_element_type=F32
        )

    def rest(t, s):
        rows = slice(t * bq, (t + 1) * bq)
        m = jnp.max(s, axis=1, keepdims=True)
        if not first:
            m_old = m_in[0, rows]
            m = jnp.maximum(m_old[:, :1], m)
        p = jnp.exp2(s * SCALE2 - m * SCALE2).astype(BF)
        o = jnp.dot(p, vs[...], preferred_element_type=F32)
        acc, l = o[:, :HD], o[:, HD:]
        m = jnp.broadcast_to(m, (bq, HD))
        if not first:
            alpha = jnp.exp2((m_old - m) * SCALE2)
            acc = acc + acc_in[0, rows] * alpha
            l = l + l_in[0, rows] * alpha
        if not last:
            acc_out[0, rows], m_out[0, rows], l_out[0, rows] = acc, m, l
            return
        o = (acc / l).astype(BF)
        lse = m * SCALE2 + jnp.log(l) * LOG2E
        tok = ROWS - 16
        eye = lax.broadcasted_iota(jnp.int32, (tok, HD), 0) == lax.broadcasted_iota(jnp.int32, (tok, HD), 1)
        for i in range(bq // tok):
            d = t * (bq // tok) + i
            out_ref[d, :tok] = o[i * tok : (i + 1) * tok]
            row = jnp.sum(jnp.where(eye, lse[i * tok : (i + 1) * tok], 0.0), axis=0, keepdims=True)
            hi = row.astype(BF).astype(F32)
            mid = (row - hi).astype(BF).astype(F32)
            low = row - hi - mid
            which = lax.broadcasted_iota(jnp.int32, (16, HD), 0)
            packed = jnp.where(which == 0, hi, jnp.where(which == 1, mid, jnp.where(which == 2, low, 0.0)))
            out_ref[d, tok:] = packed.astype(BF)

    def run(sweep):
        s = scores(sweep[0])
        for i, t in enumerate(sweep):
            ahead = scores(sweep[i + 1]) if i + 1 < len(sweep) else None
            rest(t, s)
            s = ahead

    if not fresh:
        run(range(tiles))
        return
    n0 = k_refs[0].shape[0]
    patches = nq // n0
    per = tiles // patches
    for j in range(patches):
        own = own_ref[0] == j
        ks[:n0] = jnp.where(own, fk_ref[...], k_refs[0][...])
        vs[:n0, :HD] = jnp.where(own, fv_ref[...], v_refs[0][...])
        run(range(j * per, (j + 1) * per))


def attend(q, blocks, state=None, fresh=None, own=None, last=False, bq=256, name="attend"):
    nq, width = q.shape
    heads = width // HD
    nb = len(blocks)
    keys = sum(b.shape[0] for b in blocks)
    kspec = [pl.BlockSpec((b.shape[0], HD), lambda h: (0, h)) for b in blocks]
    vspec = [pl.BlockSpec((b.shape[0], HD), lambda h: (0, heads + h)) for b in blocks]
    state_spec = pl.BlockSpec((1, nq, HD), lambda h: (h, 0, 0))
    args, specs = [], []
    if fresh is not None:
        args.append(own)
        specs.append(pl.BlockSpec(memory_space=pltpu.SMEM))
    args += [q, *blocks, *blocks]
    specs += [pl.BlockSpec((nq, HD), lambda h: (0, h)), *kspec, *vspec]
    if fresh is not None:
        args += [fresh, fresh]
        n0 = fresh.shape[0]
        specs += [pl.BlockSpec((n0, HD), lambda h: (0, h)), pl.BlockSpec((n0, HD), lambda h: (0, heads + h))]
    if state is not None:
        args += list(state)
        specs += [state_spec] * 3
    if last:
        out_shape = jax.ShapeDtypeStruct((nq // (ROWS - 16), ROWS, width), BF)
        out_specs = pl.BlockSpec((nq // (ROWS - 16), ROWS, HD), lambda h: (0, 0, h))
    else:
        out_shape = [jax.ShapeDtypeStruct((heads, nq, HD), F32)] * 3
        out_specs = [state_spec] * 3
    flops = 4 * nq * keys * width
    return pl.pallas_call(
        functools.partial(attn_kernel, nb, fresh is not None, state is None, last, bq),
        grid=(heads,),
        in_specs=specs,
        out_specs=out_specs,
        out_shape=out_shape,
        scratch_shapes=[pltpu.VMEM((keys, HD), BF), pltpu.VMEM((keys, 2 * HD), BF)],
        compiler_params=pltpu.CompilerParams(vmem_limit_bytes=LIMIT),
        cost_estimate=pl.CostEstimate(flops=flops, bytes_accessed=8 * 2**20, transcendentals=nq * keys * heads),
        name=name,
    )(*args)


def merge_kernel(groups, copies, in_ref, out_ref):
    tok = ROWS - 16
    heads = in_ref.shape[2] // HD
    eye = lax.broadcasted_iota(jnp.int32, (tok, HD), 0) == lax.broadcasted_iota(jnp.int32, (tok, HD), 1)
    for g in range(groups):
        for h in range(heads):
            cols = slice(h * HD, (h + 1) * HD)
            lses = []
            for c in range(copies):
                packed = in_ref[c * groups + g, tok:, cols].astype(F32)
                row = jnp.sum(packed, axis=0, keepdims=True)
                lses.append(jnp.sum(jnp.where(eye, jnp.broadcast_to(row, (tok, HD)), 0.0), axis=1, keepdims=True))
            top = functools.reduce(jnp.maximum, lses)
            weights = [jnp.exp2(x - top) for x in lses]
            total = sum(weights)
            acc = 0.0
            for c in range(copies):
                acc = acc + in_ref[c * groups + g, :tok, cols].astype(F32) * (weights[c] / total)
            first = (g * heads + h) * HD
            out_ref[:, first : first + HD] = acc.astype(BF)


def merge(parts, groups, copies):
    width = parts.shape[2] * groups
    return pl.pallas_call(
        functools.partial(merge_kernel, groups, copies),
        out_shape=jax.ShapeDtypeStruct((ROWS - 16, width), BF),
        in_specs=[pl.BlockSpec(memory_space=pltpu.VMEM)],
        out_specs=pl.BlockSpec(memory_space=pltpu.VMEM),
        compiler_params=pltpu.CompilerParams(vmem_limit_bytes=LIMIT),
        name="merge",
    )(parts)


Z, YL, CORE, X, YH = 8, 2, 2, 4, 2
UP = [(i, (i + 1) % Z) for i in range(Z)]
DOWN = [(i, (i - 1) % Z) for i in range(Z)]
SWAP = [(0, 1), (1, 0)]


def other_core(x):
    return lax.ppermute(x, "core", SWAP)


def body(fresh_q, fresh_k, fresh_v, stale_k, stale_v, q_gain, k_gain):
    groups = X * YH
    width_dev = stale_k.shape[1]
    payload = jnp.concatenate([stale_k, stale_v], axis=1)
    q_parts, kv_parts = prep(fresh_q, fresh_k, fresh_v, q_gain, k_gain, groups, YL)

    up1, down1 = lax.ppermute(payload, "z", UP), lax.ppermute(payload, "z", DOWN)
    q = lax.all_to_all(q_parts, ("yl", "x", "yh"), split_axis=0, concat_axis=0, tiled=True)
    q = q.reshape(-1, width_dev)
    fresh = lax.all_to_all(kv_parts, ("x", "yh"), split_axis=0, concat_axis=0, tiled=True)
    fresh = fresh.reshape(-1, 2 * width_dev)
    own = [payload, other_core(payload)]
    up2, down2 = lax.ppermute(up1, "z", UP), lax.ppermute(down1, "z", DOWN)
    r1 = [up1, down1, other_core(up1), other_core(down1)]
    up3, down3 = lax.ppermute(up2, "z", UP), lax.ppermute(down2, "z", DOWN)
    r2 = [up2, down2, other_core(up2), other_core(down2)]
    half = payload.shape[0] // 2
    up4, down4 = lax.ppermute(up3[:half], "z", UP), lax.ppermute(down3[half:], "z", DOWN)
    r3 = [up3, down3, other_core(up3), other_core(down3)]
    r4 = [up4, down4, other_core(up4), other_core(down4)]

    mine = lax.axis_index("yl").astype(jnp.int32).reshape(1)
    state = attend(q, r1, name="attend1")
    state = attend(q, own + r2, state, fresh=fresh, own=mine, bq=192, name="attend2")
    state = attend(q, r3, state, name="attend3")
    parts = attend(q, r4, state, last=True, bq=384, name="attend4")
    back = lax.all_to_all(parts, ("yl", "x", "yh"), split_axis=0, concat_axis=0, tiled=True)
    return merge(back, groups, YL), fresh[:, :width_dev]


def solution(mesh):
    fine = Mesh(mesh.devices.reshape(Z, YL, CORE, X, YH), ("z", "yl", "core", "x", "yh"))
    patch, head = ("z", "yl", "core"), ("x", "yh")
    tokens = P(patch + head, None)
    tiles = P(patch, head)
    return jax.shard_map(
        body,
        mesh=fine,
        in_specs=(tokens, tokens, tokens, tiles, tiles, P(), P()),
        out_specs=(tokens, tiles),
        check_vma=False,
    )
```

time: 218 us -> 120 us (0.55)
  matrix products: 52.8 us -> 0 us
  waiting for transfers between devices: 76.5 us -> 30.5 us
  Pallas kernels: 0 us -> 34.6 us
  other arithmetic: 21.7 us -> 0 us
  starting transfers between devices: 21 us -> 42.4 us
  blocking collectives: 17.3 us -> 0 us
  between operations: 14.2 us -> 0.79 us
  local copies, waits for them, and re-layouts: 13.9 us -> 11.3 us
    all_gather x2 -> x0, waiting for transfers between devices: 53.2 us -> none  [the longest x1 30.8 us: body(): lax.all_gather(stale_v, 'patch', axis=0, tiled=True)]
    dot_general x4 -> x0, matrix products: 52.8 us -> none  [the longest x2 26.6 us: scaled_scores(): jnp.einsum('qhe,khe->hqk', queries, key_rows, preferred_element_type=jnp....]
    pallas_call x0 -> x6, Pallas kernels: none -> 34.6 us  [the longest x4 33.1 us: attend(): pl.pallas_call(functools.partial(attn_kernel, nb, fresh is not None, stat...]
    ppermute x0 -> x17, starting transfers between devices: none -> 23.8 us  [the longest x9 8.78 us: other_core(): return lax.ppermute(x, 'core', SWAP)]
    reduce_sum x4 -> x0, other arithmetic: 20.2 us -> none  [the longest x1 19.7 us: absorb(): row_sum = row_sum * rescale + jnp.sum(weights, axis=2)]
    psum x1 -> x0, blocking collectives: 17.3 us -> none  [body(): total_q, total_k = lax.psum((squares_q, squares_k), 'head')]
    ppermute x0 -> x17, waiting for transfers between devices: none -> 16.2 us  [the longest x1 13.1 us: body(): lax.ppermute(payload, 'z', UP)]
    all_to_all x4 -> x3, waiting for transfers between devices: 23.3 us -> 14.3 us  [the longest x1 12.7 us: body(): lax.all_to_all(parts, ('yl', 'x', 'yh'), split_axis=0, concat_axis=0, til...]
  transfers between devices with their start and end apart: 6 -> 20, of which waited for: 6 -> 5; matrix products, arithmetic and copies ran while one was open for 27% -> 2% of each run, Pallas kernels for 0% -> 23%
where the time goes in v1:
time: 120 us
  starting transfers between devices  42.4 us (35%)
  Pallas kernels  34.6 us (29%)
  waiting for transfers between devices  30.5 us (25%)
  local copies, waits for them, and re-layouts  11.3 us (9%)
    pallas_call x4, Pallas kernels, attend(): pl.pallas_call(functools.partial(attn_kernel, nb, fresh is not None, stat...  33.1 us
    ppermute x1, waiting for transfers between devices, body(): lax.ppermute(payload, 'z', UP)  13.1 us
    all_to_all x1, waiting for transfers between devices, body(): lax.all_to_all(parts, ('yl', 'x', 'yh'), split_axis=0, concat_axis=0, til...  12.7 us
    ppermute x9, starting transfers between devices, other_core(): return lax.ppermute(x, 'core', SWAP)  8.78 us
    unnamed x27, local copies, waits for them, and re-layouts  8.12 us
    all_to_all x1, starting transfers between devices, body(): lax.all_to_all(parts, ('yl', 'x', 'yh'), split_axis=0, concat_axis=0, til...  6.76 us
    all_to_all x1, starting transfers between devices, body(): lax.all_to_all(q_parts, ('yl', 'x', 'yh'), split_axis=0, concat_axis=0, t...  6.75 us
    all_to_all x1, starting transfers between devices, body(): lax.all_to_all(kv_parts, ('x', 'yh'), split_axis=0, concat_axis=0, tiled=...  5.01 us
  transfers between devices with their start and end apart: 20, of which 5 were waited for; matrix products, arithmetic and copies ran while one was open for 2% of the time, Pallas kernels for 23%

profile of v1, /device:TPU:1, one launch (start us, length us, event | category | flops | bytes accessed | tf_op | source)
XLA Modules:
  0.0 119.6 jit_solution(6847179869355231407)
XLA Ops:
  0.7 1.1 constant_dynamic-update-slice_fusion.1
  2.8 2.5 %collective-permute-start = (bf16[384,768]{1,0:T(8,128)(2,1)S(1)}, bf16[384,768]{1,0:T(8,128)(2,1)}, u32[]{:S(2)}, u32[]{:S(2)}) collective-permute-start(bf16[384,768]{1,0:T(8,128)(2,1)S(1)} %constant_dynamic-update-slice_fusion.refs_2_.refs_8_), channel_id=1, source_target_pairs={{0,32},{32,64},{64,96},{96,128},{128,160},{160,192},{192,224},{224... | collective-permute-start | bytes 1769480 | tf_op jit(solution)/shard_map/ppermute | solution.py:233
  5.3 4.0 %collective-permute-start.4 = (bf16[384,768]{1,0:T(8,128)(2,1)S(1)}, bf16[384,768]{1,0:T(8,128)(2,1)}, u32[]{:S(2)}, u32[]{:S(2)}) collective-permute-start(bf16[384,768]{1,0:T(8,128)(2,1)S(1)} %constant_dynamic-update-slice_fusion.refs_2_.refs_8_), channel_id=1, source_target_pairs={{0,224},{32,0},{64,32},{96,64},{128,96},{160,128},{192,160},{224,1... | collective-permute-start | bytes 1769480 | tf_op jit(solution)/shard_map/ppermute | solution.py:233
  9.3 13.1 %collective-permute-done.refs_1_.refs_5_ = bf16[384,768]{1,0:T(8,128)(2,1)} collective-permute-done((bf16[384,768]{1,0:T(8,128)(2,1)S(1)}, bf16[384,768]{1,0:T(8,128)(2,1)}, u32[]{:S(2)}, u32[]{:S(2)}) %collective-permute-start) | collective-permute-done | bytes 589856 | tf_op jit(solution)/shard_map/ppermute | solution.py:233
  22.4 2.7 %collective-permute-start.5 = (bf16[384,768]{1,0:T(8,128)(2,1)}, bf16[384,768]{1,0:T(8,128)(2,1)}, u32[]{:S(2)}, u32[]{:S(2)}) collective-permute-start(bf16[384,768]{1,0:T(8,128)(2,1)} %collective-permute-done.4.refs_2_.refs_6_), channel_id=1, source_target_pairs={{0,224},{32,0},{64,32},{96,64},{128,96},{160,128},{192,160},{224,1... | collective-permute-start | bytes 1769480 | tf_op jit(solution)/shard_map/ppermute | solution.py:239
  25.1 1.8 %collective-permute-start.12 = (bf16[384,768]{1,0:T(8,128)(2,1)S(1)}, bf16[384,768]{1,0:T(8,128)(2,1)S(1)}, u32[]{:S(2)}, u32[]{:S(2)}) collective-permute-start(bf16[384,768]{1,0:T(8,128)(2,1)S(1)} %constant_dynamic-update-slice_fusion.refs_2_.refs_8_), channel_id=1, source_target_pairs={{0,8},{8,0},{1,9},{9,1},{2,10},{10,2},{3,11},{11,3},{4,12},{12,4},... | collective-permute-start | bytes 1769480 | tf_op jit(solution)/shard_map/ppermute | solution.py:224
  28.1 6.8 %all-to-all-start = ((bf16[16,48,384]{2,1,0:T(8,128)(2,1)}), bf16[16,48,384]{2,1,0:T(8,128)(2,1)S(1)}, u32[]{:S(2)}, u32[]{:S(2)}) async-start(bf16[16,48,384]{2,1,0:T(8,128)(2,1)} %copy-done.7), calls=%async_computation | async-start | bytes 1179648 | tf_op jit(solution)/shard_map/all_to_all | solution.py:234
  34.9 2.6 %collective-permute-done.1.refs_4_.refs_10_ = bf16[384,768]{1,0:T(8,128)(2,1)S(1)} collective-permute-done((bf16[384,768]{1,0:T(8,128)(2,1)}, bf16[384,768]{1,0:T(8,128)(2,1)S(1)}, u32[]{:S(2)}, u32[]{:S(2)}) %collective-permute-start.1) | collective-permute-done | bytes 589856 | tf_op jit(solution)/shard_map/ppermute | solution.py:239
  37.4 2.7 %collective-permute-start.6 = (bf16[384,768]{1,0:T(8,128)(2,1)}, bf16[384,768]{1,0:T(8,128)(2,1)S(1)}, u32[]{:S(2)}, u32[]{:S(2)}) collective-permute-start(bf16[384,768]{1,0:T(8,128)(2,1)} %collective-permute-done.5.refs_5_.refs_11_), channel_id=1, source_target_pairs={{0,224},{32,0},{64,32},{96,64},{128,96},{160,128},{192,160},{224,1... | collective-permute-start | bytes 1769480 | tf_op jit(solution)/shard_map/ppermute | solution.py:241
  40.1 2.7 %collective-permute-start.16 = (bf16[384,768]{1,0:T(8,128)(2,1)}, bf16[384,768]{1,0:T(8,128)(2,1)}, u32[]{:S(2)}, u32[]{:S(2)}) collective-permute-start(bf16[384,768]{1,0:T(8,128)(2,1)} %collective-permute-done.4.refs_2_.refs_6_), channel_id=1, source_target_pairs={{0,8},{8,0},{1,9},{9,1},{2,10},{10,2},{3,11},{11,3},{4,12},{12,4},... | collective-permute-start | bytes 1769480 | tf_op jit(solution)/shard_map/ppermute | solution.py:224
  44.2 1.6 %all-to-all-done = bf16[16,48,384]{2,1,0:T(8,128)(2,1)S(1)} async-done(((bf16[16,48,384]{2,1,0:T(8,128)(2,1)}), bf16[16,48,384]{2,1,0:T(8,128)(2,1)S(1)}, u32[]{:S(2)}, u32[]{:S(2)}) %all-to-all-start) | async-done | bytes 589856 | tf_op jit(solution)/shard_map/all_to_all | solution.py:234
  45.8 5.0 %all-to-all-start.1 = ((bf16[8,48,768]{2,1,0:T(8,128)(2,1)}), bf16[8,48,768]{2,1,0:T(8,128)(2,1)S(1)}, u32[]{:S(2)}, u32[]{:S(2)}) async-start(bf16[8,48,768]{2,1,0:T(8,128)(2,1)} %copy-done.6), calls=%async_computation.1 | async-start | bytes 1179648 | tf_op jit(solution)/shard_map/all_to_all | solution.py:236
  51.3 3.1 %collective-permute-start.10 = (bf16[384,768]{1,0:T(8,128)(2,1)S(1)}, bf16[384,768]{1,0:T(8,128)(2,1)}, u32[]{:S(2)}, u32[]{:S(2)}) collective-permute-start(bf16[384,768]{1,0:T(8,128)(2,1)S(1)} %collective-permute-done.2.refs_1_.refs_5_), channel_id=1, source_target_pairs={{0,8},{8,0},{1,9},{9,1},{2,10},{10,2},{3,11},{11,3},{4,12},{12,4},... | collective-permute-start | bytes 1769480 | tf_op jit(solution)/shard_map/ppermute | solution.py:224
  55.9 3.1 %collective-permute-start.7 = (bf16[192,768]{1,0:T(8,128)(2,1)}, bf16[192,768]{1,0:T(8,128)(2,1)}, u32[]{:S(2)}, u32[]{:S(2)}) collective-permute-start(bf16[192,768]{1,0:T(8,128)(2,1)} %slice.13), channel_id=1, source_target_pairs={{0,224},{32,0},{64,32},{96,64},{128,96},{160,128},{192,160},{224,1... | collective-permute-start | bytes 884744 | tf_op jit(solution)/shard_map/ppermute | solution.py:244
  59.0 7.6 %attend1.1 = (f32[3,768,128]{2,1,0:T(8,128)S(1)}, f32[3,768,128]{2,1,0:T(8,128)S(1)}, f32[3,768,128]{2,1,0:T(8,128)}) custom-call(bf16[768,384]{1,0:T(8,128)(2,1)S(1)} %bitcast.5, bf16[384,768]{1,0:T(8,128)(2,1)} %collective-permute-done.refs_1_.refs_5_, bf16[384,768]{1,0:T(8,128)(2,1)} %collective-permute-done.4.refs_2_.refs_6_, ...), custom_call_target="tpu_custom_call" | custom-call | flops 1811939328 | bytes 8388608 | tf_op jit(solution)/shard_map/attend1/pallas_call | solution.py:170
  69.3 1.1 copy-done.1
  70.4 11.3 %attend2.1 = (f32[3,768,128]{2,1,0:T(8,128)S(1)}, f32[3,768,128]{2,1,0:T(8,128)}, f32[3,768,128]{2,1,0:T(8,128)}) custom-call(s32[1]{0:T(128)} %bitcast.3.refs_0_, bf16[768,384]{1,0:T(8,128)(2,1)S(1)} %bitcast.6, bf16[384,768]{1,0:T(8,128)(2,1)S(1)} %constant_dynamic-update-slice_fusion.refs_2_.refs_8_, bf16[384,768]{1,0:T(8,128)(2,1)S(1)} %copy-done.1, ...), custom_call_target="tpu_custom_call" | custom-call | flops 2717908992 | bytes 8388608 | tf_op jit(solution)/shard_map/attend2/pallas_call | solution.py:170
  81.7 1.0 copy-done.4
  82.7 8.2 %attend3.1 = (f32[3,768,128]{2,1,0:T(8,128)S(1)}, f32[3,768,128]{2,1,0:T(8,128)S(1)}, f32[3,768,128]{2,1,0:T(8,128)}) custom-call(bf16[768,384]{1,0:T(8,128)(2,1)S(1)} %bitcast.7, bf16[384,768]{1,0:T(8,128)(2,1)S(1)} %collective-permute-done.2.refs_1_.refs_5_, bf16[384,768]{1,0:T(8,128)(2,1)S(1)} %collective-permute-done.6.refs_2_.refs_6_, ...), custom_call_target="tpu_custom_call" | custom-call | flops 1811939328 | bytes 8388608 | tf_op jit(solution)/shard_map/attend3/pallas_call | solution.py:170
  91.0 1.3 %copy-done.5 = f32[3,768,128]{2,1,0:T(8,128)S(1)} copy-done((f32[3,768,128]{2,1,0:T(8,128)S(1)}, f32[3,768,128]{2,1,0:T(8,128)}, u32[]{:S(2)}) %copy-start.5) | copy-done | bytes 1179672
  92.3 6.0 %attend4.1 = bf16[16,64,384]{2,1,0:T(8,128)(2,1)} custom-call(bf16[768,384]{1,0:T(8,128)(2,1)S(1)} %bitcast.8, bf16[192,768]{1,0:T(8,128)(2,1)} %collective-permute-done.3.refs_1_.refs_5_, bf16[192,768]{1,0:T(8,128)(2,1)} %collective-permute-done.7.refs_2_.refs_6_, bf16[192,768]{1,0:T(8,128)(2,1)} %collective-permute-done.8.refs_3_.refs_7_, ...), custom_call_target="tpu_custom_call" | custom-call | flops 905969664 | bytes 8388608 | tf_op jit(solution)/shard_map/attend4/pallas_call | solution.py:170
  98.2 6.8 %all-to-all-start.2 = ((bf16[16,64,384]{2,1,0:T(8,128)(2,1)}), bf16[16,64,384]{2,1,0:T(8,128)(2,1)S(1)}, u32[]{:S(2)}, u32[]{:S(2)}) async-start(bf16[16,64,384]{2,1,0:T(8,128)(2,1)} %attend4.1), calls=%async_computation.2 | async-start | bytes 1572864 | tf_op jit(solution)/shard_map/all_to_all | solution.py:253
  105.7 12.7 %all-to-all-done.2.in_ref = bf16[16,64,384]{2,1,0:T(8,128)(2,1)S(1)} async-done(((bf16[16,64,384]{2,1,0:T(8,128)(2,1)}), bf16[16,64,384]{2,1,0:T(8,128)(2,1)S(1)}, u32[]{:S(2)}, u32[]{:S(2)}) %all-to-all-start.2) | async-done | bytes 786464 | tf_op jit(solution)/shard_map/all_to_all | solution.py:253
  118.4 1.2 merge.1
  (53 shorter events, 9.0 us)
Async XLA Ops:
  0.6 26.3 %copy-start.11 = (f32[3072]{0:T(1024)S(1)}, f32[3072]{0:T(1024)}, u32[]{:S(2)}) copy-start(f32[3072]{0:T(1024)} %param.12) | copy-start | bytes 36868
  0.6 26.2 %copy-start.12 = (f32[3072]{0:T(1024)S(1)}, f32[3072]{0:T(1024)}, u32[]{:S(2)}) copy-start(f32[3072]{0:T(1024)} %param.13) | copy-start | bytes 36868
  0.7 26.2 %copy-start.8 = (bf16[48,3072]{1,0:T(8,128)(2,1)S(1)}, bf16[48,3072]{1,0:T(8,128)(2,1)}, u32[]{:S(2)}) copy-start(bf16[48,3072]{1,0:T(8,128)(2,1)} %q_ref.1) | copy-start | bytes 884740
  0.7 26.2 %copy-start.9 = (bf16[48,3072]{1,0:T(8,128)(2,1)S(1)}, bf16[48,3072]{1,0:T(8,128)(2,1)}, u32[]{:S(2)}) copy-start(bf16[48,3072]{1,0:T(8,128)(2,1)} %k_ref.1) | copy-start | bytes 884740
  2.8 19.6 %collective-permute-start = (bf16[384,768]{1,0:T(8,128)(2,1)S(1)}, bf16[384,768]{1,0:T(8,128)(2,1)}, u32[]{:S(2)}, u32[]{:S(2)}) collective-permute-start(bf16[384,768]{1,0:T(8,128)(2,1)S(1)} %constant_dynamic-update-slice_fusion.refs_2_.refs_8_), channel_id=1, source_target_pairs={{0,32},{32,64},{64,96},{96,128},{128,160},{160,192},{192,224},{224... | collective-permute-start | bytes 1769480 | tf_op jit(solution)/shard_map/ppermute | solution.py:233
  5.3 17.1 %collective-permute-start.4 = (bf16[384,768]{1,0:T(8,128)(2,1)S(1)}, bf16[384,768]{1,0:T(8,128)(2,1)}, u32[]{:S(2)}, u32[]{:S(2)}) collective-permute-start(bf16[384,768]{1,0:T(8,128)(2,1)S(1)} %constant_dynamic-update-slice_fusion.refs_2_.refs_8_), channel_id=1, source_target_pairs={{0,224},{32,0},{64,32},{96,64},{128,96},{160,128},{192,160},{224,1... | collective-permute-start | bytes 1769480 | tf_op jit(solution)/shard_map/ppermute | solution.py:233
  22.4 15.0 %collective-permute-start.1 = (bf16[384,768]{1,0:T(8,128)(2,1)}, bf16[384,768]{1,0:T(8,128)(2,1)S(1)}, u32[]{:S(2)}, u32[]{:S(2)}) collective-permute-start(bf16[384,768]{1,0:T(8,128)(2,1)} %collective-permute-done.refs_1_.refs_5_), channel_id=1, source_target_pairs={{0,32},{32,64},{64,96},{96,128},{128,160},{160,192},{192,224},{224... | collective-permute-start | bytes 1769480 | tf_op jit(solution)/shard_map/ppermute | solution.py:239
  22.4 15.0 %collective-permute-start.5 = (bf16[384,768]{1,0:T(8,128)(2,1)}, bf16[384,768]{1,0:T(8,128)(2,1)}, u32[]{:S(2)}, u32[]{:S(2)}) collective-permute-start(bf16[384,768]{1,0:T(8,128)(2,1)} %collective-permute-done.4.refs_2_.refs_6_), channel_id=1, source_target_pairs={{0,224},{32,0},{64,32},{96,64},{128,96},{160,128},{192,160},{224,1... | collective-permute-start | bytes 1769480 | tf_op jit(solution)/shard_map/ppermute | solution.py:239
  25.1 17.7 %collective-permute-start.12 = (bf16[384,768]{1,0:T(8,128)(2,1)S(1)}, bf16[384,768]{1,0:T(8,128)(2,1)S(1)}, u32[]{:S(2)}, u32[]{:S(2)}) collective-permute-start(bf16[384,768]{1,0:T(8,128)(2,1)S(1)} %constant_dynamic-update-slice_fusion.refs_2_.refs_8_), channel_id=1, source_target_pairs={{0,8},{8,0},{1,9},{9,1},{2,10},{10,2},{3,11},{11,3},{4,12},{12,4},... | collective-permute-start | bytes 1769480 | tf_op jit(solution)/shard_map/ppermute | solution.py:224
  26.9 16.8 %collective-permute-start.15 = (bf16[384,768]{1,0:T(8,128)(2,1)}, bf16[384,768]{1,0:T(8,128)(2,1)}, u32[]{:S(2)}, u32[]{:S(2)}) collective-permute-start(bf16[384,768]{1,0:T(8,128)(2,1)} %collective-permute-done.refs_1_.refs_5_), channel_id=1, source_target_pairs={{0,8},{8,0},{1,9},{9,1},{2,10},{10,2},{3,11},{11,3},{4,12},{12,4},... | collective-permute-start | bytes 1769480 | tf_op jit(solution)/shard_map/ppermute | solution.py:224
  28.1 17.7 %all-to-all-start = ((bf16[16,48,384]{2,1,0:T(8,128)(2,1)}), bf16[16,48,384]{2,1,0:T(8,128)(2,1)S(1)}, u32[]{:S(2)}, u32[]{:S(2)}) async-start(bf16[16,48,384]{2,1,0:T(8,128)(2,1)} %copy-done.7), calls=%async_computation | async-start | bytes 1179648 | tf_op jit(solution)/shard_map/all_to_all | solution.py:234
  37.4 13.9 %collective-permute-start.2 = (bf16[384,768]{1,0:T(8,128)(2,1)S(1)}, bf16[384,768]{1,0:T(8,128)(2,1)S(1)}, u32[]{:S(2)}, u32[]{:S(2)}) collective-permute-start(bf16[384,768]{1,0:T(8,128)(2,1)S(1)} %collective-permute-done.1.refs_4_.refs_10_), channel_id=1, source_target_pairs={{0,32},{32,64},{64,96},{96,128},{128,160},{160,192},{192,224},{224... | collective-permute-start | bytes 1769480 | tf_op jit(solution)/shard_map/ppermute | solution.py:241
  37.4 17.0 %collective-permute-start.6 = (bf16[384,768]{1,0:T(8,128)(2,1)}, bf16[384,768]{1,0:T(8,128)(2,1)S(1)}, u32[]{:S(2)}, u32[]{:S(2)}) collective-permute-start(bf16[384,768]{1,0:T(8,128)(2,1)} %collective-permute-done.5.refs_5_.refs_11_), channel_id=1, source_target_pairs={{0,224},{32,0},{64,32},{96,64},{128,96},{160,128},{192,160},{224,1... | collective-permute-start | bytes 1769480 | tf_op jit(solution)/shard_map/ppermute | solution.py:241
  40.1 15.8 %collective-permute-start.16 = (bf16[384,768]{1,0:T(8,128)(2,1)}, bf16[384,768]{1,0:T(8,128)(2,1)}, u32[]{:S(2)}, u32[]{:S(2)}) collective-permute-start(bf16[384,768]{1,0:T(8,128)(2,1)} %collective-permute-done.4.refs_2_.refs_6_), channel_id=1, source_target_pairs={{0,8},{8,0},{1,9},{9,1},{2,10},{10,2},{3,11},{11,3},{4,12},{12,4},... | collective-permute-start | bytes 1769480 | tf_op jit(solution)/shard_map/ppermute | solution.py:224
  43.6 12.2 %collective-permute-start.13 = (bf16[384,768]{1,0:T(8,128)(2,1)S(1)}, bf16[384,768]{1,0:T(8,128)(2,1)}, u32[]{:S(2)}, u32[]{:S(2)}) collective-permute-start(bf16[384,768]{1,0:T(8,128)(2,1)S(1)} %collective-permute-done.1.refs_4_.refs_10_), channel_id=1, source_target_pairs={{0,8},{8,0},{1,9},{9,1},{2,10},{10,2},{3,11},{11,3},{4,12},{12,4},... | collective-permute-start | bytes 1769480 | tf_op jit(solution)/shard_map/ppermute | solution.py:224
  43.6 25.7 %collective-permute-start.14 = (bf16[384,768]{1,0:T(8,128)(2,1)}, bf16[384,768]{1,0:T(8,128)(2,1)}, u32[]{:S(2)}, u32[]{:S(2)}) collective-permute-start(bf16[384,768]{1,0:T(8,128)(2,1)} %collective-permute-done.5.refs_5_.refs_11_), channel_id=1, source_target_pairs={{0,8},{8,0},{1,9},{9,1},{2,10},{10,2},{3,11},{11,3},{4,12},{12,4},... | collective-permute-start | bytes 1769480 | tf_op jit(solution)/shard_map/ppermute | solution.py:224
  45.8 23.5 %all-to-all-start.1 = ((bf16[8,48,768]{2,1,0:T(8,128)(2,1)}), bf16[8,48,768]{2,1,0:T(8,128)(2,1)S(1)}, u32[]{:S(2)}, u32[]{:S(2)}) async-start(bf16[8,48,768]{2,1,0:T(8,128)(2,1)} %copy-done.6), calls=%async_computation.1 | async-start | bytes 1179648 | tf_op jit(solution)/shard_map/all_to_all | solution.py:236
  51.3 31.4 %collective-permute-start.10 = (bf16[384,768]{1,0:T(8,128)(2,1)S(1)}, bf16[384,768]{1,0:T(8,128)(2,1)}, u32[]{:S(2)}, u32[]{:S(2)}) collective-permute-start(bf16[384,768]{1,0:T(8,128)(2,1)S(1)} %collective-permute-done.2.refs_1_.refs_5_), channel_id=1, source_target_pairs={{0,8},{8,0},{1,9},{9,1},{2,10},{10,2},{3,11},{11,3},{4,12},{12,4},... | collective-permute-start | bytes 1769480 | tf_op jit(solution)/shard_map/ppermute | solution.py:224
  54.4 28.3 %collective-permute-start.11 = (bf16[384,768]{1,0:T(8,128)(2,1)S(1)}, bf16[384,768]{1,0:T(8,128)(2,1)}, u32[]{:S(2)}, u32[]{:S(2)}) collective-permute-start(bf16[384,768]{1,0:T(8,128)(2,1)S(1)} %collective-permute-done.6.refs_2_.refs_6_), channel_id=1, source_target_pairs={{0,8},{8,0},{1,9},{9,1},{2,10},{10,2},{3,11},{11,3},{4,12},{12,4},... | collective-permute-start | bytes 1769480 | tf_op jit(solution)/shard_map/ppermute | solution.py:224
  55.9 12.7 %collective-permute-start.3 = (bf16[192,768]{1,0:T(8,128)(2,1)}, bf16[192,768]{1,0:T(8,128)(2,1)}, u32[]{:S(2)}, u32[]{:S(2)}) collective-permute-start(bf16[192,768]{1,0:T(8,128)(2,1)} %slice.12), channel_id=1, source_target_pairs={{0,32},{32,64},{64,96},{96,128},{128,160},{160,192},{192,224},{224... | collective-permute-start | bytes 884744 | tf_op jit(solution)/shard_map/ppermute | solution.py:244
  55.9 13.3 %collective-permute-start.7 = (bf16[192,768]{1,0:T(8,128)(2,1)}, bf16[192,768]{1,0:T(8,128)(2,1)}, u32[]{:S(2)}, u32[]{:S(2)}) collective-permute-start(bf16[192,768]{1,0:T(8,128)(2,1)} %slice.13), channel_id=1, source_target_pairs={{0,224},{32,0},{64,32},{96,64},{128,96},{160,128},{192,160},{224,1... | collective-permute-start | bytes 884744 | tf_op jit(solution)/shard_map/ppermute | solution.py:244
  68.6 22.4 %collective-permute-start.8 = (bf16[192,768]{1,0:T(8,128)(2,1)}, bf16[192,768]{1,0:T(8,128)(2,1)}, u32[]{:S(2)}, u32[]{:S(2)}) collective-permute-start(bf16[192,768]{1,0:T(8,128)(2,1)} %collective-permute-done.3.refs_1_.refs_5_), channel_id=1, source_target_pairs={{0,8},{8,0},{1,9},{9,1},{2,10},{10,2},{3,11},{11,3},{4,12},{12,4},... | collective-permute-start | bytes 884744 | tf_op jit(solution)/shard_map/ppermute | solution.py:224
  69.2 21.8 %collective-permute-start.9 = (bf16[192,768]{1,0:T(8,128)(2,1)}, bf16[192,768]{1,0:T(8,128)(2,1)}, u32[]{:S(2)}, u32[]{:S(2)}) collective-permute-start(bf16[192,768]{1,0:T(8,128)(2,1)} %collective-permute-done.7.refs_2_.refs_6_), channel_id=1, source_target_pairs={{0,8},{8,0},{1,9},{9,1},{2,10},{10,2},{3,11},{11,3},{4,12},{12,4},... | collective-permute-start | bytes 884744 | tf_op jit(solution)/shard_map/ppermute | solution.py:224
  98.2 20.2 %all-to-all-start.2 = ((bf16[16,64,384]{2,1,0:T(8,128)(2,1)}), bf16[16,64,384]{2,1,0:T(8,128)(2,1)S(1)}, u32[]{:S(2)}, u32[]{:S(2)}) async-start(bf16[16,64,384]{2,1,0:T(8,128)(2,1)} %attend4.1), calls=%async_computation.2 | async-start | bytes 1572864 | tf_op jit(solution)/shard_map/all_to_all | solution.py:253
  (9 other events, 40.1 us)

commit v2 on v1

v2 whole, which is shorter than its diff:
```python
import functools
import jax
import jax.numpy as jnp
from jax import lax
from jax.experimental import pallas as pl
from jax.experimental.pallas import tpu as pltpu
from jax.sharding import Mesh, PartitionSpec as P

HEADS = 24
HD = 128
EPSILON = 1e-06
LOG2E = 1.4426950408889634
SCALE2 = HD**-0.5 * LOG2E
BF = jnp.bfloat16
F32 = jnp.float32
LIMIT = 32 * 2**20
SMALL = 16 * 2**20
ROWS = 64


def norm(src, gain):
    values = src[...].astype(F32)
    mean = jnp.sum(values * values, axis=1, keepdims=True) / src.shape[1]
    return (values * lax.rsqrt(mean + EPSILON) * gain[...]).astype(BF)


def prep_q_kernel(groups, q_ref, gain_ref, out_ref):
    per = q_ref.shape[1] // groups
    q = norm(q_ref, gain_ref)
    for g in range(groups):
        out_ref[g] = q[:, g * per : (g + 1) * per]


def prep_kv_kernel(groups, k_ref, v_ref, gain_ref, out_ref):
    per = k_ref.shape[1] // groups
    k = norm(k_ref, gain_ref)
    for g in range(groups):
        cols = slice(g * per, (g + 1) * per)
        out_ref[g, :, :per] = k[:, cols]
        out_ref[g, :, per:] = v_ref[:, cols]


def prep(kernel, name, groups, gain, *sources):
    rows, width = sources[0].shape
    vmem = pl.BlockSpec(memory_space=pltpu.VMEM)
    return pl.pallas_call(
        functools.partial(kernel, groups),
        out_shape=jax.ShapeDtypeStruct((groups, rows, len(sources) * width // groups), BF),
        in_specs=[vmem] * (len(sources) + 1),
        out_specs=vmem,
        compiler_params=pltpu.CompilerParams(vmem_limit_bytes=SMALL),
        name=name,
    )(*sources, gain[None, :])


def attn_kernel(keys, spans, first, last, *refs):
    refs = list(refs)
    patches = len(spans)
    q_refs = [refs.pop(0) for _ in spans]
    blocks = [refs.pop(0) for _ in keys]
    states = [None if new else (refs.pop(0), refs.pop(0)) for new in first]
    if last:
        base_ref = refs.pop(0)
        out_ref = refs.pop(0)
    else:
        results = [(refs.pop(0), refs.pop(0)) for _ in spans]
    q_buf, k_buf, v_buf, o_buf, lse_buf, sems, out_sem = refs
    nq, width = q_buf.shape
    heads = width // HD
    bq = nq // patches
    total = sum(keys)

    def start(src, dst, sem):
        copy = pltpu.make_async_copy(src, dst, sem)
        copy.start()
        return copy

    early, late = [], []
    off = 0
    for n, block in zip(keys, blocks):
        early.append(start(block.at[:, pl.ds(0, width)], k_buf.at[pl.ds(off, n)], sems.at[0]))
        off += n
    for i, ref in enumerate(q_refs):
        early.append(start(ref, q_buf.at[pl.ds(i * bq, bq)], sems.at[1]))
    off = 0
    for n, block in zip(keys, blocks):
        for h in range(heads):
            src = block.at[:, pl.ds(width + h * HD, HD)]
            late.append(start(src, v_buf.at[h, pl.ds(off, n), pl.ds(0, HD)], sems.at[2]))
        off += n
    for i, state in enumerate(states):
        if state is not None:
            rows = pl.ds(i * bq, bq)
            late.append(start(state[0], o_buf.at[rows], sems.at[3]))
            late.append(start(state[1], lse_buf.at[rows], sems.at[4]))
    for h in range(heads):
        v_buf[h, :, HD:] = jnp.ones((total, HD), BF)
    for copy in early:
        copy.wait()

    def window(i):
        return slice(sum(keys[: spans[i][0]]), sum(keys[: spans[i][1]]))

    def scores(work):
        h, i = work
        cols = slice(h * HD, (h + 1) * HD)
        q = q_buf[i * bq : (i + 1) * bq, cols]
        return lax.dot_general(q, k_buf[window(i), cols], (((1,), (1,)), ((), ())), preferred_element_type=F32)

    tok = ROWS - 16
    lane = lax.broadcasted_iota(jnp.int32, (bq, HD), 1)
    eye = lax.broadcasted_iota(jnp.int32, (tok, HD), 0) == lax.broadcasted_iota(jnp.int32, (tok, HD), 1)
    which = lax.broadcasted_iota(jnp.int32, (16, HD), 0)
    done = [None] * patches

    def rest(work, s):
        h, i = work
        rows, cols = slice(i * bq, (i + 1) * bq), slice(h * HD, (h + 1) * HD)
        m = jnp.max(s, axis=1, keepdims=True) * SCALE2
        if not first[i]:
            lse_old = lse_buf[rows][:, h : h + 1]
            m = jnp.maximum(lse_old, m)
        p = jnp.exp2(s * SCALE2 - m).astype(BF)
        o = jnp.dot(p, v_buf[h, window(i)], preferred_element_type=F32)
        a, l = o[:, :HD], o[:, HD:]
        if not first[i]:
            old = jnp.exp2(lse_old - m)
            a = a + o_buf[rows, cols].astype(F32) * old
            l = l + old
        o = (a / l).astype(BF)
        lse = m + jnp.log(l) * LOG2E
        if not last:
            o_buf[rows, cols] = o
            done[i] = lse if h == 0 else jnp.where(lane == h, lse, done[i])
            if h == heads - 1:
                lse_buf[rows] = done[i]
            return
        for t in range(bq // tok):
            d = base_ref[i] + t
            out_ref[d, :tok, cols] = o[t * tok : (t + 1) * tok]
            row = jnp.sum(jnp.where(eye, lse[t * tok : (t + 1) * tok], 0.0), axis=0, keepdims=True)
            hi = row.astype(BF).astype(F32)
            mid = (row - hi).astype(BF).astype(F32)
            low = row - hi - mid
            packed = jnp.where(which == 0, hi, jnp.where(which == 1, mid, jnp.where(which == 2, low, 0.0)))
            out_ref[d, tok:, cols] = packed.astype(BF)

    pending = None
    for work in [(h, i) for h in range(heads) for i in range(patches)]:
        s = scores(work)
        if pending is None:
            for copy in late:
                copy.wait()
        else:
            rest(*pending)
        pending = (work, s)
    rest(*pending)
    if not last:
        stores = []
        for i, (o_hbm, lse_hbm) in enumerate(results):
            rows = pl.ds(i * bq, bq)
            stores.append(start(o_buf.at[rows], o_hbm, out_sem.at[0]))
            stores.append(start(lse_buf.at[rows], lse_hbm, out_sem.at[1]))
        for copy in stores:
            copy.wait()


def attend(qs, blocks, states=None, spans=None, base=None, name="attend"):
    bq, width = qs[0].shape
    patches = len(qs)
    nq = patches * bq
    heads = width // HD
    keys = tuple(b.shape[0] for b in blocks)
    states = states or [None] * patches
    spans = spans or [(0, len(keys))] * patches
    first, last = [s is None for s in states], base is not None
    total = sum(keys)
    hbm = pl.BlockSpec(memory_space=pl.ANY)
    args = [*qs, *blocks]
    alias = {}
    for i, state in enumerate(states):
        if state is not None:
            if not last:
                alias |= {len(args): 2 * i, len(args) + 1: 2 * i + 1}
            args += list(state)
    specs = [hbm] * len(args)
    if last:
        args.append(base)
        specs.append(pl.BlockSpec(memory_space=pltpu.SMEM))
        out_shape = jax.ShapeDtypeStruct((nq // (ROWS - 16), ROWS, width), BF)
        out_specs = pl.BlockSpec(memory_space=pltpu.VMEM)
    else:
        out_shape = [jax.ShapeDtypeStruct((bq, width), BF), jax.ShapeDtypeStruct((bq, HD), F32)] * patches
        out_specs = [hbm] * len(out_shape)
    seen = sum(sum(keys[a:b]) for a, b in spans)
    out = pl.pallas_call(
        functools.partial(attn_kernel, keys, spans, first, last),
        in_specs=specs,
        out_specs=out_specs,
        out_shape=out_shape,
        scratch_shapes=[
            pltpu.VMEM((nq, width), BF),
            pltpu.VMEM((total, width), BF),
            pltpu.VMEM((heads, total, 2 * HD), BF),
            pltpu.VMEM((nq, width), BF),
            pltpu.VMEM((nq, HD), F32),
            pltpu.SemaphoreType.DMA((5,)),
            pltpu.SemaphoreType.DMA((2,)),
        ],
        input_output_aliases=alias,
        compiler_params=pltpu.CompilerParams(vmem_limit_bytes=LIMIT),
        cost_estimate=pl.CostEstimate(flops=4 * bq * seen * width, bytes_accessed=2**20, transcendentals=bq * seen * heads),
        name=name,
    )(*args)
    return out if last else [out[2 * i : 2 * i + 2] for i in range(patches)]


def merge_kernel(groups, copies, in_ref, out_ref):
    tok = ROWS - 16
    heads = in_ref.shape[2] // HD
    eye = lax.broadcasted_iota(jnp.int32, (tok, HD), 0) == lax.broadcasted_iota(jnp.int32, (tok, HD), 1)
    for g in range(groups):
        for h in range(heads):
            cols = slice(h * HD, (h + 1) * HD)
            lses = []
            for c in range(copies):
                packed = in_ref[c * groups + g, tok:, cols].astype(F32)
                row = jnp.sum(packed, axis=0, keepdims=True)
                lses.append(jnp.sum(jnp.where(eye, jnp.broadcast_to(row, (tok, HD)), 0.0), axis=1, keepdims=True))
            top = functools.reduce(jnp.maximum, lses)
            weights = [jnp.exp2(x - top) for x in lses]
            total = sum(weights)
            acc = 0.0
            for c in range(copies):
                acc = acc + in_ref[c * groups + g, :tok, cols].astype(F32) * (weights[c] / total)
            first = (g * heads + h) * HD
            out_ref[:, first : first + HD] = acc.astype(BF)


def merge(parts, groups, copies):
    width = parts.shape[2] * groups
    return pl.pallas_call(
        functools.partial(merge_kernel, groups, copies),
        out_shape=jax.ShapeDtypeStruct((ROWS - 16, width), BF),
        in_specs=[pl.BlockSpec(memory_space=pltpu.VMEM)],
        out_specs=pl.BlockSpec(memory_space=pltpu.VMEM),
        compiler_params=pltpu.CompilerParams(vmem_limit_bytes=SMALL),
        name="merge",
    )(parts)


Z, YL, CORE, X, YH = 8, 2, 2, 4, 2
UP = [(i, (i + 1) % Z) for i in range(Z)]
DOWN = [(i, (i - 1) % Z) for i in range(Z)]
SWAP = [(0, 1), (1, 0)]


def other_core(x):
    return lax.ppermute(x, "core", SWAP)


def body(fresh_q, fresh_k, fresh_v, stale_k, stale_v, q_gain, k_gain):
    groups = X * YH
    width_dev = stale_k.shape[1]
    half = stale_k.shape[0] // 2
    yl = lax.axis_index("yl").astype(jnp.int32)
    base = jnp.stack([yl * groups, (1 - yl) * groups])

    def both(pair):
        return lax.ppermute(pair[0], "z", UP), lax.ppermute(pair[1], "z", DOWN)

    def swap(pair):
        return other_core(pair[0]), other_core(pair[1])

    own = jnp.concatenate([stale_k, stale_v], axis=1)
    r1 = both((own, own))
    q_parts = prep(prep_q_kernel, "prep_q", groups, q_gain, fresh_q)
    q = lax.all_to_all(q_parts, ("x", "yh"), split_axis=0, concat_axis=0, tiled=True)
    kv_parts = prep(prep_kv_kernel, "prep_kv", groups, k_gain, fresh_k, fresh_v)
    r1, q, kv_parts = lax.optimization_barrier((r1, q, kv_parts))
    q = q.reshape(-1, width_dev)
    qs = [q, lax.ppermute(q, "yl", SWAP)]
    r2 = both(r1)
    fresh = lax.all_to_all(kv_parts, ("x", "yh"), split_axis=0, concat_axis=0, tiled=True)
    own_other = other_core(own)
    r1 = [*r1, *swap(r1)]
    early = attend(qs[:1], [own_other, *r1], name="attend1")
    r2, qs[1], fresh, early = lax.optimization_barrier((r2, qs[1], fresh, early))
    fresh = fresh.reshape(-1, 2 * width_dev)

    r3 = both(r2)
    blocks = [own, own_other, *r1, *r2, *swap(r2), fresh]
    state = attend(qs, blocks, [early[0], None], [(6, 11), (0, 10)], name="attend2")
    r3, state = lax.optimization_barrier((r3, state))
    r4 = both((r3[0][:half], r3[1][half:]))
    state = attend(qs, [*r3, *swap(r3)], state, name="attend3")
    r4, state = lax.optimization_barrier((r4, state))
    parts = attend(qs, [*r4, *swap(r4)], state, base=base, name="attend4")
    back = lax.all_to_all(parts, ("yl", "x", "yh"), split_axis=0, concat_axis=0, tiled=True)
    return merge(back, groups, YL), fresh[:, :width_dev]


def solution(mesh):
    fine = Mesh(mesh.devices.reshape(Z, YL, CORE, X, YH), ("z", "yl", "core", "x", "yh"))
    patch, head = ("z", "yl", "core"), ("x", "yh")
    tokens = P(patch + head, None)
    tiles = P(patch, head)
    return jax.shard_map(
        body,
        mesh=fine,
        in_specs=(tokens, tokens, tokens, tiles, tiles, P(), P()),
        out_specs=(tokens, tiles),
        check_vma=False,
    )
```

time: 120 us -> 107 us (0.89); the launches traced: 120 us -> 105 us
  local copies, waits for them, and re-layouts: 11.3 us -> 5.91 us
  waiting for transfers between devices: 30.5 us -> 26.3 us
  Pallas kernels: 34.6 us -> 31.7 us
  starting transfers between devices: 42.4 us -> 40.2 us
    ppermute x8 -> x9, waiting for transfers between devices: 16.1 us -> 6.91 us  [the longest x1 6.89 us: body(): qs = [q, lax.ppermute(q, 'yl', SWAP)]]
    all_to_all x1, waiting for transfers between devices: 1.64 us -> 5.19 us  [body(): lax.all_to_all(q_parts, ('x', 'yh'), split_axis=0, concat_axis=0, tiled=T...]
    unnamed x27 -> x23, local copies, waits for them, and re-layouts: 8.12 us -> 5.07 us
    pallas_call x5 -> x6, Pallas kernels: 33.4 us -> 30.5 us  [the longest x4 28.6 us: attend(): pl.pallas_call(functools.partial(attn_kernel, keys, spans, first, last),...]
    all_to_all x1, starting transfers between devices: 5.01 us -> 3.54 us  [body(): lax.all_to_all(kv_parts, ('x', 'yh'), split_axis=0, concat_axis=0, tiled=...]
    ppermute x9, waiting for transfers between devices: 0.02 us -> 1.47 us  [other_core(): return lax.ppermute(x, 'core', SWAP)]
    slice x2, local copies, waits for them, and re-layouts: 1.47 us -> 0.04 us  [body(): r4 = both((r3[0][:half], r3[1][half:]))]
    ppermute x8 -> x9, starting transfers between devices: 15.1 us -> 15.3 us  [the longest x8 14.9 us: both(): return (lax.ppermute(pair[0], 'z', UP), lax.ppermute(pair[1], 'z', DOWN))]
  transfers between devices with their start and end apart: 20 -> 21, of which waited for: 5 -> 5; matrix products, arithmetic and copies ran while one was open for 2% -> 1% of each run, Pallas kernels for 23% -> 24%
where the time goes in v2:
time: 107 us; the launch traced here: 105 us
  starting transfers between devices  40.2 us (38%)
  Pallas kernels  31.7 us (30%)
  waiting for transfers between devices  26.3 us (25%)
  local copies, waits for them, and re-layouts  5.91 us (6%)
    pallas_call x4, Pallas kernels, attend(): pl.pallas_call(functools.partial(attn_kernel, keys, spans, first, last),...  28.6 us
    ppermute x8, starting transfers between devices, both(): return (lax.ppermute(pair[0], 'z', UP), lax.ppermute(pair[1], 'z', DOWN))  14.9 us
    all_to_all x1, waiting for transfers between devices, body(): lax.all_to_all(parts, ('yl', 'x', 'yh'), split_axis=0, concat_axis=0, til...  12.7 us
    ppermute x9, starting transfers between devices, other_core(): return lax.ppermute(x, 'core', SWAP)  7.64 us
    all_to_all x1, starting transfers between devices, body(): lax.all_to_all(parts, ('yl', 'x', 'yh'), split_axis=0, concat_axis=0, til...  6.98 us
    ppermute x1, waiting for transfers between devices, body(): qs = [q, lax.ppermute(q, 'yl', SWAP)]  6.89 us
    all_to_all x1, starting transfers between devices, body(): lax.all_to_all(q_parts, ('x', 'yh'), split_axis=0, concat_axis=0, tiled=T...  6.78 us
    all_to_all x1, waiting for transfers between devices, body(): lax.all_to_all(q_parts, ('x', 'yh'), split_axis=0, concat_axis=0, tiled=T...  5.19 us
  transfers between devices with their start and end apart: 21, of which 5 were waited for; matrix products, arithmetic and copies ran while one was open for 1% of the time, Pallas kernels for 24%

profile of v2, /device:TPU:1, one launch (start us, length us, event | category | flops | bytes accessed | tf_op | source)
XLA Modules:
  0.0 105.0 jit_solution(12450596460713636972)
XLA Ops:
  1.8 2.5 %collective-permute-start = (bf16[384,768]{1,0:T(8,128)(2,1)S(1)}, bf16[384,768]{1,0:T(8,128)(2,1)S(1)}, u32[]{:S(2)}, u32[]{:S(2)}) collective-permute-start(bf16[384,768]{1,0:T(8,128)(2,1)S(1)} %constant_dynamic-update-slice_fusion.refs_2_), channel_id=1, source_target_pairs={{0,32},{32,64},{64,96},{96,128},{128,160},{160,192},{192,224},{224... | collective-permute-start | bytes 1769480 | tf_op jit(solution)/shard_map/ppermute | solution.py:270
  4.3 4.0 %collective-permute-start.1 = (bf16[384,768]{1,0:T(8,128)(2,1)S(1)}, bf16[384,768]{1,0:T(8,128)(2,1)}, u32[]{:S(2)}, u32[]{:S(2)}) collective-permute-start(bf16[384,768]{1,0:T(8,128)(2,1)S(1)} %constant_dynamic-update-slice_fusion.refs_2_), channel_id=1, source_target_pairs={{0,224},{32,0},{64,32},{96,64},{128,96},{160,128},{192,160},{224,1... | collective-permute-start | bytes 1769480 | tf_op jit(solution)/shard_map/ppermute | solution.py:270
  9.2 6.8 %all-to-all-start = ((bf16[8,48,384]{2,1,0:T(8,128)(2,1)}), bf16[8,48,384]{2,1,0:T(8,128)(2,1)S(1)}, u32[]{:S(2)}, u32[]{:S(2)}) async-start(bf16[8,48,384]{2,1,0:T(8,128)(2,1)} %prep_q.1), calls=%async_computation | async-start | bytes 589824 | tf_op jit(solution)/shard_map/all_to_all | solution.py:278
  16.0 1.2 %collective-permute-start.5 = (bf16[384,768]{1,0:T(8,128)(2,1)S(1)}, bf16[384,768]{1,0:T(8,128)(2,1)S(1)}, u32[]{:S(2)}, u32[]{:S(2)}) collective-permute-start(bf16[384,768]{1,0:T(8,128)(2,1)S(1)} %constant_dynamic-update-slice_fusion.refs_2_), channel_id=1, source_target_pairs={{0,8},{8,0},{1,9},{9,1},{2,10},{10,2},{3,11},{11,3},{4,12},{12,4},... | collective-permute-start | bytes 1769480 | tf_op jit(solution)/shard_map/ppermute | solution.py:259
  18.3 5.2 %all-to-all-done = bf16[8,48,384]{2,1,0:T(8,128)(2,1)S(1)} async-done(((bf16[8,48,384]{2,1,0:T(8,128)(2,1)}), bf16[8,48,384]{2,1,0:T(8,128)(2,1)S(1)}, u32[]{:S(2)}, u32[]{:S(2)}) %all-to-all-start) | async-done | bytes 294944 | tf_op jit(solution)/shard_map/all_to_all | solution.py:278
  23.5 2.6 %collective-permute-start.6 = (bf16[384,768]{1,0:T(8,128)(2,1)S(1)}, bf16[384,768]{1,0:T(8,128)(2,1)}, u32[]{:S(2)}, u32[]{:S(2)}) collective-permute-start(bf16[384,768]{1,0:T(8,128)(2,1)S(1)} %collective-permute-done.refs_2_.refs_4_), channel_id=1, source_target_pairs={{0,8},{8,0},{1,9},{9,1},{2,10},{10,2},{3,11},{11,3},{4,12},{12,4},... | collective-permute-start | bytes 1769480 | tf_op jit(solution)/shard_map/ppermute | solution.py:259
  26.2 2.7 %collective-permute-start.3 = (bf16[384,768]{1,0:T(8,128)(2,1)}, bf16[384,768]{1,0:T(8,128)(2,1)}, u32[]{:S(2)}, u32[]{:S(2)}) collective-permute-start(bf16[384,768]{1,0:T(8,128)(2,1)} %collective-permute-done.1.refs_3_.refs_5_), channel_id=1, source_target_pairs={{0,224},{32,0},{64,32},{96,64},{128,96},{160,128},{192,160},{224,1... | collective-permute-start | bytes 1769480 | tf_op jit(solution)/shard_map/ppermute | solution.py:270
  28.9 3.5 %all-to-all-start.1 = ((bf16[8,48,768]{2,1,0:T(8,128)(2,1)}), bf16[8,48,768]{2,1,0:T(8,128)(2,1)S(1)}, u32[]{:S(2)}, u32[]{:S(2)}) async-start(bf16[8,48,768]{2,1,0:T(8,128)(2,1)} %prep_kv.1), calls=%async_computation.1 | async-start | bytes 1179648 | tf_op jit(solution)/shard_map/all_to_all | solution.py:284
  33.7 1.1 %copy-done.8 = bf16[384,768]{1,0:T(8,128)(2,1)S(1)} copy-done((bf16[384,768]{1,0:T(8,128)(2,1)S(1)}, bf16[384,768]{1,0:T(8,128)(2,1)}, u32[]{:S(2)}) %copy-start.8) | copy-done | bytes 589848
  34.7 4.8 %attend1.1 = (bf16[384,384]{1,0:T(8,128)(2,1)S(1)}, f32[384,128]{1,0:T(8,128)S(1)}) custom-call(bf16[384,384]{1,0:T(8,128)(2,1)S(1)} %bitcast.9, bf16[384,768]{1,0:T(8,128)(2,1)S(1)} %copy-done.8, bf16[384,768]{1,0:T(8,128)(2,1)S(1)} %collective-permute-done.refs_2_.refs_4_, bf16[384,768]{1,0:T(8,128)(2,1)} %collective-permute-done.1.refs_3_.refs_5_, ...), custom_call_target="tpu_custom_call" | custom-call | flops 1132462080 | bytes 1048576 | tf_op jit(solution)/shard_map/attend1/pallas_call | solution.py:196
  39.6 6.9 %collective-permute-done.4.refs_1_ = bf16[384,384]{1,0:T(8,128)(2,1)S(1)} collective-permute-done((bf16[384,384]{1,0:T(8,128)(2,1)S(1)}, bf16[384,384]{1,0:T(8,128)(2,1)S(1)}, u32[]{:S(2)}, u32[]{:S(2)}) %collective-permute-start.4) | collective-permute-done | bytes 294944 | tf_op jit(solution)/shard_map/ppermute | solution.py:282
  46.5 1.2 %collective-permute-start.10 = (bf16[384,768]{1,0:T(8,128)(2,1)}, bf16[384,768]{1,0:T(8,128)(2,1)S(1)}, u32[]{:S(2)}, u32[]{:S(2)}) collective-permute-start(bf16[384,768]{1,0:T(8,128)(2,1)} %collective-permute-done.2.refs_8_), channel_id=1, source_target_pairs={{0,8},{8,0},{1,9},{9,1},{2,10},{10,2},{3,11},{11,3},{4,12},{12,4},... | collective-permute-start | bytes 1769480 | tf_op jit(solution)/shard_map/ppermute | solution.py:259
  47.8 2.7 %collective-permute-start.9 = (bf16[384,768]{1,0:T(8,128)(2,1)}, bf16[384,768]{1,0:T(8,128)(2,1)S(1)}, u32[]{:S(2)}, u32[]{:S(2)}) collective-permute-start(bf16[384,768]{1,0:T(8,128)(2,1)} %collective-permute-done.3.refs_9_), channel_id=1, source_target_pairs={{0,224},{32,0},{64,32},{96,64},{128,96},{160,128},{192,160},{224,1... | collective-permute-start | bytes 1769480 | tf_op jit(solution)/shard_map/ppermute | solution.py:270
  50.5 1.1 %copy-done.6 = bf16[384,768]{1,0:T(8,128)(2,1)S(1)} copy-done((bf16[384,768]{1,0:T(8,128)(2,1)S(1)}, bf16[384,768]{1,0:T(8,128)(2,1)}, u32[]{:S(2)}) %copy-start.6) | copy-done | bytes 589848
  51.6 1.1 %copy-done.9 = bf16[384,768]{1,0:T(8,128)(2,1)S(1)} copy-done((bf16[384,768]{1,0:T(8,128)(2,1)S(1)}, bf16[384,768]{1,0:T(8,128)(2,1)}, u32[]{:S(2)}) %copy-start.9) | copy-done | bytes 589848
  52.6 11.2 %attend2.1 = (bf16[384,384]{1,0:T(8,128)(2,1)S(1)}, f32[384,128]{1,0:T(8,128)S(1)}, bf16[384,384]{1,0:T(8,128)(2,1)S(1)}, f32[384,128]{1,0:T(8,128)S(1)}) custom-call(bf16[384,384]{1,0:T(8,128)(2,1)S(1)} %bitcast.10, bf16[384,384]{1,0:T(8,128)(2,1)S(1)} %collective-permute-done.4.refs_1_, ...), custom_call_target="tpu_custom_call", output_to_operand_aliasing={{0}: (13, {}), {1}: (14, {})} | custom-call | flops 3397386240 | bytes 1048576 | tf_op jit(solution)/shard_map/attend2/pallas_call | solution.py:196
  63.9 1.1 %collective-permute-start.14 = (bf16[384,768]{1,0:T(8,128)(2,1)S(1)}, bf16[384,768]{1,0:T(8,128)(2,1)S(1)}, u32[]{:S(2)}, u32[]{:S(2)}) collective-permute-start(bf16[384,768]{1,0:T(8,128)(2,1)S(1)} %collective-permute-done.8.refs_2_), channel_id=1, source_target_pairs={{0,8},{8,0},{1,9},{9,1},{2,10},{10,2},{3,11},{11,3},{4,12},{12,4},... | collective-permute-start | bytes 1769480 | tf_op jit(solution)/shard_map/ppermute | solution.py:259
  65.9 2.2 %collective-permute-start.13 = (bf16[192,768]{1,0:T(8,128)(2,1)S(1)}, bf16[192,768]{1,0:T(8,128)(2,1)S(1)}, u32[]{:S(2)}, u32[]{:S(2)}) collective-permute-start(bf16[192,768]{1,0:T(8,128)(2,1)S(1)} %slice.10), channel_id=1, source_target_pairs={{0,224},{32,0},{64,32},{96,64},{128,96},{160,128},{192,160},{224,1... | collective-permute-start | bytes 884744 | tf_op jit(solution)/shard_map/ppermute | solution.py:270
  68.1 6.9 %attend3.1 = (bf16[384,384]{1,0:T(8,128)(2,1)S(1)}, f32[384,128]{1,0:T(8,128)S(1)}, bf16[384,384]{1,0:T(8,128)(2,1)S(1)}, f32[384,128]{1,0:T(8,128)S(1)}) custom-call(bf16[384,384]{1,0:T(8,128)(2,1)S(1)} %bitcast.11, bf16[384,384]{1,0:T(8,128)(2,1)S(1)} %collective-permute-done.4.refs_1_, ...), custom_call_target="tpu_custom_call", output_to_operand_aliasing={{0}: (6, {}), {1}: (7, {}), {2}: (8, {}), {3}: (9, {})} | custom-call | flops 1811939328 | bytes 1048576 | tf_op jit(solution)/shard_map/attend3/pallas_call | solution.py:196
  75.0 1.1 %collective-permute-start.16 = (bf16[192,768]{1,0:T(8,128)(2,1)S(1)}, bf16[192,768]{1,0:T(8,128)(2,1)S(1)}, u32[]{:S(2)}, u32[]{:S(2)}) collective-permute-start(bf16[192,768]{1,0:T(8,128)(2,1)S(1)} %collective-permute-done.12.refs_2_), channel_id=1, source_target_pairs={{0,8},{8,0},{1,9},{9,1},{2,10},{10,2},{3,11},{11,3},{4,12},{12,4},... | collective-permute-start | bytes 884744 | tf_op jit(solution)/shard_map/ppermute | solution.py:259
  77.7 5.7 %attend4.1 = bf16[16,64,384]{2,1,0:T(8,128)(2,1)} custom-call(bf16[384,384]{1,0:T(8,128)(2,1)S(1)} %bitcast.12, bf16[384,384]{1,0:T(8,128)(2,1)S(1)} %collective-permute-done.4.refs_1_, bf16[192,768]{1,0:T(8,128)(2,1)S(1)} %collective-permute-done.12.refs_2_, bf16[192,768]{1,0:T(8,128)(2,1)S(1)} %collective-permute-done.13.refs_3_, ...), custom_call_target="tpu_custom_call" | custom-call | flops 905969664 | bytes 1048576 | tf_op jit(solution)/shard_map/attend4/pallas_call | solution.py:196
  83.4 7.0 %all-to-all-start.2 = ((bf16[16,64,384]{2,1,0:T(8,128)(2,1)}), bf16[16,64,384]{2,1,0:T(8,128)(2,1)S(1)}, u32[]{:S(2)}, u32[]{:S(2)}) async-start(bf16[16,64,384]{2,1,0:T(8,128)(2,1)} %attend4.1), calls=%async_computation.2 | async-start | bytes 1572864 | tf_op jit(solution)/shard_map/all_to_all | solution.py:299
  91.1 12.7 %all-to-all-done.2.in_ref = bf16[16,64,384]{2,1,0:T(8,128)(2,1)S(1)} async-done(((bf16[16,64,384]{2,1,0:T(8,128)(2,1)}), bf16[16,64,384]{2,1,0:T(8,128)(2,1)S(1)}, u32[]{:S(2)}, u32[]{:S(2)}) %all-to-all-start.2) | async-done | bytes 786464 | tf_op jit(solution)/shard_map/all_to_all | solution.py:299
  103.8 1.2 %merge.1 = bf16[48,3072]{1,0:T(8,128)(2,1)} custom-call(bf16[16,64,384]{2,1,0:T(8,128)(2,1)S(1)} %all-to-all-done.2.in_ref), custom_call_target="tpu_custom_call" | custom-call | tf_op jit(solution)/shard_map/merge/pallas_call | solution.py:242
  (53 shorter events, 7.8 us)
Async XLA Ops:
  1.8 21.7 %collective-permute-start = (bf16[384,768]{1,0:T(8,128)(2,1)S(1)}, bf16[384,768]{1,0:T(8,128)(2,1)S(1)}, u32[]{:S(2)}, u32[]{:S(2)}) collective-permute-start(bf16[384,768]{1,0:T(8,128)(2,1)S(1)} %constant_dynamic-update-slice_fusion.refs_2_), channel_id=1, source_target_pairs={{0,32},{32,64},{64,96},{96,128},{128,160},{160,192},{192,224},{224... | collective-permute-start | bytes 1769480 | tf_op jit(solution)/shard_map/ppermute | solution.py:270
  4.3 19.1 %collective-permute-start.1 = (bf16[384,768]{1,0:T(8,128)(2,1)S(1)}, bf16[384,768]{1,0:T(8,128)(2,1)}, u32[]{:S(2)}, u32[]{:S(2)}) collective-permute-start(bf16[384,768]{1,0:T(8,128)(2,1)S(1)} %constant_dynamic-update-slice_fusion.refs_2_), channel_id=1, source_target_pairs={{0,224},{32,0},{64,32},{96,64},{128,96},{160,128},{192,160},{224,1... | collective-permute-start | bytes 1769480 | tf_op jit(solution)/shard_map/ppermute | solution.py:270
  8.3 8.9 %copy-start.3 = (f32[3072]{0:T(1024)S(1)}, f32[3072]{0:T(1024)}, u32[]{:S(2)}) copy-start(f32[3072]{0:T(1024)} %param.13) | copy-start | bytes 36868
  9.2 8.0 %copy-start.2 = (bf16[48,3072]{1,0:T(8,128)(2,1)S(1)}, bf16[48,3072]{1,0:T(8,128)(2,1)}, u32[]{:S(2)}) copy-start(bf16[48,3072]{1,0:T(8,128)(2,1)} %v_ref.1) | copy-start | bytes 884740
  9.2 14.2 %all-to-all-start = ((bf16[8,48,384]{2,1,0:T(8,128)(2,1)}), bf16[8,48,384]{2,1,0:T(8,128)(2,1)S(1)}, u32[]{:S(2)}, u32[]{:S(2)}) async-start(bf16[8,48,384]{2,1,0:T(8,128)(2,1)} %prep_q.1), calls=%async_computation | async-start | bytes 589824 | tf_op jit(solution)/shard_map/all_to_all | solution.py:278
  16.0 16.4 %collective-permute-start.5 = (bf16[384,768]{1,0:T(8,128)(2,1)S(1)}, bf16[384,768]{1,0:T(8,128)(2,1)S(1)}, u32[]{:S(2)}, u32[]{:S(2)}) collective-permute-start(bf16[384,768]{1,0:T(8,128)(2,1)S(1)} %constant_dynamic-update-slice_fusion.refs_2_), channel_id=1, source_target_pairs={{0,8},{8,0},{1,9},{9,1},{2,10},{10,2},{3,11},{11,3},{4,12},{12,4},... | collective-permute-start | bytes 1769480 | tf_op jit(solution)/shard_map/ppermute | solution.py:259
  23.4 10.2 %copy-start.5 = (bf16[384,768]{1,0:T(8,128)(2,1)}, bf16[384,768]{1,0:T(8,128)(2,1)S(1)}, u32[]{:S(2)}) copy-start(bf16[384,768]{1,0:T(8,128)(2,1)S(1)} %collective-permute-done.refs_2_.refs_4_) | copy-start | bytes 1769476
  23.5 10.2 %collective-permute-start.6 = (bf16[384,768]{1,0:T(8,128)(2,1)S(1)}, bf16[384,768]{1,0:T(8,128)(2,1)}, u32[]{:S(2)}, u32[]{:S(2)}) collective-permute-start(bf16[384,768]{1,0:T(8,128)(2,1)S(1)} %collective-permute-done.refs_2_.refs_4_), channel_id=1, source_target_pairs={{0,8},{8,0},{1,9},{9,1},{2,10},{10,2},{3,11},{11,3},{4,12},{12,4},... | collective-permute-start | bytes 1769480 | tf_op jit(solution)/shard_map/ppermute | solution.py:259
  26.1 7.6 %collective-permute-start.7 = (bf16[384,768]{1,0:T(8,128)(2,1)}, bf16[384,768]{1,0:T(8,128)(2,1)}, u32[]{:S(2)}, u32[]{:S(2)}) collective-permute-start(bf16[384,768]{1,0:T(8,128)(2,1)} %collective-permute-done.1.refs_3_.refs_5_), channel_id=1, source_target_pairs={{0,8},{8,0},{1,9},{9,1},{2,10},{10,2},{3,11},{11,3},{4,12},{12,4},... | collective-permute-start | bytes 1769480 | tf_op jit(solution)/shard_map/ppermute | solution.py:259
  26.2 20.3 %collective-permute-start.2 = (bf16[384,768]{1,0:T(8,128)(2,1)S(1)}, bf16[384,768]{1,0:T(8,128)(2,1)}, u32[]{:S(2)}, u32[]{:S(2)}) collective-permute-start(bf16[384,768]{1,0:T(8,128)(2,1)S(1)} %collective-permute-done.refs_2_.refs_4_), channel_id=1, source_target_pairs={{0,32},{32,64},{64,96},{96,128},{128,160},{160,192},{192,224},{224... | collective-permute-start | bytes 1769480 | tf_op jit(solution)/shard_map/ppermute | solution.py:270
  26.2 20.3 %collective-permute-start.3 = (bf16[384,768]{1,0:T(8,128)(2,1)}, bf16[384,768]{1,0:T(8,128)(2,1)}, u32[]{:S(2)}, u32[]{:S(2)}) collective-permute-start(bf16[384,768]{1,0:T(8,128)(2,1)} %collective-permute-done.1.refs_3_.refs_5_), channel_id=1, source_target_pairs={{0,224},{32,0},{64,32},{96,64},{128,96},{160,128},{192,160},{224,1... | collective-permute-start | bytes 1769480 | tf_op jit(solution)/shard_map/ppermute | solution.py:270
  28.9 17.6 %all-to-all-start.1 = ((bf16[8,48,768]{2,1,0:T(8,128)(2,1)}), bf16[8,48,768]{2,1,0:T(8,128)(2,1)S(1)}, u32[]{:S(2)}, u32[]{:S(2)}) async-start(bf16[8,48,768]{2,1,0:T(8,128)(2,1)} %prep_kv.1), calls=%async_computation.1 | async-start | bytes 1179648 | tf_op jit(solution)/shard_map/all_to_all | solution.py:284
  33.3 13.2 %collective-permute-start.4 = (bf16[384,384]{1,0:T(8,128)(2,1)S(1)}, bf16[384,384]{1,0:T(8,128)(2,1)S(1)}, u32[]{:S(2)}, u32[]{:S(2)}) collective-permute-start(bf16[384,384]{1,0:T(8,128)(2,1)S(1)} %bitcast.8), channel_id=1, source_target_pairs={{0,16},{16,0},{1,17},{17,1},{2,18},{18,2},{3,19},{19,3},{4,20},{20... | collective-permute-start | bytes 884744 | tf_op jit(solution)/shard_map/ppermute | solution.py:282
  46.5 4.0 %collective-permute-start.10 = (bf16[384,768]{1,0:T(8,128)(2,1)}, bf16[384,768]{1,0:T(8,128)(2,1)S(1)}, u32[]{:S(2)}, u32[]{:S(2)}) collective-permute-start(bf16[384,768]{1,0:T(8,128)(2,1)} %collective-permute-done.2.refs_8_), channel_id=1, source_target_pairs={{0,8},{8,0},{1,9},{9,1},{2,10},{10,2},{3,11},{11,3},{4,12},{12,4},... | collective-permute-start | bytes 1769480 | tf_op jit(solution)/shard_map/ppermute | solution.py:259
  47.7 2.8 %collective-permute-start.11 = (bf16[384,768]{1,0:T(8,128)(2,1)}, bf16[384,768]{1,0:T(8,128)(2,1)S(1)}, u32[]{:S(2)}, u32[]{:S(2)}) collective-permute-start(bf16[384,768]{1,0:T(8,128)(2,1)} %collective-permute-done.3.refs_9_), channel_id=1, source_target_pairs={{0,8},{8,0},{1,9},{9,1},{2,10},{10,2},{3,11},{11,3},{4,12},{12,4},... | collective-permute-start | bytes 1769480 | tf_op jit(solution)/shard_map/ppermute | solution.py:259
  47.8 16.1 %collective-permute-start.8 = (bf16[384,768]{1,0:T(8,128)(2,1)}, bf16[384,768]{1,0:T(8,128)(2,1)S(1)}, u32[]{:S(2)}, u32[]{:S(2)}) collective-permute-start(bf16[384,768]{1,0:T(8,128)(2,1)} %collective-permute-done.2.refs_8_), channel_id=1, source_target_pairs={{0,32},{32,64},{64,96},{96,128},{128,160},{160,192},{192,224},{224... | collective-permute-start | bytes 1769480 | tf_op jit(solution)/shard_map/ppermute | solution.py:270
  47.8 16.1 %collective-permute-start.9 = (bf16[384,768]{1,0:T(8,128)(2,1)}, bf16[384,768]{1,0:T(8,128)(2,1)S(1)}, u32[]{:S(2)}, u32[]{:S(2)}) collective-permute-start(bf16[384,768]{1,0:T(8,128)(2,1)} %collective-permute-done.3.refs_9_), channel_id=1, source_target_pairs={{0,224},{32,0},{64,32},{96,64},{128,96},{160,128},{192,160},{224,1... | collective-permute-start | bytes 1769480 | tf_op jit(solution)/shard_map/ppermute | solution.py:270
  63.9 4.2 %collective-permute-start.14 = (bf16[384,768]{1,0:T(8,128)(2,1)S(1)}, bf16[384,768]{1,0:T(8,128)(2,1)S(1)}, u32[]{:S(2)}, u32[]{:S(2)}) collective-permute-start(bf16[384,768]{1,0:T(8,128)(2,1)S(1)} %collective-permute-done.8.refs_2_), channel_id=1, source_target_pairs={{0,8},{8,0},{1,9},{9,1},{2,10},{10,2},{3,11},{11,3},{4,12},{12,4},... | collective-permute-start | bytes 1769480 | tf_op jit(solution)/shard_map/ppermute | solution.py:259
  65.0 3.1 %collective-permute-start.15 = (bf16[384,768]{1,0:T(8,128)(2,1)S(1)}, bf16[384,768]{1,0:T(8,128)(2,1)S(1)}, u32[]{:S(2)}, u32[]{:S(2)}) collective-permute-start(bf16[384,768]{1,0:T(8,128)(2,1)S(1)} %collective-permute-done.9.refs_3_), channel_id=1, source_target_pairs={{0,8},{8,0},{1,9},{9,1},{2,10},{10,2},{3,11},{11,3},{4,12},{12,4},... | collective-permute-start | bytes 1769480 | tf_op jit(solution)/shard_map/ppermute | solution.py:259
  65.1 9.9 %collective-permute-start.12 = (bf16[192,768]{1,0:T(8,128)(2,1)S(1)}, bf16[192,768]{1,0:T(8,128)(2,1)S(1)}, u32[]{:S(2)}, u32[]{:S(2)}) collective-permute-start(bf16[192,768]{1,0:T(8,128)(2,1)S(1)} %slice.9), channel_id=1, source_target_pairs={{0,32},{32,64},{64,96},{96,128},{128,160},{160,192},{192,224},{224... | collective-permute-start | bytes 884744 | tf_op jit(solution)/shard_map/ppermute | solution.py:270
  65.9 9.0 %collective-permute-start.13 = (bf16[192,768]{1,0:T(8,128)(2,1)S(1)}, bf16[192,768]{1,0:T(8,128)(2,1)S(1)}, u32[]{:S(2)}, u32[]{:S(2)}) collective-permute-start(bf16[192,768]{1,0:T(8,128)(2,1)S(1)} %slice.10), channel_id=1, source_target_pairs={{0,224},{32,0},{64,32},{96,64},{128,96},{160,128},{192,160},{224,1... | collective-permute-start | bytes 884744 | tf_op jit(solution)/shard_map/ppermute | solution.py:270
  75.0 2.3 %collective-permute-start.16 = (bf16[192,768]{1,0:T(8,128)(2,1)S(1)}, bf16[192,768]{1,0:T(8,128)(2,1)S(1)}, u32[]{:S(2)}, u32[]{:S(2)}) collective-permute-start(bf16[192,768]{1,0:T(8,128)(2,1)S(1)} %collective-permute-done.12.refs_2_), channel_id=1, source_target_pairs={{0,8},{8,0},{1,9},{9,1},{2,10},{10,2},{3,11},{11,3},{4,12},{12,4},... | collective-permute-start | bytes 884744 | tf_op jit(solution)/shard_map/ppermute | solution.py:259
  76.1 1.6 %collective-permute-start.17 = (bf16[192,768]{1,0:T(8,128)(2,1)S(1)}, bf16[192,768]{1,0:T(8,128)(2,1)S(1)}, u32[]{:S(2)}, u32[]{:S(2)}) collective-permute-start(bf16[192,768]{1,0:T(8,128)(2,1)S(1)} %collective-permute-done.13.refs_3_), channel_id=1, source_target_pairs={{0,8},{8,0},{1,9},{9,1},{2,10},{10,2},{3,11},{11,3},{4,12},{12,4},... | collective-permute-start | bytes 884744 | tf_op jit(solution)/shard_map/ppermute | solution.py:259
  83.4 20.5 %all-to-all-start.2 = ((bf16[16,64,384]{2,1,0:T(8,128)(2,1)}), bf16[16,64,384]{2,1,0:T(8,128)(2,1)S(1)}, u32[]{:S(2)}, u32[]{:S(2)}) async-start(bf16[16,64,384]{2,1,0:T(8,128)(2,1)} %attend4.1), calls=%async_computation.2 | async-start | bytes 1572864 | tf_op jit(solution)/shard_map/all_to_all | solution.py:299
  (8 other events, 26.4 us)

commit v3 on v2

--- a/solution.py
+++ b/solution.py
@@ -15,7 +15,7 @@
 F32 = jnp.float32
 LIMIT = 32 * 2**20
 SMALL = 16 * 2**20
-ROWS = 64
+TOK, EXTRA = 48, 8
 
 
 def norm(src, gain):
@@ -24,14 +24,15 @@
     return (values * lax.rsqrt(mean + EPSILON) * gain[...]).astype(BF)
 
 
-def prep_q_kernel(groups, q_ref, gain_ref, out_ref):
+def prep_q_kernel(copies, groups, q_ref, gain_ref, out_ref):
     per = q_ref.shape[1] // groups
     q = norm(q_ref, gain_ref)
     for g in range(groups):
-        out_ref[g] = q[:, g * per : (g + 1) * per]
-
-
-def prep_kv_kernel(groups, k_ref, v_ref, gain_ref, out_ref):
+        for c in range(copies):
+            out_ref[c * groups + g] = q[:, g * per : (g + 1) * per]
+
+
+def prep_kv_kernel(copies, groups, k_ref, v_ref, gain_ref, out_ref):
     per = k_ref.shape[1] // groups
     k = norm(k_ref, gain_ref)
     for g in range(groups):
@@ -40,12 +41,12 @@
         out_ref[g, :, per:] = v_ref[:, cols]
 
 
-def prep(kernel, name, groups, gain, *sources):
+def prep(kernel, name, copies, groups, gain, *sources):
     rows, width = sources[0].shape
     vmem = pl.BlockSpec(memory_space=pltpu.VMEM)
     return pl.pallas_call(
-        functools.partial(kernel, groups),
-        out_shape=jax.ShapeDtypeStruct((groups, rows, len(sources) * width // groups), BF),
+        functools.partial(kernel, copies, groups),
+        out_shape=jax.ShapeDtypeStruct((copies * groups, rows, len(sources) * width // groups), BF),
         in_specs=[vmem] * (len(sources) + 1),
         out_specs=vmem,
         compiler_params=pltpu.CompilerParams(vmem_limit_bytes=SMALL),
@@ -56,11 +57,12 @@
 def attn_kernel(keys, spans, first, last, *refs):
     refs = list(refs)
     patches = len(spans)
-    q_refs = [refs.pop(0) for _ in spans]
+    q_ref = refs.pop(0)
     blocks = [refs.pop(0) for _ in keys]
     states = [None if new else (refs.pop(0), refs.pop(0)) for new in first]
+    yl_ref = refs.pop(0)
+    place = [yl_ref[0], 1 - yl_ref[0]]
     if last:
-        base_ref = refs.pop(0)
         out_ref = refs.pop(0)
     else:
         results = [(refs.pop(0), refs.pop(0)) for _ in spans]
@@ -80,8 +82,9 @@
     for n, block in zip(keys, blocks):
         early.append(start(block.at[:, pl.ds(0, width)], k_buf.at[pl.ds(off, n)], sems.at[0]))
         off += n
-    for i, ref in enumerate(q_refs):
-        early.append(start(ref, q_buf.at[pl.ds(i * bq, bq)], sems.at[1]))
+    for i in range(patches):
+        src = q_ref.at[pl.ds(pl.multiple_of(place[i] * bq, bq), bq)]
+        early.append(start(src, q_buf.at[pl.ds(i * bq, bq)], sems.at[1]))
     off = 0
     for n, block in zip(keys, blocks):
         for h in range(heads):
@@ -107,10 +110,10 @@
         q = q_buf[i * bq : (i + 1) * bq, cols]
         return lax.dot_general(q, k_buf[window(i), cols], (((1,), (1,)), ((), ())), preferred_element_type=F32)
 
-    tok = ROWS - 16
+    tok = TOK
     lane = lax.broadcasted_iota(jnp.int32, (bq, HD), 1)
     eye = lax.broadcasted_iota(jnp.int32, (tok, HD), 0) == lax.broadcasted_iota(jnp.int32, (tok, HD), 1)
-    which = lax.broadcasted_iota(jnp.int32, (16, HD), 0)
+    which = lax.broadcasted_iota(jnp.int32, (EXTRA, HD), 0)
     done = [None] * patches
 
     def rest(work, s):
@@ -136,14 +139,13 @@
                 lse_buf[rows] = done[i]
             return
         for t in range(bq // tok):
-            d = base_ref[i] + t
-            out_ref[d, :tok, cols] = o[t * tok : (t + 1) * tok]
+            d = place[i] * (bq // tok) + t
             row = jnp.sum(jnp.where(eye, lse[t * tok : (t + 1) * tok], 0.0), axis=0, keepdims=True)
             hi = row.astype(BF).astype(F32)
             mid = (row - hi).astype(BF).astype(F32)
             low = row - hi - mid
             packed = jnp.where(which == 0, hi, jnp.where(which == 1, mid, jnp.where(which == 2, low, 0.0)))
-            out_ref[d, tok:, cols] = packed.astype(BF)
+            out_ref[d, :, cols] = jnp.concatenate([o[t * tok : (t + 1) * tok], packed.astype(BF)], axis=0)
 
     pending = None
     for work in [(h, i) for h in range(heads) for i in range(patches)]:
@@ -165,29 +167,28 @@
             copy.wait()
 
 
-def attend(qs, blocks, states=None, spans=None, base=None, name="attend"):
-    bq, width = qs[0].shape
-    patches = len(qs)
-    nq = patches * bq
+def attend(q, yl, blocks, states=None, spans=None, last=False, name="attend"):
+    nq, width = q.shape
+    patches = YL
+    bq = nq // patches
     heads = width // HD
     keys = tuple(b.shape[0] for b in blocks)
     states = states or [None] * patches
     spans = spans or [(0, len(keys))] * patches
-    first, last = [s is None for s in states], base is not None
+    first = [s is None for s in states]
     total = sum(keys)
     hbm = pl.BlockSpec(memory_space=pl.ANY)
-    args = [*qs, *blocks]
+    args = [q, *blocks]
     alias = {}
     for i, state in enumerate(states):
         if state is not None:
             if not last:
                 alias |= {len(args): 2 * i, len(args) + 1: 2 * i + 1}
             args += list(state)
-    specs = [hbm] * len(args)
+    args.append(yl)
+    specs = [hbm] * (len(args) - 1) + [pl.BlockSpec(memory_space=pltpu.SMEM)]
     if last:
-        args.append(base)
-        specs.append(pl.BlockSpec(memory_space=pltpu.SMEM))
-        out_shape = jax.ShapeDtypeStruct((nq // (ROWS - 16), ROWS, width), BF)
+        out_shape = jax.ShapeDtypeStruct((nq // TOK, TOK + EXTRA, width), BF)
         out_specs = pl.BlockSpec(memory_space=pltpu.VMEM)
     else:
         out_shape = [jax.ShapeDtypeStruct((bq, width), BF), jax.ShapeDtypeStruct((bq, HD), F32)] * patches
@@ -216,23 +217,21 @@
 
 
 def merge_kernel(groups, copies, in_ref, out_ref):
-    tok = ROWS - 16
+    tok = TOK
     heads = in_ref.shape[2] // HD
     eye = lax.broadcasted_iota(jnp.int32, (tok, HD), 0) == lax.broadcasted_iota(jnp.int32, (tok, HD), 1)
     for g in range(groups):
         for h in range(heads):
             cols = slice(h * HD, (h + 1) * HD)
+            parts = [in_ref[c * groups + g, :, cols].astype(F32) for c in range(copies)]
             lses = []
-            for c in range(copies):
-                packed = in_ref[c * groups + g, tok:, cols].astype(F32)
-                row = jnp.sum(packed, axis=0, keepdims=True)
+            for part in parts:
+                row = jnp.sum(part[tok:], axis=0, keepdims=True)
                 lses.append(jnp.sum(jnp.where(eye, jnp.broadcast_to(row, (tok, HD)), 0.0), axis=1, keepdims=True))
             top = functools.reduce(jnp.maximum, lses)
             weights = [jnp.exp2(x - top) for x in lses]
             total = sum(weights)
-            acc = 0.0
-            for c in range(copies):
-                acc = acc + in_ref[c * groups + g, :tok, cols].astype(F32) * (weights[c] / total)
+            acc = sum(part[:tok] * (weight / total) for part, weight in zip(parts, weights))
             first = (g * heads + h) * HD
             out_ref[:, first : first + HD] = acc.astype(BF)
 
@@ -241,7 +240,7 @@
     width = parts.shape[2] * groups
     return pl.pallas_call(
         functools.partial(merge_kernel, groups, copies),
-        out_shape=jax.ShapeDtypeStruct((ROWS - 16, width), BF),
+        out_shape=jax.ShapeDtypeStruct((TOK, width), BF),
         in_specs=[pl.BlockSpec(memory_space=pltpu.VMEM)],
         out_specs=pl.BlockSpec(memory_space=pltpu.VMEM),
         compiler_params=pltpu.CompilerParams(vmem_limit_bytes=SMALL),
@@ -263,8 +262,7 @@
     groups = X * YH
     width_dev = stale_k.shape[1]
     half = stale_k.shape[0] // 2
-    yl = lax.axis_index("yl").astype(jnp.int32)
-    base = jnp.stack([yl * groups, (1 - yl) * groups])
+    yl = lax.axis_index("yl").astype(jnp.int32).reshape(1)
 
     def both(pair):
         return lax.ppermute(pair[0], "z", UP), lax.ppermute(pair[1], "z", DOWN)
@@ -274,28 +272,26 @@
 
     own = jnp.concatenate([stale_k, stale_v], axis=1)
     r1 = both((own, own))
-    q_parts = prep(prep_q_kernel, "prep_q", groups, q_gain, fresh_q)
-    q = lax.all_to_all(q_parts, ("x", "yh"), split_axis=0, concat_axis=0, tiled=True)
-    kv_parts = prep(prep_kv_kernel, "prep_kv", groups, k_gain, fresh_k, fresh_v)
+    q_parts = prep(prep_q_kernel, "prep_q", YL, groups, q_gain, fresh_q)
+    q = lax.all_to_all(q_parts, ("yl", "x", "yh"), split_axis=0, concat_axis=0, tiled=True)
+    kv_parts = prep(prep_kv_kernel, "prep_kv", 1, groups, k_gain, fresh_k, fresh_v)
     r1, q, kv_parts = lax.optimization_barrier((r1, q, kv_parts))
     q = q.reshape(-1, width_dev)
-    qs = [q, lax.ppermute(q, "yl", SWAP)]
     r2 = both(r1)
     fresh = lax.all_to_all(kv_parts, ("x", "yh"), split_axis=0, concat_axis=0, tiled=True)
     own_other = other_core(own)
-    r1 = [*r1, *swap(r1)]
-    early = attend(qs[:1], [own_other, *r1], name="attend1")
-    r2, qs[1], fresh, early = lax.optimization_barrier((r2, qs[1], fresh, early))
+    state = attend(q, yl, [*r1, *swap(r1)], name="attend1")
+    r2, state, fresh = lax.optimization_barrier((r2, state, fresh))
     fresh = fresh.reshape(-1, 2 * width_dev)
 
     r3 = both(r2)
-    blocks = [own, own_other, *r1, *r2, *swap(r2), fresh]
-    state = attend(qs, blocks, [early[0], None], [(6, 11), (0, 10)], name="attend2")
+    blocks = [own, own_other, *r2, *swap(r2), fresh]
+    state = attend(q, yl, blocks, state, [(1, 7), (0, 6)], name="attend2")
     r3, state = lax.optimization_barrier((r3, state))
     r4 = both((r3[0][:half], r3[1][half:]))
-    state = attend(qs, [*r3, *swap(r3)], state, name="attend3")
+    state = attend(q, yl, [*r3, *swap(r3)], state, name="attend3")
     r4, state = lax.optimization_barrier((r4, state))
-    parts = attend(qs, [*r4, *swap(r4)], state, base=base, name="attend4")
+    parts = attend(q, yl, [*r4, *swap(r4)], state, last=True, name="attend4")
     back = lax.all_to_all(parts, ("yl", "x", "yh"), split_axis=0, concat_axis=0, tiled=True)
     return merge(back, groups, YL), fresh[:, :width_dev]
 

time: 107 us -> 103 us (0.963)
  starting transfers between devices: 40.2 us -> 37.9 us
  local copies, waits for them, and re-layouts: 5.91 us -> 3.77 us
  waiting for transfers between devices: 26.3 us -> 27.9 us
    ppermute x1 -> x0, waiting for transfers between devices: 6.89 us -> none  [body(): qs = [q, lax.ppermute(q, 'yl', SWAP)]]
    all_to_all x1, waiting for transfers between devices: 5.19 us -> 9.42 us  [body(): lax.all_to_all(q_parts, ('yl', 'x', 'yh'), split_axis=0, concat_axis=0, t...]
    ppermute x8, waiting for transfers between devices: 0.02 us -> 3.84 us  [both(): return (lax.ppermute(pair[0], 'z', UP), lax.ppermute(pair[1], 'z', DOWN))]
    all_to_all x1, starting transfers between devices: 6.98 us -> 4.74 us  [body(): lax.all_to_all(parts, ('yl', 'x', 'yh'), split_axis=0, concat_axis=0, til...]
    unnamed x23 -> x17, local copies, waits for them, and re-layouts: 5.07 us -> 2.94 us
    all_to_all x1, waiting for transfers between devices: 0.01 us -> 1.41 us  [body(): lax.all_to_all(kv_parts, ('x', 'yh'), split_axis=0, concat_axis=0, tiled=...]
  transfers between devices with their start and end apart: 21 -> 20, of which waited for: 5 -> 6; matrix products, arithmetic and copies ran while one was open for 1% -> 1% of each run, Pallas kernels for 24% -> 24%
where the time goes in v3:
time: 103 us; the launch traced here: 101 us
  starting transfers between devices  37.9 us (37%)
  Pallas kernels  31 us (30%)
  waiting for transfers between devices  27.9 us (27%)
  local copies, waits for them, and re-layouts  3.77 us (4%)
    pallas_call x4, Pallas kernels, attend(): pl.pallas_call(functools.partial(attn_kernel, keys, spans, first, last),...  27.9 us
    ppermute x8, starting transfers between devices, both(): return (lax.ppermute(pair[0], 'z', UP), lax.ppermute(pair[1], 'z', DOWN))  15.2 us
    all_to_all x1, waiting for transfers between devices, body(): lax.all_to_all(parts, ('yl', 'x', 'yh'), split_axis=0, concat_axis=0, til...  11.7 us
    all_to_all x1, waiting for transfers between devices, body(): lax.all_to_all(q_parts, ('yl', 'x', 'yh'), split_axis=0, concat_axis=0, t...  9.42 us
    ppermute x9, starting transfers between devices, other_core(): return lax.ppermute(x, 'core', SWAP)  7.53 us
    all_to_all x1, starting transfers between devices, body(): lax.all_to_all(q_parts, ('yl', 'x', 'yh'), split_axis=0, concat_axis=0, t...  6.89 us
    all_to_all x1, starting transfers between devices, body(): lax.all_to_all(parts, ('yl', 'x', 'yh'), split_axis=0, concat_axis=0, til...  4.74 us
    ppermute x8, waiting for transfers between devices, both(): return (lax.ppermute(pair[0], 'z', UP), lax.ppermute(pair[1], 'z', DOWN))  3.84 us
  transfers between devices with their start and end apart: 20, of which 6 were waited for; matrix products, arithmetic and copies ran while one was open for 1% of the time, Pallas kernels for 24%

profile of v3, /device:TPU:1, one launch (start us, length us, event | category | flops | bytes accessed | tf_op | source)
XLA Modules:
  0.0 101.4 jit_solution(1390614249689117345)
XLA Ops:
  0.6 1.0 %constant_dynamic-update-slice_fusion.1 = bf16[384,768]{1,0:T(8,128)(2,1)S(1)} fusion(bf16[384,384]{1,0:T(8,128)(2,1)} %param.10), kind=kLoop, calls=%fused_computation.1 | loop fusion | bytes 589824
  1.8 2.5 %collective-permute-start = (bf16[384,768]{1,0:T(8,128)(2,1)S(1)}, bf16[384,768]{1,0:T(8,128)(2,1)}, u32[]{:S(2)}, u32[]{:S(2)}) collective-permute-start(bf16[384,768]{1,0:T(8,128)(2,1)S(1)} %constant_dynamic-update-slice_fusion.refs_1_), channel_id=1, source_target_pairs={{0,32},{32,64},{64,96},{96,128},{128,160},{160,192},{192,224},{224... | collective-permute-start | bytes 1769480 | tf_op jit(solution)/shard_map/ppermute | solution.py:268
  4.3 4.0 %collective-permute-start.1 = (bf16[384,768]{1,0:T(8,128)(2,1)S(1)}, bf16[384,768]{1,0:T(8,128)(2,1)}, u32[]{:S(2)}, u32[]{:S(2)}) collective-permute-start(bf16[384,768]{1,0:T(8,128)(2,1)S(1)} %constant_dynamic-update-slice_fusion.refs_1_), channel_id=1, source_target_pairs={{0,224},{32,0},{64,32},{96,64},{128,96},{160,128},{192,160},{224,1... | collective-permute-start | bytes 1769480 | tf_op jit(solution)/shard_map/ppermute | solution.py:268
  9.4 6.9 %all-to-all-start = ((bf16[16,48,384]{2,1,0:T(8,128)(2,1)}), bf16[16,48,384]{2,1,0:T(8,128)(2,1)S(1)}, u32[]{:S(2)}, u32[]{:S(2)}) async-start(bf16[16,48,384]{2,1,0:T(8,128)(2,1)} %prep_q.1), calls=%async_computation | async-start | bytes 1179648 | tf_op jit(solution)/shard_map/all_to_all | solution.py:276
  17.3 9.4 %all-to-all-done = bf16[16,48,384]{2,1,0:T(8,128)(2,1)S(1)} async-done(((bf16[16,48,384]{2,1,0:T(8,128)(2,1)}), bf16[16,48,384]{2,1,0:T(8,128)(2,1)S(1)}, u32[]{:S(2)}, u32[]{:S(2)}) %all-to-all-start) | async-done | bytes 589856 | tf_op jit(solution)/shard_map/all_to_all | solution.py:276
  26.7 2.7 %collective-permute-start.4 = (bf16[384,768]{1,0:T(8,128)(2,1)}, bf16[384,768]{1,0:T(8,128)(2,1)S(1)}, u32[]{:S(2)}, u32[]{:S(2)}) collective-permute-start(bf16[384,768]{1,0:T(8,128)(2,1)} %collective-permute-done.refs_1_), channel_id=1, source_target_pairs={{0,8},{8,0},{1,9},{9,1},{2,10},{10,2},{3,11},{11,3},{4,12},{12,4},... | collective-permute-start | bytes 1769480 | tf_op jit(solution)/shard_map/ppermute | solution.py:258
  29.5 2.7 %collective-permute-start.3 = (bf16[384,768]{1,0:T(8,128)(2,1)}, bf16[384,768]{1,0:T(8,128)(2,1)}, u32[]{:S(2)}, u32[]{:S(2)}) collective-permute-start(bf16[384,768]{1,0:T(8,128)(2,1)} %collective-permute-done.1.refs_2_), channel_id=1, source_target_pairs={{0,224},{32,0},{64,32},{96,64},{128,96},{160,128},{192,160},{224,1... | collective-permute-start | bytes 1769480 | tf_op jit(solution)/shard_map/ppermute | solution.py:268
  32.2 3.5 %all-to-all-start.1 = ((bf16[8,48,768]{2,1,0:T(8,128)(2,1)}), bf16[8,48,768]{2,1,0:T(8,128)(2,1)S(1)}, u32[]{:S(2)}, u32[]{:S(2)}) async-start(bf16[8,48,768]{2,1,0:T(8,128)(2,1)} %prep_kv.1), calls=%async_computation.1 | async-start | bytes 1179648 | tf_op jit(solution)/shard_map/all_to_all | solution.py:281
  35.7 1.1 %collective-permute-start.8 = (bf16[384,768]{1,0:T(8,128)(2,1)S(1)}, bf16[384,768]{1,0:T(8,128)(2,1)}, u32[]{:S(2)}, u32[]{:S(2)}) collective-permute-start(bf16[384,768]{1,0:T(8,128)(2,1)S(1)} %constant_dynamic-update-slice_fusion.refs_1_), channel_id=1, source_target_pairs={{0,8},{8,0},{1,9},{9,1},{2,10},{10,2},{3,11},{11,3},{4,12},{12,4},... | collective-permute-start | bytes 1769480 | tf_op jit(solution)/shard_map/ppermute | solution.py:258
  37.6 1.1 %copy-done.6 = bf16[384,768]{1,0:T(8,128)(2,1)S(1)} copy-done((bf16[384,768]{1,0:T(8,128)(2,1)S(1)}, bf16[384,768]{1,0:T(8,128)(2,1)}, u32[]{:S(2)}) %copy-start.6) | copy-done | bytes 589848
  38.6 6.6 %attend1.1 = (bf16[384,384]{1,0:T(8,128)(2,1)S(1)}, f32[384,128]{1,0:T(8,128)S(1)}, bf16[384,384]{1,0:T(8,128)(2,1)S(1)}, f32[384,128]{1,0:T(8,128)S(1)}) custom-call(bf16[768,384]{1,0:T(8,128)(2,1)S(1)} %bitcast.5, bf16[384,768]{1,0:T(8,128)(2,1)} %collective-permute-done.refs_1_, bf16[384,768]{1,0:T(8,128)(2,1)} %collective-permute-done.1.refs_2_, ...), custom_call_target="tpu_custom_call" | custom-call | flops 1811939328 | bytes 1048576 | tf_op jit(solution)/shard_map/attend1/pallas_call | solution.py:197
  45.3 1.4 %all-to-all-done.1 = bf16[8,48,768]{2,1,0:T(8,128)(2,1)S(1)} async-done(((bf16[8,48,768]{2,1,0:T(8,128)(2,1)}), bf16[8,48,768]{2,1,0:T(8,128)(2,1)S(1)}, u32[]{:S(2)}, u32[]{:S(2)}) %all-to-all-start.1) | async-done | bytes 589856 | tf_op jit(solution)/shard_map/all_to_all | solution.py:281
  46.7 1.4 %collective-permute-start.10 = (bf16[384,768]{1,0:T(8,128)(2,1)}, bf16[384,768]{1,0:T(8,128)(2,1)S(1)}, u32[]{:S(2)}, u32[]{:S(2)}) collective-permute-start(bf16[384,768]{1,0:T(8,128)(2,1)} %collective-permute-done.3.refs_4_), channel_id=1, source_target_pairs={{0,8},{8,0},{1,9},{9,1},{2,10},{10,2},{3,11},{11,3},{4,12},{12,4},... | collective-permute-start | bytes 1769480 | tf_op jit(solution)/shard_map/ppermute | solution.py:258
  48.2 2.7 %collective-permute-start.7 = (bf16[384,768]{1,0:T(8,128)(2,1)}, bf16[384,768]{1,0:T(8,128)(2,1)S(1)}, u32[]{:S(2)}, u32[]{:S(2)}) collective-permute-start(bf16[384,768]{1,0:T(8,128)(2,1)} %collective-permute-done.3.refs_4_), channel_id=1, source_target_pairs={{0,224},{32,0},{64,32},{96,64},{128,96},{160,128},{192,160},{224,1... | collective-permute-start | bytes 1769480 | tf_op jit(solution)/shard_map/ppermute | solution.py:268
  50.9 9.2 %attend2.1 = (bf16[384,384]{1,0:T(8,128)(2,1)S(1)}, f32[384,128]{1,0:T(8,128)S(1)}, bf16[384,384]{1,0:T(8,128)(2,1)S(1)}, f32[384,128]{1,0:T(8,128)S(1)}) custom-call(bf16[768,384]{1,0:T(8,128)(2,1)S(1)} %bitcast.6, ...), custom_call_target="tpu_custom_call", output_to_operand_aliasing={{0}: (8, {}), {1}: (9, {}), {2}: (10, {}), {3}: (11, {})} | custom-call | flops 2717908992 | bytes 1048576 | tf_op jit(solution)/shard_map/attend2/pallas_call | solution.py:197
  60.1 3.8 %collective-permute-done.6.refs_1_ = bf16[384,768]{1,0:T(8,128)(2,1)S(1)} collective-permute-done((bf16[384,768]{1,0:T(8,128)(2,1)S(1)}, bf16[384,768]{1,0:T(8,128)(2,1)S(1)}, u32[]{:S(2)}, u32[]{:S(2)}) %collective-permute-start.6) | collective-permute-done | bytes 589856 | tf_op jit(solution)/shard_map/ppermute | solution.py:268
  63.9 1.3 %collective-permute-start.13 = (bf16[384,768]{1,0:T(8,128)(2,1)S(1)}, bf16[384,768]{1,0:T(8,128)(2,1)S(1)}, u32[]{:S(2)}, u32[]{:S(2)}) collective-permute-start(bf16[384,768]{1,0:T(8,128)(2,1)S(1)} %collective-permute-done.6.refs_1_), channel_id=1, source_target_pairs={{0,8},{8,0},{1,9},{9,1},{2,10},{10,2},{3,11},{11,3},{4,12},{12,4},... | collective-permute-start | bytes 1769480 | tf_op jit(solution)/shard_map/ppermute | solution.py:258
  66.1 2.3 %collective-permute-start.12 = (bf16[192,768]{1,0:T(8,128)(2,1)S(1)}, bf16[192,768]{1,0:T(8,128)(2,1)S(1)}, u32[]{:S(2)}, u32[]{:S(2)}) collective-permute-start(bf16[192,768]{1,0:T(8,128)(2,1)S(1)} %slice.10), channel_id=1, source_target_pairs={{0,224},{32,0},{64,32},{96,64},{128,96},{160,128},{192,160},{224,1... | collective-permute-start | bytes 884744 | tf_op jit(solution)/shard_map/ppermute | solution.py:268
  68.5 6.9 %attend3.1 = (bf16[384,384]{1,0:T(8,128)(2,1)S(1)}, f32[384,128]{1,0:T(8,128)S(1)}, bf16[384,384]{1,0:T(8,128)(2,1)S(1)}, f32[384,128]{1,0:T(8,128)S(1)}) custom-call(bf16[768,384]{1,0:T(8,128)(2,1)S(1)} %bitcast.7, bf16[384,768]{1,0:T(8,128)(2,1)S(1)} %collective-permute-done.6.refs_1_, ...), custom_call_target="tpu_custom_call", output_to_operand_aliasing={{0}: (5, {}), {1}: (6, {}), {2}: (7, {}), {3}: (8, {})} | custom-call | flops 1811939328 | bytes 1048576 | tf_op jit(solution)/shard_map/attend3/pallas_call | solution.py:197
  76.4 1.1 %collective-permute-done.15.refs_3_ = bf16[192,768]{1,0:T(8,128)(2,1)S(1)} collective-permute-done((bf16[192,768]{1,0:T(8,128)(2,1)S(1)}, bf16[192,768]{1,0:T(8,128)(2,1)S(1)}, u32[]{:S(2)}, u32[]{:S(2)}) %collective-permute-start.15) | collective-permute-done | bytes 294944 | tf_op jit(solution)/shard_map/ppermute | solution.py:258
  77.9 5.2 %attend4.1 = bf16[16,56,384]{2,1,0:T(8,128)(2,1)} custom-call(bf16[768,384]{1,0:T(8,128)(2,1)S(1)} %bitcast.8, bf16[192,768]{1,0:T(8,128)(2,1)S(1)} %collective-permute-done.11.refs_1_, bf16[192,768]{1,0:T(8,128)(2,1)S(1)} %collective-permute-done.12.refs_2_, bf16[192,768]{1,0:T(8,128)(2,1)S(1)} %collective-permute-done.15.refs_3_, ...), custom_call_target="tpu_custom_call" | custom-call | flops 905969664 | bytes 1048576 | tf_op jit(solution)/shard_map/attend4/pallas_call | solution.py:197
  83.1 4.7 %all-to-all-start.2 = ((bf16[16,56,384]{2,1,0:T(8,128)(2,1)}), bf16[16,56,384]{2,1,0:T(8,128)(2,1)S(1)}, u32[]{:S(2)}, u32[]{:S(2)}) async-start(bf16[16,56,384]{2,1,0:T(8,128)(2,1)} %attend4.1), calls=%async_computation.2 | async-start | bytes 1376256 | tf_op jit(solution)/shard_map/all_to_all | solution.py:295
  88.6 11.7 %all-to-all-done.2.in_ref = bf16[16,56,384]{2,1,0:T(8,128)(2,1)S(1)} async-done(((bf16[16,56,384]{2,1,0:T(8,128)(2,1)}), bf16[16,56,384]{2,1,0:T(8,128)(2,1)S(1)}, u32[]{:S(2)}, u32[]{:S(2)}) %all-to-all-start.2) | async-done | bytes 688160 | tf_op jit(solution)/shard_map/all_to_all | solution.py:295
  100.2 1.2 %merge.1 = bf16[48,3072]{1,0:T(8,128)(2,1)} custom-call(bf16[16,56,384]{2,1,0:T(8,128)(2,1)S(1)} %all-to-all-done.2.in_ref), custom_call_target="tpu_custom_call" | custom-call | tf_op jit(solution)/shard_map/merge/pallas_call | solution.py:241
  (44 shorter events, 6.3 us)
Async XLA Ops:
  1.7 6.7 %copy-start = (bf16[48,3072]{1,0:T(8,128)(2,1)S(1)}, bf16[48,3072]{1,0:T(8,128)(2,1)}, u32[]{:S(2)}) copy-start(bf16[48,3072]{1,0:T(8,128)(2,1)} %q_ref.1) | copy-start | bytes 884740
  1.8 24.9 %collective-permute-start = (bf16[384,768]{1,0:T(8,128)(2,1)S(1)}, bf16[384,768]{1,0:T(8,128)(2,1)}, u32[]{:S(2)}, u32[]{:S(2)}) collective-permute-start(bf16[384,768]{1,0:T(8,128)(2,1)S(1)} %constant_dynamic-update-slice_fusion.refs_1_), channel_id=1, source_target_pairs={{0,32},{32,64},{64,96},{96,128},{128,160},{160,192},{192,224},{224... | collective-permute-start | bytes 1769480 | tf_op jit(solution)/shard_map/ppermute | solution.py:268
  4.3 22.4 %collective-permute-start.1 = (bf16[384,768]{1,0:T(8,128)(2,1)S(1)}, bf16[384,768]{1,0:T(8,128)(2,1)}, u32[]{:S(2)}, u32[]{:S(2)}) collective-permute-start(bf16[384,768]{1,0:T(8,128)(2,1)S(1)} %constant_dynamic-update-slice_fusion.refs_1_), channel_id=1, source_target_pairs={{0,224},{32,0},{64,32},{96,64},{128,96},{160,128},{192,160},{224,1... | collective-permute-start | bytes 1769480 | tf_op jit(solution)/shard_map/ppermute | solution.py:268
  9.4 6.9 %copy-start.1 = (bf16[48,3072]{1,0:T(8,128)(2,1)S(1)}, bf16[48,3072]{1,0:T(8,128)(2,1)}, u32[]{:S(2)}) copy-start(bf16[48,3072]{1,0:T(8,128)(2,1)} %k_ref.1) | copy-start | bytes 884740
  9.4 6.9 %copy-start.2 = (bf16[48,3072]{1,0:T(8,128)(2,1)S(1)}, bf16[48,3072]{1,0:T(8,128)(2,1)}, u32[]{:S(2)}) copy-start(bf16[48,3072]{1,0:T(8,128)(2,1)} %v_ref.1) | copy-start | bytes 884740
  9.4 6.9 %copy-start.4 = (f32[3072]{0:T(1024)S(1)}, f32[3072]{0:T(1024)}, u32[]{:S(2)}) copy-start(f32[3072]{0:T(1024)} %param.13) | copy-start | bytes 36868
  9.4 17.4 %all-to-all-start = ((bf16[16,48,384]{2,1,0:T(8,128)(2,1)}), bf16[16,48,384]{2,1,0:T(8,128)(2,1)S(1)}, u32[]{:S(2)}, u32[]{:S(2)}) async-start(bf16[16,48,384]{2,1,0:T(8,128)(2,1)} %prep_q.1), calls=%async_computation | async-start | bytes 1179648 | tf_op jit(solution)/shard_map/all_to_all | solution.py:276
  26.7 10.0 %collective-permute-start.4 = (bf16[384,768]{1,0:T(8,128)(2,1)}, bf16[384,768]{1,0:T(8,128)(2,1)S(1)}, u32[]{:S(2)}, u32[]{:S(2)}) collective-permute-start(bf16[384,768]{1,0:T(8,128)(2,1)} %collective-permute-done.refs_1_), channel_id=1, source_target_pairs={{0,8},{8,0},{1,9},{9,1},{2,10},{10,2},{3,11},{11,3},{4,12},{12,4},... | collective-permute-start | bytes 1769480 | tf_op jit(solution)/shard_map/ppermute | solution.py:258
  29.4 8.2 %collective-permute-start.5 = (bf16[384,768]{1,0:T(8,128)(2,1)}, bf16[384,768]{1,0:T(8,128)(2,1)}, u32[]{:S(2)}, u32[]{:S(2)}) collective-permute-start(bf16[384,768]{1,0:T(8,128)(2,1)} %collective-permute-done.1.refs_2_), channel_id=1, source_target_pairs={{0,8},{8,0},{1,9},{9,1},{2,10},{10,2},{3,11},{11,3},{4,12},{12,4},... | collective-permute-start | bytes 1769480 | tf_op jit(solution)/shard_map/ppermute | solution.py:258
  29.5 17.2 %collective-permute-start.2 = (bf16[384,768]{1,0:T(8,128)(2,1)}, bf16[384,768]{1,0:T(8,128)(2,1)S(1)}, u32[]{:S(2)}, u32[]{:S(2)}) collective-permute-start(bf16[384,768]{1,0:T(8,128)(2,1)} %collective-permute-done.refs_1_), channel_id=1, source_target_pairs={{0,32},{32,64},{64,96},{96,128},{128,160},{160,192},{192,224},{224... | collective-permute-start | bytes 1769480 | tf_op jit(solution)/shard_map/ppermute | solution.py:268
  29.5 17.2 %collective-permute-start.3 = (bf16[384,768]{1,0:T(8,128)(2,1)}, bf16[384,768]{1,0:T(8,128)(2,1)}, u32[]{:S(2)}, u32[]{:S(2)}) collective-permute-start(bf16[384,768]{1,0:T(8,128)(2,1)} %collective-permute-done.1.refs_2_), channel_id=1, source_target_pairs={{0,224},{32,0},{64,32},{96,64},{128,96},{160,128},{192,160},{224,1... | collective-permute-start | bytes 1769480 | tf_op jit(solution)/shard_map/ppermute | solution.py:268
  32.2 14.5 %all-to-all-start.1 = ((bf16[8,48,768]{2,1,0:T(8,128)(2,1)}), bf16[8,48,768]{2,1,0:T(8,128)(2,1)S(1)}, u32[]{:S(2)}, u32[]{:S(2)}) async-start(bf16[8,48,768]{2,1,0:T(8,128)(2,1)} %prep_kv.1), calls=%async_computation.1 | async-start | bytes 1179648 | tf_op jit(solution)/shard_map/all_to_all | solution.py:281
  35.7 15.2 %collective-permute-start.8 = (bf16[384,768]{1,0:T(8,128)(2,1)S(1)}, bf16[384,768]{1,0:T(8,128)(2,1)}, u32[]{:S(2)}, u32[]{:S(2)}) collective-permute-start(bf16[384,768]{1,0:T(8,128)(2,1)S(1)} %constant_dynamic-update-slice_fusion.refs_1_), channel_id=1, source_target_pairs={{0,8},{8,0},{1,9},{9,1},{2,10},{10,2},{3,11},{11,3},{4,12},{12,4},... | collective-permute-start | bytes 1769480 | tf_op jit(solution)/shard_map/ppermute | solution.py:258
  46.7 4.2 %collective-permute-start.10 = (bf16[384,768]{1,0:T(8,128)(2,1)}, bf16[384,768]{1,0:T(8,128)(2,1)S(1)}, u32[]{:S(2)}, u32[]{:S(2)}) collective-permute-start(bf16[384,768]{1,0:T(8,128)(2,1)} %collective-permute-done.3.refs_4_), channel_id=1, source_target_pairs={{0,8},{8,0},{1,9},{9,1},{2,10},{10,2},{3,11},{11,3},{4,12},{12,4},... | collective-permute-start | bytes 1769480 | tf_op jit(solution)/shard_map/ppermute | solution.py:258
  48.1 2.8 %collective-permute-start.9 = (bf16[384,768]{1,0:T(8,128)(2,1)S(1)}, bf16[384,768]{1,0:T(8,128)(2,1)S(1)}, u32[]{:S(2)}, u32[]{:S(2)}) collective-permute-start(bf16[384,768]{1,0:T(8,128)(2,1)S(1)} %collective-permute-done.2.refs_3_), channel_id=1, source_target_pairs={{0,8},{8,0},{1,9},{9,1},{2,10},{10,2},{3,11},{11,3},{4,12},{12,4},... | collective-permute-start | bytes 1769480 | tf_op jit(solution)/shard_map/ppermute | solution.py:258
  48.2 15.7 %collective-permute-start.6 = (bf16[384,768]{1,0:T(8,128)(2,1)S(1)}, bf16[384,768]{1,0:T(8,128)(2,1)S(1)}, u32[]{:S(2)}, u32[]{:S(2)}) collective-permute-start(bf16[384,768]{1,0:T(8,128)(2,1)S(1)} %collective-permute-done.2.refs_3_), channel_id=1, source_target_pairs={{0,32},{32,64},{64,96},{96,128},{128,160},{160,192},{192,224},{224... | collective-permute-start | bytes 1769480 | tf_op jit(solution)/shard_map/ppermute | solution.py:268
  48.2 15.7 %collective-permute-start.7 = (bf16[384,768]{1,0:T(8,128)(2,1)}, bf16[384,768]{1,0:T(8,128)(2,1)S(1)}, u32[]{:S(2)}, u32[]{:S(2)}) collective-permute-start(bf16[384,768]{1,0:T(8,128)(2,1)} %collective-permute-done.3.refs_4_), channel_id=1, source_target_pairs={{0,224},{32,0},{64,32},{96,64},{128,96},{160,128},{192,160},{224,1... | collective-permute-start | bytes 1769480 | tf_op jit(solution)/shard_map/ppermute | solution.py:268
  63.9 4.6 %collective-permute-start.13 = (bf16[384,768]{1,0:T(8,128)(2,1)S(1)}, bf16[384,768]{1,0:T(8,128)(2,1)S(1)}, u32[]{:S(2)}, u32[]{:S(2)}) collective-permute-start(bf16[384,768]{1,0:T(8,128)(2,1)S(1)} %collective-permute-done.6.refs_1_), channel_id=1, source_target_pairs={{0,8},{8,0},{1,9},{9,1},{2,10},{10,2},{3,11},{11,3},{4,12},{12,4},... | collective-permute-start | bytes 1769480 | tf_op jit(solution)/shard_map/ppermute | solution.py:258
  65.1 3.3 %collective-permute-start.14 = (bf16[384,768]{1,0:T(8,128)(2,1)S(1)}, bf16[384,768]{1,0:T(8,128)(2,1)S(1)}, u32[]{:S(2)}, u32[]{:S(2)}) collective-permute-start(bf16[384,768]{1,0:T(8,128)(2,1)S(1)} %collective-permute-done.7.refs_2_), channel_id=1, source_target_pairs={{0,8},{8,0},{1,9},{9,1},{2,10},{10,2},{3,11},{11,3},{4,12},{12,4},... | collective-permute-start | bytes 1769480 | tf_op jit(solution)/shard_map/ppermute | solution.py:258
  65.2 10.2 %collective-permute-start.11 = (bf16[192,768]{1,0:T(8,128)(2,1)S(1)}, bf16[192,768]{1,0:T(8,128)(2,1)S(1)}, u32[]{:S(2)}, u32[]{:S(2)}) collective-permute-start(bf16[192,768]{1,0:T(8,128)(2,1)S(1)} %slice.9), channel_id=1, source_target_pairs={{0,32},{32,64},{64,96},{96,128},{128,160},{160,192},{192,224},{224... | collective-permute-start | bytes 884744 | tf_op jit(solution)/shard_map/ppermute | solution.py:268
  66.1 9.2 %collective-permute-start.12 = (bf16[192,768]{1,0:T(8,128)(2,1)S(1)}, bf16[192,768]{1,0:T(8,128)(2,1)S(1)}, u32[]{:S(2)}, u32[]{:S(2)}) collective-permute-start(bf16[192,768]{1,0:T(8,128)(2,1)S(1)} %slice.10), channel_id=1, source_target_pairs={{0,224},{32,0},{64,32},{96,64},{128,96},{160,128},{192,160},{224,1... | collective-permute-start | bytes 884744 | tf_op jit(solution)/shard_map/ppermute | solution.py:268
  75.4 2.1 %collective-permute-start.15 = (bf16[192,768]{1,0:T(8,128)(2,1)S(1)}, bf16[192,768]{1,0:T(8,128)(2,1)S(1)}, u32[]{:S(2)}, u32[]{:S(2)}) collective-permute-start(bf16[192,768]{1,0:T(8,128)(2,1)S(1)} %collective-permute-done.11.refs_1_), channel_id=1, source_target_pairs={{0,8},{8,0},{1,9},{9,1},{2,10},{10,2},{3,11},{11,3},{4,12},{12,4},... | collective-permute-start | bytes 884744 | tf_op jit(solution)/shard_map/ppermute | solution.py:258
  76.3 1.6 %collective-permute-start.16 = (bf16[192,768]{1,0:T(8,128)(2,1)S(1)}, bf16[192,768]{1,0:T(8,128)(2,1)S(1)}, u32[]{:S(2)}, u32[]{:S(2)}) collective-permute-start(bf16[192,768]{1,0:T(8,128)(2,1)S(1)} %collective-permute-done.12.refs_2_), channel_id=1, source_target_pairs={{0,8},{8,0},{1,9},{9,1},{2,10},{10,2},{3,11},{11,3},{4,12},{12,4},... | collective-permute-start | bytes 884744 | tf_op jit(solution)/shard_map/ppermute | solution.py:258
  83.1 17.2 %all-to-all-start.2 = ((bf16[16,56,384]{2,1,0:T(8,128)(2,1)}), bf16[16,56,384]{2,1,0:T(8,128)(2,1)S(1)}, u32[]{:S(2)}, u32[]{:S(2)}) async-start(bf16[16,56,384]{2,1,0:T(8,128)(2,1)} %attend4.1), calls=%async_computation.2 | async-start | bytes 1376256 | tf_op jit(solution)/shard_map/all_to_all | solution.py:295
  (4 other events, 9.6 us)

commit v4 on v3

--- a/solution.py
+++ b/solution.py
@@ -275,7 +275,8 @@
     q_parts = prep(prep_q_kernel, "prep_q", YL, groups, q_gain, fresh_q)
     q = lax.all_to_all(q_parts, ("yl", "x", "yh"), split_axis=0, concat_axis=0, tiled=True)
     kv_parts = prep(prep_kv_kernel, "prep_kv", 1, groups, k_gain, fresh_k, fresh_v)
-    r1, q, kv_parts = lax.optimization_barrier((r1, q, kv_parts))
+    down1, q, kv_parts = lax.optimization_barrier((r1[1], q, kv_parts))
+    r1 = (r1[0], down1)
     q = q.reshape(-1, width_dev)
     r2 = both(r1)
     fresh = lax.all_to_all(kv_parts, ("x", "yh"), split_axis=0, concat_axis=0, tiled=True)

time: 103 us -> 102 us (level); the launches traced: 101 us -> 101 us
  starting transfers between devices: 37.9 us -> 36.3 us
  waiting for transfers between devices: 27.9 us -> 29.5 us
    all_to_all x1, starting transfers between devices: 4.74 us -> 3.61 us  [body(): lax.all_to_all(parts, ('yl', 'x', 'yh'), split_axis=0, concat_axis=0, til...]
  transfers between devices with their start and end apart: 20 -> 20, of which waited for: 6 -> 7; matrix products, arithmetic and copies ran while one was open for 1% -> 1% of each run, Pallas kernels for 24% -> 24%
where the time goes in v4:
time: 102 us; the launch traced here: 101 us
  starting transfers between devices  36.3 us (36%)
  Pallas kernels  31 us (30%)
  waiting for transfers between devices  29.5 us (29%)
  local copies, waits for them, and re-layouts  3.77 us (4%)
    pallas_call x4, Pallas kernels, attend(): pl.pallas_call(functools.partial(attn_kernel, keys, spans, first, last),...  27.9 us
    ppermute x8, starting transfers between devices, both(): return (lax.ppermute(pair[0], 'z', UP), lax.ppermute(pair[1], 'z', DOWN))  14.7 us
    all_to_all x1, waiting for transfers between devices, body(): lax.all_to_all(parts, ('yl', 'x', 'yh'), split_axis=0, concat_axis=0, til...  11.8 us
    all_to_all x1, waiting for transfers between devices, body(): lax.all_to_all(q_parts, ('yl', 'x', 'yh'), split_axis=0, concat_axis=0, t...  9.42 us
    ppermute x9, starting transfers between devices, other_core(): return lax.ppermute(x, 'core', SWAP)  7.64 us
    all_to_all x1, starting transfers between devices, body(): lax.all_to_all(q_parts, ('yl', 'x', 'yh'), split_axis=0, concat_axis=0, t...  6.89 us
    ppermute x8, waiting for transfers between devices, both(): return (lax.ppermute(pair[0], 'z', UP), lax.ppermute(pair[1], 'z', DOWN))  4.76 us
    all_to_all x1, starting transfers between devices, body(): lax.all_to_all(parts, ('yl', 'x', 'yh'), split_axis=0, concat_axis=0, til...  3.61 us
  transfers between devices with their start and end apart: 20, of which 7 were waited for; matrix products, arithmetic and copies ran while one was open for 1% of the time, Pallas kernels for 24%

profile of v4, /device:TPU:1, one launch (start us, length us, event | category | flops | bytes accessed | tf_op | source)
XLA Modules:
  0.0 101.5 jit_solution(7223460516443835450)
XLA Ops:
  0.6 1.0 %constant_dynamic-update-slice_fusion.1 = bf16[384,768]{1,0:T(8,128)(2,1)S(1)} fusion(bf16[384,384]{1,0:T(8,128)(2,1)} %param.10), kind=kLoop, calls=%fused_computation.1 | loop fusion | bytes 589824
  1.8 6.5 %collective-permute-start = (bf16[384,768]{1,0:T(8,128)(2,1)S(1)}, bf16[384,768]{1,0:T(8,128)(2,1)}, u32[]{:S(2)}, u32[]{:S(2)}) collective-permute-start(bf16[384,768]{1,0:T(8,128)(2,1)S(1)} %constant_dynamic-update-slice_fusion.refs_1_), channel_id=1, source_target_pairs={{0,224},{32,0},{64,32},{96,64},{128,96},{160,128},{192,160},{224,1... | collective-permute-start | bytes 1769480 | tf_op jit(solution)/shard_map/ppermute | solution.py:268
  9.3 6.9 %all-to-all-start = ((bf16[16,48,384]{2,1,0:T(8,128)(2,1)}), bf16[16,48,384]{2,1,0:T(8,128)(2,1)S(1)}, u32[]{:S(2)}, u32[]{:S(2)}) async-start(bf16[16,48,384]{2,1,0:T(8,128)(2,1)} %prep_q.1), calls=%async_computation | async-start | bytes 1179648 | tf_op jit(solution)/shard_map/all_to_all | solution.py:276
  16.2 1.0 prep_kv.1
  17.2 9.4 %all-to-all-done = bf16[16,48,384]{2,1,0:T(8,128)(2,1)S(1)} async-done(((bf16[16,48,384]{2,1,0:T(8,128)(2,1)}), bf16[16,48,384]{2,1,0:T(8,128)(2,1)S(1)}, u32[]{:S(2)}, u32[]{:S(2)}) %all-to-all-start) | async-done | bytes 589856 | tf_op jit(solution)/shard_map/all_to_all | solution.py:276
  26.6 2.7 %collective-permute-start.5 = (bf16[384,768]{1,0:T(8,128)(2,1)}, bf16[384,768]{1,0:T(8,128)(2,1)S(1)}, u32[]{:S(2)}, u32[]{:S(2)}) collective-permute-start(bf16[384,768]{1,0:T(8,128)(2,1)} %collective-permute-done.refs_2_), channel_id=1, source_target_pairs={{0,8},{8,0},{1,9},{9,1},{2,10},{10,2},{3,11},{11,3},{4,12},{12,4},... | collective-permute-start | bytes 1769480 | tf_op jit(solution)/shard_map/ppermute | solution.py:258
  29.4 2.7 %collective-permute-start.3 = (bf16[384,768]{1,0:T(8,128)(2,1)}, bf16[384,768]{1,0:T(8,128)(2,1)S(1)}, u32[]{:S(2)}, u32[]{:S(2)}) collective-permute-start(bf16[384,768]{1,0:T(8,128)(2,1)} %collective-permute-done.refs_2_), channel_id=1, source_target_pairs={{0,224},{32,0},{64,32},{96,64},{128,96},{160,128},{192,160},{224,1... | collective-permute-start | bytes 1769480 | tf_op jit(solution)/shard_map/ppermute | solution.py:268
  32.1 3.5 %all-to-all-start.1 = ((bf16[8,48,768]{2,1,0:T(8,128)(2,1)}), bf16[8,48,768]{2,1,0:T(8,128)(2,1)S(1)}, u32[]{:S(2)}, u32[]{:S(2)}) async-start(bf16[8,48,768]{2,1,0:T(8,128)(2,1)} %prep_kv.1), calls=%async_computation.1 | async-start | bytes 1179648 | tf_op jit(solution)/shard_map/all_to_all | solution.py:282
  37.2 1.1 %copy-done.6 = bf16[384,768]{1,0:T(8,128)(2,1)S(1)} copy-done((bf16[384,768]{1,0:T(8,128)(2,1)S(1)}, bf16[384,768]{1,0:T(8,128)(2,1)}, u32[]{:S(2)}) %copy-start.6) | copy-done | bytes 589848
  38.3 6.6 %attend1.1 = (bf16[384,384]{1,0:T(8,128)(2,1)S(1)}, f32[384,128]{1,0:T(8,128)S(1)}, bf16[384,384]{1,0:T(8,128)(2,1)S(1)}, f32[384,128]{1,0:T(8,128)S(1)}) custom-call(bf16[768,384]{1,0:T(8,128)(2,1)S(1)} %bitcast.5, bf16[384,768]{1,0:T(8,128)(2,1)} %collective-permute-done.1.refs_1_, bf16[384,768]{1,0:T(8,128)(2,1)} %collective-permute-done.refs_2_, ...), custom_call_target="tpu_custom_call" | custom-call | flops 1811939328 | bytes 1048576 | tf_op jit(solution)/shard_map/attend1/pallas_call | solution.py:197
  44.9 2.0 %all-to-all-done.1 = bf16[8,48,768]{2,1,0:T(8,128)(2,1)S(1)} async-done(((bf16[8,48,768]{2,1,0:T(8,128)(2,1)}), bf16[8,48,768]{2,1,0:T(8,128)(2,1)S(1)}, u32[]{:S(2)}, u32[]{:S(2)}) %all-to-all-start.1) | async-done | bytes 589856 | tf_op jit(solution)/shard_map/all_to_all | solution.py:282
  47.7 1.6 %collective-permute-start.10 = (bf16[384,768]{1,0:T(8,128)(2,1)S(1)}, bf16[384,768]{1,0:T(8,128)(2,1)S(1)}, u32[]{:S(2)}, u32[]{:S(2)}) collective-permute-start(bf16[384,768]{1,0:T(8,128)(2,1)S(1)} %collective-permute-done.3.refs_4_), channel_id=1, source_target_pairs={{0,8},{8,0},{1,9},{9,1},{2,10},{10,2},{3,11},{11,3},{4,12},{12,4},... | collective-permute-start | bytes 1769480 | tf_op jit(solution)/shard_map/ppermute | solution.py:258
  49.3 2.7 %collective-permute-start.7 = (bf16[384,768]{1,0:T(8,128)(2,1)S(1)}, bf16[384,768]{1,0:T(8,128)(2,1)S(1)}, u32[]{:S(2)}, u32[]{:S(2)}) collective-permute-start(bf16[384,768]{1,0:T(8,128)(2,1)S(1)} %collective-permute-done.3.refs_4_), channel_id=1, source_target_pairs={{0,224},{32,0},{64,32},{96,64},{128,96},{160,128},{192,160},{224,1... | collective-permute-start | bytes 1769480 | tf_op jit(solution)/shard_map/ppermute | solution.py:268
  52.0 9.2 %attend2.1 = (bf16[384,384]{1,0:T(8,128)(2,1)S(1)}, f32[384,128]{1,0:T(8,128)S(1)}, bf16[384,384]{1,0:T(8,128)(2,1)S(1)}, f32[384,128]{1,0:T(8,128)S(1)}) custom-call(bf16[768,384]{1,0:T(8,128)(2,1)S(1)} %bitcast.6, ...), custom_call_target="tpu_custom_call", output_to_operand_aliasing={{0}: (8, {}), {1}: (9, {}), {2}: (10, {}), {3}: (11, {})} | custom-call | flops 2717908992 | bytes 1048576 | tf_op jit(solution)/shard_map/attend2/pallas_call | solution.py:197
  61.2 3.9 %collective-permute-done.6.refs_1_ = bf16[384,768]{1,0:T(8,128)(2,1)S(1)} collective-permute-done((bf16[384,768]{1,0:T(8,128)(2,1)}, bf16[384,768]{1,0:T(8,128)(2,1)S(1)}, u32[]{:S(2)}, u32[]{:S(2)}) %collective-permute-start.6) | collective-permute-done | bytes 589856 | tf_op jit(solution)/shard_map/ppermute | solution.py:268
  65.1 1.4 %collective-permute-start.13 = (bf16[384,768]{1,0:T(8,128)(2,1)S(1)}, bf16[384,768]{1,0:T(8,128)(2,1)S(1)}, u32[]{:S(2)}, u32[]{:S(2)}) collective-permute-start(bf16[384,768]{1,0:T(8,128)(2,1)S(1)} %collective-permute-done.6.refs_1_), channel_id=1, source_target_pairs={{0,8},{8,0},{1,9},{9,1},{2,10},{10,2},{3,11},{11,3},{4,12},{12,4},... | collective-permute-start | bytes 1769480 | tf_op jit(solution)/shard_map/ppermute | solution.py:258
  66.6 2.8 %collective-permute-start.12 = (bf16[192,768]{1,0:T(8,128)(2,1)S(1)}, bf16[192,768]{1,0:T(8,128)(2,1)S(1)}, u32[]{:S(2)}, u32[]{:S(2)}) collective-permute-start(bf16[192,768]{1,0:T(8,128)(2,1)S(1)} %slice.10), channel_id=1, source_target_pairs={{0,224},{32,0},{64,32},{96,64},{128,96},{160,128},{192,160},{224,1... | collective-permute-start | bytes 884744 | tf_op jit(solution)/shard_map/ppermute | solution.py:268
  69.4 6.9 %attend3.1 = (bf16[384,384]{1,0:T(8,128)(2,1)S(1)}, f32[384,128]{1,0:T(8,128)S(1)}, bf16[384,384]{1,0:T(8,128)(2,1)S(1)}, f32[384,128]{1,0:T(8,128)S(1)}) custom-call(bf16[768,384]{1,0:T(8,128)(2,1)S(1)} %bitcast.7, bf16[384,768]{1,0:T(8,128)(2,1)S(1)} %collective-permute-done.6.refs_1_, ...), custom_call_target="tpu_custom_call", output_to_operand_aliasing={{0}: (5, {}), {1}: (6, {}), {2}: (7, {}), {3}: (8, {})} | custom-call | flops 1811939328 | bytes 1048576 | tf_op jit(solution)/shard_map/attend3/pallas_call | solution.py:197
  76.3 1.1 %collective-permute-start.15 = (bf16[192,768]{1,0:T(8,128)(2,1)S(1)}, bf16[192,768]{1,0:T(8,128)(2,1)S(1)}, u32[]{:S(2)}, u32[]{:S(2)}) collective-permute-start(bf16[192,768]{1,0:T(8,128)(2,1)S(1)} %collective-permute-done.11.refs_1_), channel_id=1, source_target_pairs={{0,8},{8,0},{1,9},{9,1},{2,10},{10,2},{3,11},{11,3},{4,12},{12,4},... | collective-permute-start | bytes 884744 | tf_op jit(solution)/shard_map/ppermute | solution.py:258
  77.5 1.1 %collective-permute-done.15.refs_3_ = bf16[192,768]{1,0:T(8,128)(2,1)S(1)} collective-permute-done((bf16[192,768]{1,0:T(8,128)(2,1)S(1)}, bf16[192,768]{1,0:T(8,128)(2,1)S(1)}, u32[]{:S(2)}, u32[]{:S(2)}) %collective-permute-start.15) | collective-permute-done | bytes 294944 | tf_op jit(solution)/shard_map/ppermute | solution.py:258
  79.0 5.2 %attend4.1 = bf16[16,56,384]{2,1,0:T(8,128)(2,1)} custom-call(bf16[768,384]{1,0:T(8,128)(2,1)S(1)} %bitcast.8, bf16[192,768]{1,0:T(8,128)(2,1)S(1)} %collective-permute-done.11.refs_1_, bf16[192,768]{1,0:T(8,128)(2,1)S(1)} %collective-permute-done.12.refs_2_, bf16[192,768]{1,0:T(8,128)(2,1)S(1)} %collective-permute-done.15.refs_3_, ...), custom_call_target="tpu_custom_call" | custom-call | flops 905969664 | bytes 1048576 | tf_op jit(solution)/shard_map/attend4/pallas_call | solution.py:197
  84.2 3.6 %all-to-all-start.2 = ((bf16[16,56,384]{2,1,0:T(8,128)(2,1)}), bf16[16,56,384]{2,1,0:T(8,128)(2,1)S(1)}, u32[]{:S(2)}, u32[]{:S(2)}) async-start(bf16[16,56,384]{2,1,0:T(8,128)(2,1)} %attend4.1), calls=%async_computation.2 | async-start | bytes 1376256 | tf_op jit(solution)/shard_map/all_to_all | solution.py:296
  88.5 11.8 %all-to-all-done.2.in_ref = bf16[16,56,384]{2,1,0:T(8,128)(2,1)S(1)} async-done(((bf16[16,56,384]{2,1,0:T(8,128)(2,1)}), bf16[16,56,384]{2,1,0:T(8,128)(2,1)S(1)}, u32[]{:S(2)}, u32[]{:S(2)}) %all-to-all-start.2) | async-done | bytes 688160 | tf_op jit(solution)/shard_map/all_to_all | solution.py:296
  100.3 1.2 %merge.1 = bf16[48,3072]{1,0:T(8,128)(2,1)} custom-call(bf16[16,56,384]{2,1,0:T(8,128)(2,1)S(1)} %all-to-all-done.2.in_ref), custom_call_target="tpu_custom_call" | custom-call | tf_op jit(solution)/shard_map/merge/pallas_call | solution.py:241
  (44 shorter events, 5.0 us)
Async XLA Ops:
  1.7 6.6 %copy-start = (bf16[48,3072]{1,0:T(8,128)(2,1)S(1)}, bf16[48,3072]{1,0:T(8,128)(2,1)}, u32[]{:S(2)}) copy-start(bf16[48,3072]{1,0:T(8,128)(2,1)} %q_ref.1) | copy-start | bytes 884740
  1.8 24.9 %collective-permute-start = (bf16[384,768]{1,0:T(8,128)(2,1)S(1)}, bf16[384,768]{1,0:T(8,128)(2,1)}, u32[]{:S(2)}, u32[]{:S(2)}) collective-permute-start(bf16[384,768]{1,0:T(8,128)(2,1)S(1)} %constant_dynamic-update-slice_fusion.refs_1_), channel_id=1, source_target_pairs={{0,224},{32,0},{64,32},{96,64},{128,96},{160,128},{192,160},{224,1... | collective-permute-start | bytes 1769480 | tf_op jit(solution)/shard_map/ppermute | solution.py:268
  8.3 21.0 %collective-permute-start.1 = (bf16[384,768]{1,0:T(8,128)(2,1)S(1)}, bf16[384,768]{1,0:T(8,128)(2,1)}, u32[]{:S(2)}, u32[]{:S(2)}) collective-permute-start(bf16[384,768]{1,0:T(8,128)(2,1)S(1)} %constant_dynamic-update-slice_fusion.refs_1_), channel_id=1, source_target_pairs={{0,32},{32,64},{64,96},{96,128},{128,160},{160,192},{192,224},{224... | collective-permute-start | bytes 1769480 | tf_op jit(solution)/shard_map/ppermute | solution.py:268
  9.3 6.9 %copy-start.1 = (bf16[48,3072]{1,0:T(8,128)(2,1)S(1)}, bf16[48,3072]{1,0:T(8,128)(2,1)}, u32[]{:S(2)}) copy-start(bf16[48,3072]{1,0:T(8,128)(2,1)} %k_ref.1) | copy-start | bytes 884740
  9.3 6.9 %copy-start.2 = (bf16[48,3072]{1,0:T(8,128)(2,1)S(1)}, bf16[48,3072]{1,0:T(8,128)(2,1)}, u32[]{:S(2)}) copy-start(bf16[48,3072]{1,0:T(8,128)(2,1)} %v_ref.1) | copy-start | bytes 884740
  9.3 6.9 %copy-start.4 = (f32[3072]{0:T(1024)S(1)}, f32[3072]{0:T(1024)}, u32[]{:S(2)}) copy-start(f32[3072]{0:T(1024)} %param.13) | copy-start | bytes 36868
  9.3 17.4 %all-to-all-start = ((bf16[16,48,384]{2,1,0:T(8,128)(2,1)}), bf16[16,48,384]{2,1,0:T(8,128)(2,1)S(1)}, u32[]{:S(2)}, u32[]{:S(2)}) async-start(bf16[16,48,384]{2,1,0:T(8,128)(2,1)} %prep_q.1), calls=%async_computation | async-start | bytes 1179648 | tf_op jit(solution)/shard_map/all_to_all | solution.py:276
  26.6 9.8 %collective-permute-start.5 = (bf16[384,768]{1,0:T(8,128)(2,1)}, bf16[384,768]{1,0:T(8,128)(2,1)S(1)}, u32[]{:S(2)}, u32[]{:S(2)}) collective-permute-start(bf16[384,768]{1,0:T(8,128)(2,1)} %collective-permute-done.refs_2_), channel_id=1, source_target_pairs={{0,8},{8,0},{1,9},{9,1},{2,10},{10,2},{3,11},{11,3},{4,12},{12,4},... | collective-permute-start | bytes 1769480 | tf_op jit(solution)/shard_map/ppermute | solution.py:258
  29.3 7.9 %collective-permute-start.4 = (bf16[384,768]{1,0:T(8,128)(2,1)}, bf16[384,768]{1,0:T(8,128)(2,1)}, u32[]{:S(2)}, u32[]{:S(2)}) collective-permute-start(bf16[384,768]{1,0:T(8,128)(2,1)} %collective-permute-done.1.refs_1_), channel_id=1, source_target_pairs={{0,8},{8,0},{1,9},{9,1},{2,10},{10,2},{3,11},{11,3},{4,12},{12,4},... | collective-permute-start | bytes 1769480 | tf_op jit(solution)/shard_map/ppermute | solution.py:258
  29.4 17.5 %collective-permute-start.3 = (bf16[384,768]{1,0:T(8,128)(2,1)}, bf16[384,768]{1,0:T(8,128)(2,1)S(1)}, u32[]{:S(2)}, u32[]{:S(2)}) collective-permute-start(bf16[384,768]{1,0:T(8,128)(2,1)} %collective-permute-done.refs_2_), channel_id=1, source_target_pairs={{0,224},{32,0},{64,32},{96,64},{128,96},{160,128},{192,160},{224,1... | collective-permute-start | bytes 1769480 | tf_op jit(solution)/shard_map/ppermute | solution.py:268
  32.1 15.7 %collective-permute-start.2 = (bf16[384,768]{1,0:T(8,128)(2,1)}, bf16[384,768]{1,0:T(8,128)(2,1)}, u32[]{:S(2)}, u32[]{:S(2)}) collective-permute-start(bf16[384,768]{1,0:T(8,128)(2,1)} %collective-permute-done.1.refs_1_), channel_id=1, source_target_pairs={{0,32},{32,64},{64,96},{96,128},{128,160},{160,192},{192,224},{224... | collective-permute-start | bytes 1769480 | tf_op jit(solution)/shard_map/ppermute | solution.py:268
  32.1 14.9 %all-to-all-start.1 = ((bf16[8,48,768]{2,1,0:T(8,128)(2,1)}), bf16[8,48,768]{2,1,0:T(8,128)(2,1)S(1)}, u32[]{:S(2)}, u32[]{:S(2)}) async-start(bf16[8,48,768]{2,1,0:T(8,128)(2,1)} %prep_kv.1), calls=%async_computation.1 | async-start | bytes 1179648 | tf_op jit(solution)/shard_map/all_to_all | solution.py:282
  35.6 16.4 %collective-permute-start.8 = (bf16[384,768]{1,0:T(8,128)(2,1)S(1)}, bf16[384,768]{1,0:T(8,128)(2,1)}, u32[]{:S(2)}, u32[]{:S(2)}) collective-permute-start(bf16[384,768]{1,0:T(8,128)(2,1)S(1)} %constant_dynamic-update-slice_fusion.refs_1_), channel_id=1, source_target_pairs={{0,8},{8,0},{1,9},{9,1},{2,10},{10,2},{3,11},{11,3},{4,12},{12,4},... | collective-permute-start | bytes 1769480 | tf_op jit(solution)/shard_map/ppermute | solution.py:258
  47.7 4.3 %collective-permute-start.10 = (bf16[384,768]{1,0:T(8,128)(2,1)S(1)}, bf16[384,768]{1,0:T(8,128)(2,1)S(1)}, u32[]{:S(2)}, u32[]{:S(2)}) collective-permute-start(bf16[384,768]{1,0:T(8,128)(2,1)S(1)} %collective-permute-done.3.refs_4_), channel_id=1, source_target_pairs={{0,8},{8,0},{1,9},{9,1},{2,10},{10,2},{3,11},{11,3},{4,12},{12,4},... | collective-permute-start | bytes 1769480 | tf_op jit(solution)/shard_map/ppermute | solution.py:258
  49.3 2.7 %collective-permute-start.9 = (bf16[384,768]{1,0:T(8,128)(2,1)}, bf16[384,768]{1,0:T(8,128)(2,1)S(1)}, u32[]{:S(2)}, u32[]{:S(2)}) collective-permute-start(bf16[384,768]{1,0:T(8,128)(2,1)} %collective-permute-done.2.refs_3_), channel_id=1, source_target_pairs={{0,8},{8,0},{1,9},{9,1},{2,10},{10,2},{3,11},{11,3},{4,12},{12,4},... | collective-permute-start | bytes 1769480 | tf_op jit(solution)/shard_map/ppermute | solution.py:258
  49.3 15.8 %collective-permute-start.6 = (bf16[384,768]{1,0:T(8,128)(2,1)}, bf16[384,768]{1,0:T(8,128)(2,1)S(1)}, u32[]{:S(2)}, u32[]{:S(2)}) collective-permute-start(bf16[384,768]{1,0:T(8,128)(2,1)} %collective-permute-done.2.refs_3_), channel_id=1, source_target_pairs={{0,32},{32,64},{64,96},{96,128},{128,160},{160,192},{192,224},{224... | collective-permute-start | bytes 1769480 | tf_op jit(solution)/shard_map/ppermute | solution.py:268
  49.3 15.8 %collective-permute-start.7 = (bf16[384,768]{1,0:T(8,128)(2,1)S(1)}, bf16[384,768]{1,0:T(8,128)(2,1)S(1)}, u32[]{:S(2)}, u32[]{:S(2)}) collective-permute-start(bf16[384,768]{1,0:T(8,128)(2,1)S(1)} %collective-permute-done.3.refs_4_), channel_id=1, source_target_pairs={{0,224},{32,0},{64,32},{96,64},{128,96},{160,128},{192,160},{224,1... | collective-permute-start | bytes 1769480 | tf_op jit(solution)/shard_map/ppermute | solution.py:268
  65.1 4.3 %collective-permute-start.13 = (bf16[384,768]{1,0:T(8,128)(2,1)S(1)}, bf16[384,768]{1,0:T(8,128)(2,1)S(1)}, u32[]{:S(2)}, u32[]{:S(2)}) collective-permute-start(bf16[384,768]{1,0:T(8,128)(2,1)S(1)} %collective-permute-done.6.refs_1_), channel_id=1, source_target_pairs={{0,8},{8,0},{1,9},{9,1},{2,10},{10,2},{3,11},{11,3},{4,12},{12,4},... | collective-permute-start | bytes 1769480 | tf_op jit(solution)/shard_map/ppermute | solution.py:258
  66.5 2.9 %collective-permute-start.14 = (bf16[384,768]{1,0:T(8,128)(2,1)S(1)}, bf16[384,768]{1,0:T(8,128)(2,1)S(1)}, u32[]{:S(2)}, u32[]{:S(2)}) collective-permute-start(bf16[384,768]{1,0:T(8,128)(2,1)S(1)} %collective-permute-done.7.refs_2_), channel_id=1, source_target_pairs={{0,8},{8,0},{1,9},{9,1},{2,10},{10,2},{3,11},{11,3},{4,12},{12,4},... | collective-permute-start | bytes 1769480 | tf_op jit(solution)/shard_map/ppermute | solution.py:258
  66.6 9.7 %collective-permute-start.11 = (bf16[192,768]{1,0:T(8,128)(2,1)S(1)}, bf16[192,768]{1,0:T(8,128)(2,1)S(1)}, u32[]{:S(2)}, u32[]{:S(2)}) collective-permute-start(bf16[192,768]{1,0:T(8,128)(2,1)S(1)} %slice.9), channel_id=1, source_target_pairs={{0,32},{32,64},{64,96},{96,128},{128,160},{160,192},{192,224},{224... | collective-permute-start | bytes 884744 | tf_op jit(solution)/shard_map/ppermute | solution.py:268
  66.6 9.7 %collective-permute-start.12 = (bf16[192,768]{1,0:T(8,128)(2,1)S(1)}, bf16[192,768]{1,0:T(8,128)(2,1)S(1)}, u32[]{:S(2)}, u32[]{:S(2)}) collective-permute-start(bf16[192,768]{1,0:T(8,128)(2,1)S(1)} %slice.10), channel_id=1, source_target_pairs={{0,224},{32,0},{64,32},{96,64},{128,96},{160,128},{192,160},{224,1... | collective-permute-start | bytes 884744 | tf_op jit(solution)/shard_map/ppermute | solution.py:268
  76.3 2.3 %collective-permute-start.15 = (bf16[192,768]{1,0:T(8,128)(2,1)S(1)}, bf16[192,768]{1,0:T(8,128)(2,1)S(1)}, u32[]{:S(2)}, u32[]{:S(2)}) collective-permute-start(bf16[192,768]{1,0:T(8,128)(2,1)S(1)} %collective-permute-done.11.refs_1_), channel_id=1, source_target_pairs={{0,8},{8,0},{1,9},{9,1},{2,10},{10,2},{3,11},{11,3},{4,12},{12,4},... | collective-permute-start | bytes 884744 | tf_op jit(solution)/shard_map/ppermute | solution.py:258
  77.4 1.6 %collective-permute-start.16 = (bf16[192,768]{1,0:T(8,128)(2,1)S(1)}, bf16[192,768]{1,0:T(8,128)(2,1)S(1)}, u32[]{:S(2)}, u32[]{:S(2)}) collective-permute-start(bf16[192,768]{1,0:T(8,128)(2,1)S(1)} %collective-permute-done.12.refs_2_), channel_id=1, source_target_pairs={{0,8},{8,0},{1,9},{9,1},{2,10},{10,2},{3,11},{11,3},{4,12},{12,4},... | collective-permute-start | bytes 884744 | tf_op jit(solution)/shard_map/ppermute | solution.py:258
  84.2 16.2 %all-to-all-start.2 = ((bf16[16,56,384]{2,1,0:T(8,128)(2,1)}), bf16[16,56,384]{2,1,0:T(8,128)(2,1)S(1)}, u32[]{:S(2)}, u32[]{:S(2)}) async-start(bf16[16,56,384]{2,1,0:T(8,128)(2,1)} %attend4.1), calls=%async_computation.2 | async-start | bytes 1376256 | tf_op jit(solution)/shard_map/all_to_all | solution.py:296
  (4 other events, 9.5 us)

commit v5 on v4

--- a/solution.py
+++ b/solution.py
@@ -282,10 +282,11 @@
     fresh = lax.all_to_all(kv_parts, ("x", "yh"), split_axis=0, concat_axis=0, tiled=True)
     own_other = other_core(own)
     state = attend(q, yl, [*r1, *swap(r1)], name="attend1")
-    r2, state, fresh = lax.optimization_barrier((r2, state, fresh))
+    r2, state = lax.optimization_barrier((r2, state))
+
+    r3 = both(r2)
+    r2, fresh = lax.optimization_barrier((r2, fresh))
     fresh = fresh.reshape(-1, 2 * width_dev)
-
-    r3 = both(r2)
     blocks = [own, own_other, *r2, *swap(r2), fresh]
     state = attend(q, yl, blocks, state, [(1, 7), (0, 6)], name="attend2")
     r3, state = lax.optimization_barrier((r3, state))

time: 102 us -> 102 us (level)
    ppermute x8, waiting for transfers between devices: 4.76 us -> 6.75 us  [both(): return (lax.ppermute(pair[0], 'z', UP), lax.ppermute(pair[1], 'z', DOWN))]
    all_to_all x1, waiting for transfers between devices: 1.99 us -> 0.01 us  [body(): lax.all_to_all(kv_parts, ('x', 'yh'), split_axis=0, concat_axis=0, tiled=...]
  transfers between devices with their start and end apart: 20 -> 20, of which waited for: 7 -> 6; matrix products, arithmetic and copies ran while one was open for 1% -> 1% of each run, Pallas kernels for 24% -> 24%
where the time goes in v5:
time: 102 us
  starting transfers between devices  36.3 us (36%)
  Pallas kernels  31 us (30%)
  waiting for transfers between devices  29.5 us (29%)
  local copies, waits for them, and re-layouts  3.77 us (4%)
    pallas_call x4, Pallas kernels, attend(): pl.pallas_call(functools.partial(attn_kernel, keys, spans, first, last),...  27.9 us
    ppermute x8, starting transfers between devices, both(): return (lax.ppermute(pair[0], 'z', UP), lax.ppermute(pair[1], 'z', DOWN))  14.7 us
    all_to_all x1, waiting for transfers between devices, body(): lax.all_to_all(parts, ('yl', 'x', 'yh'), split_axis=0, concat_axis=0, til...  11.8 us
    all_to_all x1, waiting for transfers between devices, body(): lax.all_to_all(q_parts, ('yl', 'x', 'yh'), split_axis=0, concat_axis=0, t...  9.44 us
    ppermute x9, starting transfers between devices, other_core(): return lax.ppermute(x, 'core', SWAP)  7.64 us
    all_to_all x1, starting transfers between devices, body(): lax.all_to_all(q_parts, ('yl', 'x', 'yh'), split_axis=0, concat_axis=0, t...  6.89 us
    ppermute x8, waiting for transfers between devices, both(): return (lax.ppermute(pair[0], 'z', UP), lax.ppermute(pair[1], 'z', DOWN))  6.75 us
    all_to_all x1, starting transfers between devices, body(): lax.all_to_all(parts, ('yl', 'x', 'yh'), split_axis=0, concat_axis=0, til...  3.61 us
  transfers between devices with their start and end apart: 20, of which 6 were waited for; matrix products, arithmetic and copies ran while one was open for 1% of the time, Pallas kernels for 24%

profile of v5, /device:TPU:1, one launch (start us, length us, event | category | flops | bytes accessed | tf_op | source)
XLA Modules:
  0.0 101.5 jit_solution(10880726531265388024)
XLA Ops:
  0.6 1.0 %constant_dynamic-update-slice_fusion.1 = bf16[384,768]{1,0:T(8,128)(2,1)S(1)} fusion(bf16[384,384]{1,0:T(8,128)(2,1)} %param.10), kind=kLoop, calls=%fused_computation.1 | loop fusion | bytes 589824
  1.8 6.5 %collective-permute-start = (bf16[384,768]{1,0:T(8,128)(2,1)S(1)}, bf16[384,768]{1,0:T(8,128)(2,1)}, u32[]{:S(2)}, u32[]{:S(2)}) collective-permute-start(bf16[384,768]{1,0:T(8,128)(2,1)S(1)} %constant_dynamic-update-slice_fusion.refs_1_), channel_id=1, source_target_pairs={{0,224},{32,0},{64,32},{96,64},{128,96},{160,128},{192,160},{224,1... | collective-permute-start | bytes 1769480 | tf_op jit(solution)/shard_map/ppermute | solution.py:268
  8.3 1.0 %prep_q.1 = bf16[16,48,384]{2,1,0:T(8,128)(2,1)} custom-call(bf16[48,3072]{1,0:T(8,128)(2,1)S(1)} %copy-done, f32[1,3072]{1,0:T(1,128)S(1)} %bitcast.11), custom_call_target="tpu_custom_call" | custom-call | tf_op jit(solution)/shard_map/prep_q/pallas_call | solution.py:47
  9.3 6.9 %all-to-all-start = ((bf16[16,48,384]{2,1,0:T(8,128)(2,1)}), bf16[16,48,384]{2,1,0:T(8,128)(2,1)S(1)}, u32[]{:S(2)}, u32[]{:S(2)}) async-start(bf16[16,48,384]{2,1,0:T(8,128)(2,1)} %prep_q.1), calls=%async_computation | async-start | bytes 1179648 | tf_op jit(solution)/shard_map/all_to_all | solution.py:276
  17.2 9.4 %all-to-all-done = bf16[16,48,384]{2,1,0:T(8,128)(2,1)S(1)} async-done(((bf16[16,48,384]{2,1,0:T(8,128)(2,1)}), bf16[16,48,384]{2,1,0:T(8,128)(2,1)S(1)}, u32[]{:S(2)}, u32[]{:S(2)}) %all-to-all-start) | async-done | bytes 589856 | tf_op jit(solution)/shard_map/all_to_all | solution.py:276
  26.6 2.7 %collective-permute-start.5 = (bf16[384,768]{1,0:T(8,128)(2,1)}, bf16[384,768]{1,0:T(8,128)(2,1)S(1)}, u32[]{:S(2)}, u32[]{:S(2)}) collective-permute-start(bf16[384,768]{1,0:T(8,128)(2,1)} %collective-permute-done.refs_2_), channel_id=1, source_target_pairs={{0,8},{8,0},{1,9},{9,1},{2,10},{10,2},{3,11},{11,3},{4,12},{12,4},... | collective-permute-start | bytes 1769480 | tf_op jit(solution)/shard_map/ppermute | solution.py:258
  29.4 2.7 %collective-permute-start.3 = (bf16[384,768]{1,0:T(8,128)(2,1)}, bf16[384,768]{1,0:T(8,128)(2,1)S(1)}, u32[]{:S(2)}, u32[]{:S(2)}) collective-permute-start(bf16[384,768]{1,0:T(8,128)(2,1)} %collective-permute-done.refs_2_), channel_id=1, source_target_pairs={{0,224},{32,0},{64,32},{96,64},{128,96},{160,128},{192,160},{224,1... | collective-permute-start | bytes 1769480 | tf_op jit(solution)/shard_map/ppermute | solution.py:268
  32.1 3.5 %all-to-all-start.1 = ((bf16[8,48,768]{2,1,0:T(8,128)(2,1)}), bf16[8,48,768]{2,1,0:T(8,128)(2,1)S(1)}, u32[]{:S(2)}, u32[]{:S(2)}) async-start(bf16[8,48,768]{2,1,0:T(8,128)(2,1)} %prep_kv.1), calls=%async_computation.1 | async-start | bytes 1179648 | tf_op jit(solution)/shard_map/all_to_all | solution.py:282
  37.2 1.1 %copy-done.6 = bf16[384,768]{1,0:T(8,128)(2,1)S(1)} copy-done((bf16[384,768]{1,0:T(8,128)(2,1)S(1)}, bf16[384,768]{1,0:T(8,128)(2,1)}, u32[]{:S(2)}) %copy-start.6) | copy-done | bytes 589848
  38.3 6.6 %attend1.1 = (bf16[384,384]{1,0:T(8,128)(2,1)S(1)}, f32[384,128]{1,0:T(8,128)S(1)}, bf16[384,384]{1,0:T(8,128)(2,1)S(1)}, f32[384,128]{1,0:T(8,128)S(1)}) custom-call(bf16[768,384]{1,0:T(8,128)(2,1)S(1)} %bitcast.5, bf16[384,768]{1,0:T(8,128)(2,1)} %collective-permute-done.1.refs_1_, bf16[384,768]{1,0:T(8,128)(2,1)} %collective-permute-done.refs_2_, ...), custom_call_target="tpu_custom_call" | custom-call | flops 1811939328 | bytes 1048576 | tf_op jit(solution)/shard_map/attend1/pallas_call | solution.py:197
  44.9 2.8 %collective-permute-done.2.refs_3_ = bf16[384,768]{1,0:T(8,128)(2,1)} collective-permute-done((bf16[384,768]{1,0:T(8,128)(2,1)}, bf16[384,768]{1,0:T(8,128)(2,1)}, u32[]{:S(2)}, u32[]{:S(2)}) %collective-permute-start.2) | collective-permute-done | bytes 589856 | tf_op jit(solution)/shard_map/ppermute | solution.py:268
  47.8 1.6 %collective-permute-start.10 = (bf16[384,768]{1,0:T(8,128)(2,1)S(1)}, bf16[384,768]{1,0:T(8,128)(2,1)S(1)}, u32[]{:S(2)}, u32[]{:S(2)}) collective-permute-start(bf16[384,768]{1,0:T(8,128)(2,1)S(1)} %collective-permute-done.3.refs_4_), channel_id=1, source_target_pairs={{0,8},{8,0},{1,9},{9,1},{2,10},{10,2},{3,11},{11,3},{4,12},{12,4},... | collective-permute-start | bytes 1769480 | tf_op jit(solution)/shard_map/ppermute | solution.py:258
  49.4 2.7 %collective-permute-start.7 = (bf16[384,768]{1,0:T(8,128)(2,1)S(1)}, bf16[384,768]{1,0:T(8,128)(2,1)S(1)}, u32[]{:S(2)}, u32[]{:S(2)}) collective-permute-start(bf16[384,768]{1,0:T(8,128)(2,1)S(1)} %collective-permute-done.3.refs_4_), channel_id=1, source_target_pairs={{0,224},{32,0},{64,32},{96,64},{128,96},{160,128},{192,160},{224,1... | collective-permute-start | bytes 1769480 | tf_op jit(solution)/shard_map/ppermute | solution.py:268
  52.0 9.2 %attend2.1 = (bf16[384,384]{1,0:T(8,128)(2,1)S(1)}, f32[384,128]{1,0:T(8,128)S(1)}, bf16[384,384]{1,0:T(8,128)(2,1)S(1)}, f32[384,128]{1,0:T(8,128)S(1)}) custom-call(bf16[768,384]{1,0:T(8,128)(2,1)S(1)} %bitcast.6, ...), custom_call_target="tpu_custom_call", output_to_operand_aliasing={{0}: (8, {}), {1}: (9, {}), {2}: (10, {}), {3}: (11, {})} | custom-call | flops 2717908992 | bytes 1048576 | tf_op jit(solution)/shard_map/attend2/pallas_call | solution.py:197
  61.2 3.9 %collective-permute-done.6.refs_1_ = bf16[384,768]{1,0:T(8,128)(2,1)S(1)} collective-permute-done((bf16[384,768]{1,0:T(8,128)(2,1)}, bf16[384,768]{1,0:T(8,128)(2,1)S(1)}, u32[]{:S(2)}, u32[]{:S(2)}) %collective-permute-start.6) | collective-permute-done | bytes 589856 | tf_op jit(solution)/shard_map/ppermute | solution.py:268
  65.2 1.4 %collective-permute-start.13 = (bf16[384,768]{1,0:T(8,128)(2,1)S(1)}, bf16[384,768]{1,0:T(8,128)(2,1)S(1)}, u32[]{:S(2)}, u32[]{:S(2)}) collective-permute-start(bf16[384,768]{1,0:T(8,128)(2,1)S(1)} %collective-permute-done.6.refs_1_), channel_id=1, source_target_pairs={{0,8},{8,0},{1,9},{9,1},{2,10},{10,2},{3,11},{11,3},{4,12},{12,4},... | collective-permute-start | bytes 1769480 | tf_op jit(solution)/shard_map/ppermute | solution.py:258
  66.7 2.8 %collective-permute-start.12 = (bf16[192,768]{1,0:T(8,128)(2,1)S(1)}, bf16[192,768]{1,0:T(8,128)(2,1)S(1)}, u32[]{:S(2)}, u32[]{:S(2)}) collective-permute-start(bf16[192,768]{1,0:T(8,128)(2,1)S(1)} %slice.10), channel_id=1, source_target_pairs={{0,224},{32,0},{64,32},{96,64},{128,96},{160,128},{192,160},{224,1... | collective-permute-start | bytes 884744 | tf_op jit(solution)/shard_map/ppermute | solution.py:268
  69.4 6.9 %attend3.1 = (bf16[384,384]{1,0:T(8,128)(2,1)S(1)}, f32[384,128]{1,0:T(8,128)S(1)}, bf16[384,384]{1,0:T(8,128)(2,1)S(1)}, f32[384,128]{1,0:T(8,128)S(1)}) custom-call(bf16[768,384]{1,0:T(8,128)(2,1)S(1)} %bitcast.7, bf16[384,768]{1,0:T(8,128)(2,1)S(1)} %collective-permute-done.6.refs_1_, ...), custom_call_target="tpu_custom_call", output_to_operand_aliasing={{0}: (5, {}), {1}: (6, {}), {2}: (7, {}), {3}: (8, {})} | custom-call | flops 1811939328 | bytes 1048576 | tf_op jit(solution)/shard_map/attend3/pallas_call | solution.py:197
  76.3 1.1 %collective-permute-start.15 = (bf16[192,768]{1,0:T(8,128)(2,1)S(1)}, bf16[192,768]{1,0:T(8,128)(2,1)S(1)}, u32[]{:S(2)}, u32[]{:S(2)}) collective-permute-start(bf16[192,768]{1,0:T(8,128)(2,1)S(1)} %collective-permute-done.11.refs_1_), channel_id=1, source_target_pairs={{0,8},{8,0},{1,9},{9,1},{2,10},{10,2},{3,11},{11,3},{4,12},{12,4},... | collective-permute-start | bytes 884744 | tf_op jit(solution)/shard_map/ppermute | solution.py:258
  77.5 1.1 %collective-permute-done.15.refs_3_ = bf16[192,768]{1,0:T(8,128)(2,1)S(1)} collective-permute-done((bf16[192,768]{1,0:T(8,128)(2,1)S(1)}, bf16[192,768]{1,0:T(8,128)(2,1)S(1)}, u32[]{:S(2)}, u32[]{:S(2)}) %collective-permute-start.15) | collective-permute-done | bytes 294944 | tf_op jit(solution)/shard_map/ppermute | solution.py:258
  79.0 5.2 %attend4.1 = bf16[16,56,384]{2,1,0:T(8,128)(2,1)} custom-call(bf16[768,384]{1,0:T(8,128)(2,1)S(1)} %bitcast.8, bf16[192,768]{1,0:T(8,128)(2,1)S(1)} %collective-permute-done.11.refs_1_, bf16[192,768]{1,0:T(8,128)(2,1)S(1)} %collective-permute-done.12.refs_2_, bf16[192,768]{1,0:T(8,128)(2,1)S(1)} %collective-permute-done.15.refs_3_, ...), custom_call_target="tpu_custom_call" | custom-call | flops 905969664 | bytes 1048576 | tf_op jit(solution)/shard_map/attend4/pallas_call | solution.py:197
  84.2 3.6 %all-to-all-start.2 = ((bf16[16,56,384]{2,1,0:T(8,128)(2,1)}), bf16[16,56,384]{2,1,0:T(8,128)(2,1)S(1)}, u32[]{:S(2)}, u32[]{:S(2)}) async-start(bf16[16,56,384]{2,1,0:T(8,128)(2,1)} %attend4.1), calls=%async_computation.2 | async-start | bytes 1376256 | tf_op jit(solution)/shard_map/all_to_all | solution.py:297
  88.5 11.8 %all-to-all-done.2.in_ref = bf16[16,56,384]{2,1,0:T(8,128)(2,1)S(1)} async-done(((bf16[16,56,384]{2,1,0:T(8,128)(2,1)}), bf16[16,56,384]{2,1,0:T(8,128)(2,1)S(1)}, u32[]{:S(2)}, u32[]{:S(2)}) %all-to-all-start.2) | async-done | bytes 688160 | tf_op jit(solution)/shard_map/all_to_all | solution.py:297
  100.3 1.2 %merge.1 = bf16[48,3072]{1,0:T(8,128)(2,1)} custom-call(bf16[16,56,384]{2,1,0:T(8,128)(2,1)S(1)} %all-to-all-done.2.in_ref), custom_call_target="tpu_custom_call" | custom-call | tf_op jit(solution)/shard_map/merge/pallas_call | solution.py:241
  (44 shorter events, 4.2 us)
Async XLA Ops:
  1.7 6.6 %copy-start = (bf16[48,3072]{1,0:T(8,128)(2,1)S(1)}, bf16[48,3072]{1,0:T(8,128)(2,1)}, u32[]{:S(2)}) copy-start(bf16[48,3072]{1,0:T(8,128)(2,1)} %q_ref.1) | copy-start | bytes 884740
  1.8 24.9 %collective-permute-start = (bf16[384,768]{1,0:T(8,128)(2,1)S(1)}, bf16[384,768]{1,0:T(8,128)(2,1)}, u32[]{:S(2)}, u32[]{:S(2)}) collective-permute-start(bf16[384,768]{1,0:T(8,128)(2,1)S(1)} %constant_dynamic-update-slice_fusion.refs_1_), channel_id=1, source_target_pairs={{0,224},{32,0},{64,32},{96,64},{128,96},{160,128},{192,160},{224,1... | collective-permute-start | bytes 1769480 | tf_op jit(solution)/shard_map/ppermute | solution.py:268
  8.3 21.1 %collective-permute-start.1 = (bf16[384,768]{1,0:T(8,128)(2,1)S(1)}, bf16[384,768]{1,0:T(8,128)(2,1)}, u32[]{:S(2)}, u32[]{:S(2)}) collective-permute-start(bf16[384,768]{1,0:T(8,128)(2,1)S(1)} %constant_dynamic-update-slice_fusion.refs_1_), channel_id=1, source_target_pairs={{0,32},{32,64},{64,96},{96,128},{128,160},{160,192},{192,224},{224... | collective-permute-start | bytes 1769480 | tf_op jit(solution)/shard_map/ppermute | solution.py:268
  9.3 6.9 %copy-start.1 = (bf16[48,3072]{1,0:T(8,128)(2,1)S(1)}, bf16[48,3072]{1,0:T(8,128)(2,1)}, u32[]{:S(2)}) copy-start(bf16[48,3072]{1,0:T(8,128)(2,1)} %k_ref.1) | copy-start | bytes 884740
  9.3 6.9 %copy-start.2 = (bf16[48,3072]{1,0:T(8,128)(2,1)S(1)}, bf16[48,3072]{1,0:T(8,128)(2,1)}, u32[]{:S(2)}) copy-start(bf16[48,3072]{1,0:T(8,128)(2,1)} %v_ref.1) | copy-start | bytes 884740
  9.3 6.9 %copy-start.4 = (f32[3072]{0:T(1024)S(1)}, f32[3072]{0:T(1024)}, u32[]{:S(2)}) copy-start(f32[3072]{0:T(1024)} %param.13) | copy-start | bytes 36868
  9.3 17.4 %all-to-all-start = ((bf16[16,48,384]{2,1,0:T(8,128)(2,1)}), bf16[16,48,384]{2,1,0:T(8,128)(2,1)S(1)}, u32[]{:S(2)}, u32[]{:S(2)}) async-start(bf16[16,48,384]{2,1,0:T(8,128)(2,1)} %prep_q.1), calls=%async_computation | async-start | bytes 1179648 | tf_op jit(solution)/shard_map/all_to_all | solution.py:276
  26.6 9.8 %collective-permute-start.5 = (bf16[384,768]{1,0:T(8,128)(2,1)}, bf16[384,768]{1,0:T(8,128)(2,1)S(1)}, u32[]{:S(2)}, u32[]{:S(2)}) collective-permute-start(bf16[384,768]{1,0:T(8,128)(2,1)} %collective-permute-done.refs_2_), channel_id=1, source_target_pairs={{0,8},{8,0},{1,9},{9,1},{2,10},{10,2},{3,11},{11,3},{4,12},{12,4},... | collective-permute-start | bytes 1769480 | tf_op jit(solution)/shard_map/ppermute | solution.py:258
  29.3 7.9 %collective-permute-start.4 = (bf16[384,768]{1,0:T(8,128)(2,1)}, bf16[384,768]{1,0:T(8,128)(2,1)}, u32[]{:S(2)}, u32[]{:S(2)}) collective-permute-start(bf16[384,768]{1,0:T(8,128)(2,1)} %collective-permute-done.1.refs_1_), channel_id=1, source_target_pairs={{0,8},{8,0},{1,9},{9,1},{2,10},{10,2},{3,11},{11,3},{4,12},{12,4},... | collective-permute-start | bytes 1769480 | tf_op jit(solution)/shard_map/ppermute | solution.py:258
  29.4 15.5 %collective-permute-start.3 = (bf16[384,768]{1,0:T(8,128)(2,1)}, bf16[384,768]{1,0:T(8,128)(2,1)S(1)}, u32[]{:S(2)}, u32[]{:S(2)}) collective-permute-start(bf16[384,768]{1,0:T(8,128)(2,1)} %collective-permute-done.refs_2_), channel_id=1, source_target_pairs={{0,224},{32,0},{64,32},{96,64},{128,96},{160,128},{192,160},{224,1... | collective-permute-start | bytes 1769480 | tf_op jit(solution)/shard_map/ppermute | solution.py:268
  32.1 15.7 %collective-permute-start.2 = (bf16[384,768]{1,0:T(8,128)(2,1)}, bf16[384,768]{1,0:T(8,128)(2,1)}, u32[]{:S(2)}, u32[]{:S(2)}) collective-permute-start(bf16[384,768]{1,0:T(8,128)(2,1)} %collective-permute-done.1.refs_1_), channel_id=1, source_target_pairs={{0,32},{32,64},{64,96},{96,128},{128,160},{160,192},{192,224},{224... | collective-permute-start | bytes 1769480 | tf_op jit(solution)/shard_map/ppermute | solution.py:268
  32.1 15.7 %all-to-all-start.1 = ((bf16[8,48,768]{2,1,0:T(8,128)(2,1)}), bf16[8,48,768]{2,1,0:T(8,128)(2,1)S(1)}, u32[]{:S(2)}, u32[]{:S(2)}) async-start(bf16[8,48,768]{2,1,0:T(8,128)(2,1)} %prep_kv.1), calls=%async_computation.1 | async-start | bytes 1179648 | tf_op jit(solution)/shard_map/all_to_all | solution.py:282
  35.6 16.4 %collective-permute-start.8 = (bf16[384,768]{1,0:T(8,128)(2,1)S(1)}, bf16[384,768]{1,0:T(8,128)(2,1)}, u32[]{:S(2)}, u32[]{:S(2)}) collective-permute-start(bf16[384,768]{1,0:T(8,128)(2,1)S(1)} %constant_dynamic-update-slice_fusion.refs_1_), channel_id=1, source_target_pairs={{0,8},{8,0},{1,9},{9,1},{2,10},{10,2},{3,11},{11,3},{4,12},{12,4},... | collective-permute-start | bytes 1769480 | tf_op jit(solution)/shard_map/ppermute | solution.py:258
  47.8 4.3 %collective-permute-start.10 = (bf16[384,768]{1,0:T(8,128)(2,1)S(1)}, bf16[384,768]{1,0:T(8,128)(2,1)S(1)}, u32[]{:S(2)}, u32[]{:S(2)}) collective-permute-start(bf16[384,768]{1,0:T(8,128)(2,1)S(1)} %collective-permute-done.3.refs_4_), channel_id=1, source_target_pairs={{0,8},{8,0},{1,9},{9,1},{2,10},{10,2},{3,11},{11,3},{4,12},{12,4},... | collective-permute-start | bytes 1769480 | tf_op jit(solution)/shard_map/ppermute | solution.py:258
  49.3 2.7 %collective-permute-start.9 = (bf16[384,768]{1,0:T(8,128)(2,1)}, bf16[384,768]{1,0:T(8,128)(2,1)S(1)}, u32[]{:S(2)}, u32[]{:S(2)}) collective-permute-start(bf16[384,768]{1,0:T(8,128)(2,1)} %collective-permute-done.2.refs_3_), channel_id=1, source_target_pairs={{0,8},{8,0},{1,9},{9,1},{2,10},{10,2},{3,11},{11,3},{4,12},{12,4},... | collective-permute-start | bytes 1769480 | tf_op jit(solution)/shard_map/ppermute | solution.py:258
  49.3 15.8 %collective-permute-start.6 = (bf16[384,768]{1,0:T(8,128)(2,1)}, bf16[384,768]{1,0:T(8,128)(2,1)S(1)}, u32[]{:S(2)}, u32[]{:S(2)}) collective-permute-start(bf16[384,768]{1,0:T(8,128)(2,1)} %collective-permute-done.2.refs_3_), channel_id=1, source_target_pairs={{0,32},{32,64},{64,96},{96,128},{128,160},{160,192},{192,224},{224... | collective-permute-start | bytes 1769480 | tf_op jit(solution)/shard_map/ppermute | solution.py:268
  49.4 15.8 %collective-permute-start.7 = (bf16[384,768]{1,0:T(8,128)(2,1)S(1)}, bf16[384,768]{1,0:T(8,128)(2,1)S(1)}, u32[]{:S(2)}, u32[]{:S(2)}) collective-permute-start(bf16[384,768]{1,0:T(8,128)(2,1)S(1)} %collective-permute-done.3.refs_4_), channel_id=1, source_target_pairs={{0,224},{32,0},{64,32},{96,64},{128,96},{160,128},{192,160},{224,1... | collective-permute-start | bytes 1769480 | tf_op jit(solution)/shard_map/ppermute | solution.py:268
  65.2 4.3 %collective-permute-start.13 = (bf16[384,768]{1,0:T(8,128)(2,1)S(1)}, bf16[384,768]{1,0:T(8,128)(2,1)S(1)}, u32[]{:S(2)}, u32[]{:S(2)}) collective-permute-start(bf16[384,768]{1,0:T(8,128)(2,1)S(1)} %collective-permute-done.6.refs_1_), channel_id=1, source_target_pairs={{0,8},{8,0},{1,9},{9,1},{2,10},{10,2},{3,11},{11,3},{4,12},{12,4},... | collective-permute-start | bytes 1769480 | tf_op jit(solution)/shard_map/ppermute | solution.py:258
  66.5 2.9 %collective-permute-start.14 = (bf16[384,768]{1,0:T(8,128)(2,1)S(1)}, bf16[384,768]{1,0:T(8,128)(2,1)S(1)}, u32[]{:S(2)}, u32[]{:S(2)}) collective-permute-start(bf16[384,768]{1,0:T(8,128)(2,1)S(1)} %collective-permute-done.7.refs_2_), channel_id=1, source_target_pairs={{0,8},{8,0},{1,9},{9,1},{2,10},{10,2},{3,11},{11,3},{4,12},{12,4},... | collective-permute-start | bytes 1769480 | tf_op jit(solution)/shard_map/ppermute | solution.py:258
  66.6 9.7 %collective-permute-start.11 = (bf16[192,768]{1,0:T(8,128)(2,1)S(1)}, bf16[192,768]{1,0:T(8,128)(2,1)S(1)}, u32[]{:S(2)}, u32[]{:S(2)}) collective-permute-start(bf16[192,768]{1,0:T(8,128)(2,1)S(1)} %slice.9), channel_id=1, source_target_pairs={{0,32},{32,64},{64,96},{96,128},{128,160},{160,192},{192,224},{224... | collective-permute-start | bytes 884744 | tf_op jit(solution)/shard_map/ppermute | solution.py:268
  66.7 9.7 %collective-permute-start.12 = (bf16[192,768]{1,0:T(8,128)(2,1)S(1)}, bf16[192,768]{1,0:T(8,128)(2,1)S(1)}, u32[]{:S(2)}, u32[]{:S(2)}) collective-permute-start(bf16[192,768]{1,0:T(8,128)(2,1)S(1)} %slice.10), channel_id=1, source_target_pairs={{0,224},{32,0},{64,32},{96,64},{128,96},{160,128},{192,160},{224,1... | collective-permute-start | bytes 884744 | tf_op jit(solution)/shard_map/ppermute | solution.py:268
  76.3 2.3 %collective-permute-start.15 = (bf16[192,768]{1,0:T(8,128)(2,1)S(1)}, bf16[192,768]{1,0:T(8,128)(2,1)S(1)}, u32[]{:S(2)}, u32[]{:S(2)}) collective-permute-start(bf16[192,768]{1,0:T(8,128)(2,1)S(1)} %collective-permute-done.11.refs_1_), channel_id=1, source_target_pairs={{0,8},{8,0},{1,9},{9,1},{2,10},{10,2},{3,11},{11,3},{4,12},{12,4},... | collective-permute-start | bytes 884744 | tf_op jit(solution)/shard_map/ppermute | solution.py:258
  77.4 1.6 %collective-permute-start.16 = (bf16[192,768]{1,0:T(8,128)(2,1)S(1)}, bf16[192,768]{1,0:T(8,128)(2,1)S(1)}, u32[]{:S(2)}, u32[]{:S(2)}) collective-permute-start(bf16[192,768]{1,0:T(8,128)(2,1)S(1)} %collective-permute-done.12.refs_2_), channel_id=1, source_target_pairs={{0,8},{8,0},{1,9},{9,1},{2,10},{10,2},{3,11},{11,3},{4,12},{12,4},... | collective-permute-start | bytes 884744 | tf_op jit(solution)/shard_map/ppermute | solution.py:258
  84.2 16.2 %all-to-all-start.2 = ((bf16[16,56,384]{2,1,0:T(8,128)(2,1)}), bf16[16,56,384]{2,1,0:T(8,128)(2,1)S(1)}, u32[]{:S(2)}, u32[]{:S(2)}) async-start(bf16[16,56,384]{2,1,0:T(8,128)(2,1)} %attend4.1), calls=%async_computation.2 | async-start | bytes 1376256 | tf_op jit(solution)/shard_map/all_to_all | solution.py:297
  (4 other events, 9.5 us)
